TPU v7x, 256 devices: a whole 4x4x8 slice. The times are simulated.
256 devices in a mesh: seq: 32 (over x, z), tp: 8 (over y, core).
Axes of the slice: x: 4, y: 4, z: 8, core: 2. Of those that a mesh axis runs over, the one named last changes fastest.
Arguments:
- queries: bfloat16 [4096, 8192], P('seq', 'tp'), may hold values from -100 to 100, as said below
- key_rows: bfloat16 [4096, 1024], P('seq', 'tp'), may hold values from -4 to 4
- value_rows: bfloat16 [4096, 1024], P('seq', 'tp'), may hold values from -100 to 100
- text_mask: int32 [4096], P('seq'), may hold values from 0 to 1, as said below
- kept_slot: int32 [4096], P('seq'), may hold values from -1 to 1023, as said below
- norm_gain: float32 [8192], P('tp'), may hold values from 0.5 to 1.5
Outputs:
- context: bfloat16 [4096, 8192], P('seq', 'tp')
- visual_mass: float32 [4096], P('seq')
- kept_rows: bfloat16 [1024, 8192], P('seq', 'tp')
Inputs may be any that keep to these rules, and one draw needn't show every extreme that they name: `queries`: queries of one token and head stay within the stated range. `text_mask`: the text tokens form two runs of one or more tokens: one that starts at token 0 and one that ends at the last token; together they hold one seventeenth of 4096, rounded down. All other tokens are visual. `kept_slot`: every slot 0 to 1023 is held by exactly one token; slot // 32 is the destination shard, so each destination receives exactly 32 tokens. At most 2 tokens of one shard of 128 tokens go to one destination, and some pair of shards reaches 2 in every draw. Within a destination, slots follow the order of the source shards. Other tokens hold -1.
All inputs are finite; a program needn't handle non-finite values.
Results may differ from a plain program's by a relative error of at most 0.0095.
Values may be sent and summed in bfloat16 or wider, within the bound.
No kernel may reach another device: no remote copies, remote signals or barrier semaphores. Data moves between devices by JAX's collectives and lax.ppermute only.
A program may use at most 64 MiB of HBM per device.

v0:
```python
import math

import jax
import jax.numpy as jnp
from jax import lax
from jax.sharding import PartitionSpec as P

HD = 128
D = 8192


def on_device(queries, key_rows, value_rows, text_mask, kept_slot, norm_gain):
    row_count, width = queries.shape
    kv_width = key_rows.shape[1]
    kv_local = kv_width // HD
    group = width // kv_width
    shards = lax.axis_size("seq")
    mine = lax.axis_index("seq")
    scale = 1.0 / math.sqrt(HD)
    own_pos = mine * row_count + jnp.arange(row_count, dtype=jnp.int32)
    is_text = text_mask.astype(jnp.float32)
    grouped = queries.reshape(row_count, kv_local, group, HD)

    def scores_of(key_piece):
        length = key_piece.shape[0]
        key_heads = key_piece.reshape(length, kv_local, HD)
        scores = (
            jnp.einsum("tkgd,rkd->kgtr", grouped, key_heads, preferred_element_type=jnp.float32)
            * scale
        )
        key_pos = jnp.arange(length, dtype=jnp.int32)
        allowed = key_pos[None, :] <= own_pos[:, None]
        return (scores, allowed)

    pieces = (
        lax.all_gather(key_rows, "seq", axis=0, tiled=True),
        lax.all_gather(value_rows, "seq", axis=0, tiled=True),
    )
    row_max = jnp.full((kv_local, group, row_count), -1e30, jnp.float32)
    length = pieces[0].shape[0]
    scores, allowed = scores_of(pieces[0])
    masked = jnp.where(allowed[None, None], scores, jnp.float32(-1e30))
    new_max = jnp.maximum(row_max, jnp.max(masked, axis=-1))
    weights = jnp.where(allowed[None, None], jnp.exp(scores - new_max[..., None]), jnp.float32(0.0))
    row_total = jnp.sum(weights, axis=-1)
    value_heads = pieces[1].reshape(length, kv_local, HD)
    added = jnp.einsum(
        "kgtr,rkd->tkgd",
        weights.astype(jnp.bfloat16),
        value_heads,
        preferred_element_type=jnp.float32,
    )
    final = (new_max, row_total, added)
    log_totals = final[0] + jnp.log(final[1])
    scores, allowed = scores_of(lax.all_gather(key_rows, "seq", axis=0, tiled=True))
    probability = jnp.where(
        allowed[None, None], jnp.exp(scores - log_totals[..., None]), jnp.float32(0.0)
    )
    summed = jnp.sum(probability, axis=(0, 1))
    mass_terms = jnp.sum(summed * is_text[:, None], axis=0)
    context_rows = (
        (final[2] / jnp.transpose(final[1], (2, 0, 1))[..., None])
        .reshape(row_count, width)
        .astype(jnp.bfloat16)
    )
    mass_mine = lax.psum_scatter(mass_terms, "seq", scatter_dimension=0, tiled=True)
    head_mass = lax.psum(mass_mine, "tp")
    visual_mass = head_mass * (1.0 - is_text)
    keep_count = row_count // 4
    capacity = max(2, 5 * keep_count // (2 * shards))
    destination = jnp.where(kept_slot >= 0, kept_slot // keep_count, -1)
    member = (destination[:, None] == jnp.arange(shards, dtype=jnp.int32)[None, :]).astype(
        jnp.int32
    )
    earlier = jnp.cumsum(member, axis=0) - member
    ranks = jnp.sum(earlier * member, axis=1)
    placed = jnp.where(destination >= 0, destination * capacity + ranks, -1)
    select = jnp.arange(shards * capacity, dtype=jnp.int32)[:, None] == placed[None, :]
    send_rows = jnp.dot(
        select.astype(jnp.bfloat16), context_rows, preferred_element_type=jnp.float32
    ).astype(jnp.bfloat16)
    send_rows = send_rows.reshape(shards, capacity, width)
    send_slots = jnp.max(jnp.where(select, kept_slot[None, :], -1), axis=1).reshape(
        shards, capacity
    )
    got_rows, got_slots = (
        lax.all_to_all(send_rows, "seq", split_axis=0, concat_axis=0, tiled=True),
        lax.all_to_all(send_slots, "seq", split_axis=0, concat_axis=0, tiled=True),
    )
    target = got_slots.reshape(-1) - mine * keep_count
    putting = jnp.arange(keep_count, dtype=jnp.int32)[:, None] == target[None, :]
    gathered = jnp.dot(
        putting.astype(jnp.bfloat16),
        got_rows.reshape(shards * capacity, width),
        preferred_element_type=jnp.float32,
    )
    kept_square = lax.psum(jnp.sum(gathered * gathered, axis=1), "tp")
    kept_rows = (
        gathered * lax.rsqrt(kept_square / D + 1e-06)[:, None] * norm_gain[None, :]
    ).astype(jnp.bfloat16)
    return (context_rows, visual_mass, kept_rows)


def solution(mesh):
    placed = (P("seq", "tp"), P("seq", "tp"), P("seq", "tp"), P("seq"), P("seq"), P("tp"))
    return jax.shard_map(
        on_device,
        mesh=mesh,
        in_specs=placed,
        out_specs=(P("seq", "tp"), P("seq"), P("seq", "tp")),
        check_vma=False,
    )
```

profile of v0, /device:TPU:1, one launch (start us, length us, event | category | flops | bytes accessed | tf_op | source)
XLA Modules:
  0.0 354.8 jit_solution(14191386393714350272)
XLA Ops:
  7.2 0.0 copy-start
  7.2 0.0 all-gather.3.cloned.1.call-start
  7.2 0.7 all-gather.3.cloned.1.call-update
  7.9 0.7 compare_select_fusion.1
  8.6 0.1 fusion.30
  8.7 0.2 reduce_window_sum.11
  8.8 0.2 select_reduce_fusion
  9.0 0.7 compare_select_fusion
  9.7 0.8 select_reduce_fusion.1
  10.5 0.7 all_to_all.9
  11.2 11.9 %all-to-all-start = ((s32[32,1,2]{2,1,0:T(1,128)}), s32[32,1,2]{2,1,0:T(1,128)S(1)}, u32[]{:S(2)}, u32[]{:S(2)}) async-start(s32[32,1,2]{2,1,0:T(1,128)} %bitcast.13), calls=%async_computation | async-start | bytes 32768 | tf_op jit(solution)/shard_map/all_to_all | solution.py:88
  23.1 0.0 all-gather.5.cloned.1.call-start
  23.1 1.5 copy.23
  24.6 0.0 all-gather.5.cloned.1.call-update
  24.6 0.3 iota_compare_fusion
  25.0 0.7 convert_element_type.26
  25.6 1.3 dynamic-slice
  27.6 4.1 %all-to-all-done = s32[32,1,2]{2,1,0:T(1,128)S(1)} async-done(((s32[32,1,2]{2,1,0:T(1,128)}), s32[32,1,2]{2,1,0:T(1,128)S(1)}, u32[]{:S(2)}, u32[]{:S(2)}) %all-to-all-start) | async-done | bytes 288 | tf_op jit(solution)/shard_map/all_to_all | solution.py:88
  31.7 0.1 sub.54
  31.8 54.4 %all-gather.3.cloned.1.call-done = bf16[4096,128]{1,0:T(8,128)(2,1)} async-done(((bf16[128,128]{1,0:T(8,128)(2,1)}), bf16[4096,128]{1,0:T(8,128)(2,1)}) %all-gather.3.cloned.1.call-update) | async-done | bytes 1048592 | tf_op jit(solution)/shard_map/all_gather | solution.py:36
  86.2 0.0 copy-done
  86.2 8.2 %fusion = (f32[8,128]{1,0:T(8,128)S(1)}, f32[4096,128,8]{1,0,2:T(8,128)}) fusion(pred[128,4096]{0,1:T(8,128)(4,1)S(1)} %iota_compare_fusion, bf16[4096,128]{1,0:T(8,128)(2,1)} %all-gather.3.cloned.1.call-done, bf16[128,1024]{1,0:T(8,128)(2,1)S(1)} %copy-done), kind=kOutput, calls=%fused_computation.3 | convolution fusion | flops 1086323712 | bytes 18616320 | tf_op jit(solution)/shard_map/tkgd,rkd->kgtr/dot_general | solution.py:28
  94.3 9.2 %fusion.6 = f32[8,128]{1,0:T(8,128)S(1)} fusion(f32[4096,128,8]{1,0,2:T(8,128)} %get-tuple-element.18, f32[8,128]{1,0:T(8,128)S(1)} %broadcast_maximum_fusion, pred[128,4096]{0,1:T(8,128)(4,1)S(1)} %iota_compare_fusion), kind=kLoop, calls=%fused_computation.9 | loop fusion | flops 16776192 | bytes 17309696 | tf_op jit(solution)/shard_map/reduce_sum | solution.py:45
  103.6 54.7 %all-gather.5.cloned.1.call-done = bf16[4096,128]{0,1:T(8,128)(2,1)} async-done(((bf16[128,128]{0,1:T(8,128)(2,1)}), bf16[4096,128]{0,1:T(8,128)(2,1)}) %all-gather.5.cloned.1.call-update) | async-done | bytes 1048592 | tf_op jit(solution)/shard_map/all_gather | solution.py:37
  158.2 9.4 %fusion.23 = bf16[128,1,8,128]{0,3,2,1:T(8,128)(2,1)S(1)} fusion(f32[4096,128,8]{1,0,2:T(8,128)} %get-tuple-element.18, f32[8,128]{1,0:T(8,128)S(1)} %broadcast_maximum_fusion, pred[128,4096]{0,1:T(8,128)(4,1)S(1)} %iota_compare_fusion, bf16[4096,128]{0,1:T(8,128)(2,1)} %all-gather.5.cloned.1.call-done, f32[128,8]{0,1:T(8,128)S(1)} %bitcast.83), kind=kOutput, calls=%fused_computation.22 | convolution fusion | flops 1090781184 | bytes 18620416 | tf_op jit(solution)/shard_map/kgtr,rkd->tkgd/dot_general | solution.py:47
  167.6 0.0 copy-start.2
  167.6 0.0 copy-start.1
  167.6 0.2 convolution_convert_fusion
  167.9 0.7 reshape.105
  168.5 7.2 %all-to-all-start.1 = ((bf16[32,2,1024]{2,1,0:T(2,128)(2,1)}), bf16[32,2,1024]{2,1,0:T(2,128)(2,1)S(1)}, u32[]{:S(2)}, u32[]{:S(2)}) async-start(bf16[32,2,1024]{2,1,0:T(2,128)(2,1)} %reshape.105), calls=%async_computation.1 | async-start | bytes 262144 | tf_op jit(solution)/shard_map/all_to_all | solution.py:87
  175.8 9.4 %fusion.5 = f32[128,4096]{0,1:T(8,128)S(1)} fusion(f32[4096,128,8]{1,0,2:T(8,128)} %get-tuple-element.18, f32[8,128]{1,0:T(8,128)S(1)} %log_add_fusion, pred[128,4096]{0,1:T(8,128)(4,1)S(1)} %iota_compare_fusion), kind=kLoop, calls=%fused_computation.8 | loop fusion | flops 16252928 | bytes 19402752 | tf_op jit(solution)/shard_map/reduce_sum | solution.py:59
  185.2 0.9 copy.26
  186.0 0.6 multiply_reduce_fusion
  186.7 115.0 %all-reduce = f32[4096]{0:T(1024)S(1)} all-reduce(f32[4096]{0:T(1024)S(1)} %multiply_reduce_fusion), channel_id=2, replica_groups=mesh['seq'=32,'tp'=8] {'seq'}, use_global_device_ids=true, to_apply=%region_4.5.clone | all-reduce | flops 4096 | bytes 32768
  301.7 0.1 dynamic-slice.1
  301.7 0.0 all-to-all-done.1
  301.7 0.1 reshape.106
  301.8 0.3 multiply_reduce_fusion.1
  302.1 44.7 %all-reduce.1 = (f32[128]{0:T(128)S(1)}, f32[32]{0:T(128)S(1)}) all-reduce(f32[128]{0:T(128)S(1)} %dynamic-slice.1, f32[32]{0:T(128)S(1)} %get-tuple-element.19), channel_id=1, replica_groups=mesh['seq'=32,'tp'=8] {'tp'}, use_global_device_ids=true, to_apply=%region_5.6 | all-reduce | flops 160 | bytes 1280 | tf_op jit(solution)/shard_map/psum | solution.py:67
  346.7 0.0 copy-done.2
  346.7 0.5 subtract_multiply_fusion
  347.2 0.0 copy-done.1
  347.2 0.7 multiply_convert_fusion
  (5 shorter events, 0.1 us)
Async XLA Ops:
  7.2 79.0 %copy-start = (bf16[128,1024]{1,0:T(8,128)(2,1)S(1)}, bf16[128,1024]{1,0:T(8,128)(2,1)}, u32[]{:S(2)}) copy-start(bf16[128,1024]{1,0:T(8,128)(2,1)} %param.6) | copy-start | bytes 786436
  7.2 79.0 %all-gather.3.cloned.1.call-start = ((), (), s32[]{:S(2)}) async-start(), calls=%async_computation.2 | async-start | bytes 1081344 | tf_op jit(solution)/shard_map/all_gather | solution.py:36
  11.2 20.4 %all-to-all-start = ((s32[32,1,2]{2,1,0:T(1,128)}), s32[32,1,2]{2,1,0:T(1,128)S(1)}, u32[]{:S(2)}, u32[]{:S(2)}) async-start(s32[32,1,2]{2,1,0:T(1,128)} %bitcast.13), calls=%async_computation | async-start | bytes 32768 | tf_op jit(solution)/shard_map/all_to_all | solution.py:88
  23.1 135.2 %all-gather.5.cloned.1.call-start = ((), (), s32[]{:S(2)}) async-start(), calls=%async_computation.3 | async-start | bytes 1081344 | tf_op jit(solution)/shard_map/all_gather | solution.py:37
  167.6 179.1 %copy-start.2 = (s32[128]{0:T(128)S(1)}, s32[128]{0:T(128)}, u32[]{:S(2)}) copy-start(s32[128]{0:T(128)} %param.9) | copy-start | bytes 1540
  167.6 179.6 %copy-start.1 = (f32[1024]{0:T(1024)S(1)}, f32[1024]{0:T(1024)}, u32[]{:S(2)}) copy-start(f32[1024]{0:T(1024)} %param.11) | copy-start | bytes 12292
  168.5 133.2 %all-to-all-start.1 = ((bf16[32,2,1024]{2,1,0:T(2,128)(2,1)}), bf16[32,2,1024]{2,1,0:T(2,128)(2,1)S(1)}, u32[]{:S(2)}, u32[]{:S(2)}) async-start(bf16[32,2,1024]{2,1,0:T(2,128)(2,1)} %reshape.105), calls=%async_computation.1 | async-start | bytes 262144 | tf_op jit(solution)/shard_map/all_to_all | solution.py:87
Sparse Core Ops, SparseCore 0:
  10.6 75.4 all-gather.2
  89.2 69.0 all-gather.4
where the time goes:
time: 355 us
  blocking collectives  160 us (45%)
  waiting for transfers between devices  114 us (32%)
  other arithmetic  24.1 us (7%)
  starting transfers between devices  19.2 us (5%)
  matrix products  18 us (5%)
  between operations  14.8 us (4%)
  local copies, waits for them, and re-layouts  5.24 us (1%)
    unnamed x1, blocking collectives  115 us
    all_gather x1, waiting for transfers between devices, on_device(): lax.all_gather(value_rows, 'seq', axis=0, tiled=True)  54.7 us
    all_gather x1, waiting for transfers between devices, on_device(): lax.all_gather(key_rows, 'seq', axis=0, tiled=True)  54.4 us
    psum x1, blocking collectives, on_device(): head_mass = lax.psum(mass_mine, 'tp')  44.7 us
    all_to_all x1, starting transfers between devices, on_device(): lax.all_to_all(send_slots, 'seq', split_axis=0, concat_axis=0, tiled=True)  11.9 us
    reduce_sum x1, other arithmetic, on_device(): summed = jnp.sum(probability, axis=(0, 1))  9.41 us
    dot_general x1, matrix products, on_device(): jnp.einsum('kgtr,rkd->tkgd', weights.astype(jnp.bfloat16), value_heads, p...  9.36 us
    reduce_sum x1, other arithmetic, on_device(): row_total = jnp.sum(weights, axis=-1)  9.21 us
  transfers between devices with their start and end apart: 4, of which 3 were waited for; matrix products, arithmetic and copies ran while one was open for 10% of the time, Pallas kernels for 0%

commit v1 on v0

v1 whole, which is shorter than its diff:
```python
import math

import jax
import jax.numpy as jnp
from jax import lax
from jax.experimental import pallas as pl
from jax.experimental.pallas import tpu as pltpu
from jax.sharding import Mesh, PartitionSpec as P

HD = 128
D = 8192
TOK = 128
GROUP = 8
ROWS = GROUP * TOK
NX = 4
NZ = 8
SHARDS = NX * NZ
KEEP = 32
SUB = 24
SEND = SHARDS * SUB
PICK = ROWS + 2 * TOK
PAY = 8 + KEEP
BLOCK = 256
SLAB = NZ * TOK
FACTOR = math.log2(math.e) / math.sqrt(HD)
LOW = -1e30
NT = (((1,), (1,)), ((), ()))
TN = (((0,), (0,)), ((), ()))
VMEM_BYTES = 48 * 1024 * 1024


def smem():
    return pl.BlockSpec(memory_space=pltpu.SMEM)


def vmem():
    return pl.BlockSpec(memory_space=pltpu.VMEM)


def params():
    return pltpu.CompilerParams(vmem_limit_bytes=VMEM_BYTES)


def rows_of_queries(q_ref, block):
    heads = BLOCK // TOK
    return jnp.concatenate(
        [q_ref[:, (block * heads + i) * HD : (block * heads + i + 1) * HD] for i in range(heads)],
        axis=0,
    )


def own_mask(z, width):
    token = lax.broadcasted_iota(jnp.int32, (BLOCK, width), 0) & (TOK - 1)
    key = lax.broadcasted_iota(jnp.int32, (BLOCK, width), 1)
    return key <= token + z * TOK


def flash(query, key, value, old, mask=None):
    scores = lax.dot_general(query, key, NT, preferred_element_type=jnp.float32)
    if mask is not None:
        scores = jnp.where(mask, scores, LOW)
    top = jnp.max(scores, axis=1, keepdims=True)
    if old is not None:
        top = jnp.maximum(old[0], top)
    weights = jnp.exp2((scores - top) * FACTOR)
    total = jnp.sum(weights, axis=1, keepdims=True)
    mixed = jnp.dot(weights.astype(jnp.bfloat16), value, preferred_element_type=jnp.float32)
    if old is not None:
        shrink = jnp.exp2((old[0] - top) * FACTOR)
        total = total + old[1] * shrink
        mixed = mixed + old[2] * shrink
    return top, total, mixed


def wide(column):
    return jnp.broadcast_to(column, (column.shape[0], 128))


def keys_of(ref):
    return ref[:, 0].reshape(-1, HD)


def values_of(ref):
    return ref[:, 1].reshape(-1, HD)


def own_kernel(place_ref, q_ref, slab_ref, slot_row_ref, top_ref, total_ref, mixed_ref, pick_ref):
    z = place_ref[1]
    key = keys_of(slab_ref)
    value = values_of(slab_ref)
    mask = own_mask(z, SLAB)
    for block in range(ROWS // BLOCK):
        rows = slice(block * BLOCK, (block + 1) * BLOCK)
        top, total, mixed = flash(rows_of_queries(q_ref, block), key, value, None, mask)
        top_ref[rows] = wide(top)
        total_ref[rows] = wide(total)
        mixed_ref[rows] = mixed
    slot_row = slot_row_ref[...]
    target_row = jnp.where(slot_row >= 0, slot_row >> 5, -1)
    target_col = jnp.transpose(jnp.broadcast_to(target_row, (TOK, TOK)))
    first = lax.broadcasted_iota(jnp.int32, (TOK, TOK), 0)
    second = lax.broadcasted_iota(jnp.int32, (TOK, TOK), 1)
    earlier = jnp.where((target_col == target_row) & (first < second), 1, 0)
    rank = jnp.sum(earlier, axis=0, keepdims=True)
    placed = jnp.where(target_row >= 0, target_row * 2 + rank, -1)[None]
    shape = (SHARDS, SUB, TOK)
    to = lax.broadcasted_iota(jnp.int32, shape, 0)
    sub = lax.broadcasted_iota(jnp.int32, shape, 1)
    lane = lax.broadcasted_iota(jnp.int32, shape, 2)
    head = jnp.where(sub < 16, sub & 7, -1)
    same = placed == to * 2 + (sub >> 3)

    def put(at, hit):
        picked = jnp.where(hit, 1.0, 0.0).reshape(SEND, TOK)
        pick_ref[:, at : at + TOK] = picked.astype(jnp.bfloat16)

    for h in range(GROUP):
        put(h * TOK, same & (head == h))
    put(ROWS, (placed == to * 2 + (sub - 18)) & ((sub == 18) | (sub == 19)))
    put(ROWS + TOK, lane == jnp.where(sub == 16, to, jnp.where(sub == 17, to + SHARDS, -1)))


def next_kernel(
    place_ref, q_ref, left_ref, right_ref, top_in, total_in, mixed_in, top_ref, total_ref, mixed_ref
):
    x = place_ref[0]
    top_ref[...] = top_in[...]
    total_ref[...] = total_in[...]
    mixed_ref[...] = mixed_in[...]

    def add(slab_ref):
        key = keys_of(slab_ref)
        value = values_of(slab_ref)
        for block in range(ROWS // BLOCK):
            rows = slice(block * BLOCK, (block + 1) * BLOCK)
            old = (top_ref[rows, 0:1], total_ref[rows, 0:1], mixed_ref[rows])
            top, total, mixed = flash(rows_of_queries(q_ref, block), key, value, old)
            top_ref[rows] = wide(top)
            total_ref[rows] = wide(total)
            mixed_ref[rows] = mixed

    @pl.when(x > 0)
    def _():
        add(left_ref)

    @pl.when(x == NX - 1)
    def _():
        add(right_ref)


def last_kernel(
    place_ref,
    q_ref,
    far_left_ref,
    far_right_ref,
    own_ref,
    left_ref,
    right_ref,
    text_ref,
    slots_ref,
    pick_ref,
    top_in,
    total_in,
    mixed_in,
    context_ref,
    send_ref,
    top_ref,
    total_ref,
    mixed_ref,
    mass_ref,
):
    x = place_ref[0]
    z = place_ref[1]
    has_text = place_ref[2]
    top_ref[...] = top_in[...]
    total_ref[...] = total_in[...]
    mixed_ref[...] = mixed_in[...]
    mass_ref[...] = jnp.zeros_like(mass_ref)

    @pl.when(x >= 2)
    def _():
        key = jnp.concatenate([keys_of(far_left_ref), keys_of(far_right_ref)], axis=0)
        value = jnp.concatenate([values_of(far_left_ref), values_of(far_right_ref)], axis=0)
        for block in range(ROWS // BLOCK):
            rows = slice(block * BLOCK, (block + 1) * BLOCK)
            old = (top_ref[rows, 0:1], total_ref[rows, 0:1], mixed_ref[rows])
            top, total, mixed = flash(rows_of_queries(q_ref, block), key, value, old)
            top_ref[rows] = wide(top)
            total_ref[rows] = wide(total)
            mixed_ref[rows] = mixed

    context = (mixed_ref[...] / total_ref[...]).astype(jnp.bfloat16)
    for h in range(GROUP):
        context_ref[:, h * HD : (h + 1) * HD] = context[h * TOK : (h + 1) * TOK]

    @pl.when(has_text > 0)
    def _():
        text = jnp.concatenate([text_ref[...]] * (BLOCK // TOK), axis=0)[:, 0:1]
        mask = own_mask(z, SLAB)

        def mass_of(key, at, masked):
            shift = lax.rem(at, NX) * NZ
            added = jnp.zeros((1, SLAB), jnp.float32)
            for block in range(ROWS // BLOCK):
                rows = slice(block * BLOCK, (block + 1) * BLOCK)
                query = rows_of_queries(q_ref, block)
                scores = lax.dot_general(query, key, NT, preferred_element_type=jnp.float32)
                level = top_ref[rows, 0:1] * FACTOR + jnp.log2(total_ref[rows, 0:1])
                level = jnp.where(text > 0.0, level, -LOW)
                probability = jnp.exp2(scores * FACTOR - level)
                if masked:
                    probability = jnp.where(mask, probability, 0.0)
                added = added + jnp.sum(probability, axis=0, keepdims=True)
            for i in range(NZ):
                mass_ref[pl.ds(shift + i, 1), :] = added[:, i * TOK : (i + 1) * TOK]

        mass_of(keys_of(own_ref), x, True)

        @pl.when(x > 0)
        def _():
            mass_of(keys_of(left_ref), x + NX - 1, False)

        @pl.when(x == NX - 1)
        def _():
            mass_of(keys_of(right_ref), x + 1, False)

        @pl.when(x >= 2)
        def _():
            key = jnp.concatenate([keys_of(far_left_ref), keys_of(far_right_ref)], axis=0)
            mass_of(key, x + 2, False)

    mass = mass_ref[...]
    high = mass.astype(jnp.bfloat16).astype(jnp.float32)
    low = mass - high
    both = jnp.concatenate([high, low, jnp.zeros((TOK - 2 * SHARDS, HD), jnp.float32)], axis=0)
    slots = slots_ref[...]
    slots = jnp.where(slots >= 0, (slots & (KEEP - 1)) + 1, 0).astype(jnp.float32)
    source = jnp.concatenate(
        [context, slots.astype(jnp.bfloat16), both.astype(jnp.bfloat16)], axis=0
    )
    send_ref[...] = jnp.dot(pick_ref[...], source, preferred_element_type=jnp.float32).astype(
        jnp.bfloat16
    )


def place_kernel(got_ref, rows_ref, pay_ref):
    got = got_ref[...].astype(jnp.float32).reshape(SHARDS, SUB, HD)
    mass = jnp.sum(got[:, 16:17, :] + got[:, 17:18, :], axis=0)
    slots = jnp.concatenate(
        [
            jnp.broadcast_to(got[:, 18:19, :], (SHARDS, 8, HD)),
            jnp.broadcast_to(got[:, 19:20, :], (SHARDS, 8, HD)),
            jnp.zeros((SHARDS, 8, HD), jnp.float32),
        ],
        axis=1,
    ).astype(jnp.int32)
    shape = (SHARDS, SUB, HD)
    head = lax.broadcasted_iota(jnp.int32, shape, 1) & 7
    lane = lax.broadcasted_iota(jnp.int32, shape, 2)
    parts = []
    for half in range(2):
        hit = (slots == (lane & (KEEP - 1)) + 1) & (head == (lane >> 5) + 4 * half)
        parts.append(jnp.where(hit, 1.0, 0.0).reshape(SEND, HD))
    put = jnp.concatenate(parts, axis=1).astype(jnp.bfloat16)
    rows = lax.dot_general(put, got_ref[...], TN, preferred_element_type=jnp.float32)
    rows_ref[...] = rows
    squares = jnp.sum((rows * rows).reshape(GROUP, KEEP, HD), axis=0)
    squares = jnp.sum(squares, axis=1, keepdims=True)
    pay_ref[...] = jnp.concatenate([jnp.broadcast_to(mass, (8, HD)), wide(squares)], axis=0)


def finish_kernel(a_ref, b_ref, c_ref, d_ref, rows_ref, gain_ref, text_ref, mass_ref, kept_ref):
    pay = (a_ref[...] + b_ref[...]) + (c_ref[...] + d_ref[...])
    mass_ref[...] = pay[0:1] * (1.0 - text_ref[...].astype(jnp.float32))
    factor = lax.rsqrt(pay[8:] / D + 1e-06)
    for h in range(GROUP):
        columns = slice(h * HD, (h + 1) * HD)
        kept_ref[:, columns] = (
            rows_ref[h * KEEP : (h + 1) * KEEP] * factor * gain_ref[:, columns]
        ).astype(jnp.bfloat16)


def shape_of(shape, dtype):
    return jax.ShapeDtypeStruct(shape, dtype)


def shifted(value, axis, step, count):
    return lax.ppermute(value, axis, [(i, (i + step) % count) for i in range(count)])


def on_device(queries, key_rows, value_rows, text_mask, kept_slot, norm_gain):
    f32, bf16 = jnp.float32, jnp.bfloat16
    x = lax.axis_index("x")
    z = lax.axis_index("z")
    place = jnp.stack([x, z, jnp.max(text_mask)]).astype(jnp.int32)
    text_columns = jnp.broadcast_to(text_mask[:, None], (TOK, HD)).astype(f32)
    slot_columns = jnp.broadcast_to(kept_slot[:, None], (TOK, HD))

    both = jnp.stack([key_rows, value_rows])
    own = lax.all_to_all(
        jnp.broadcast_to(both[None], (NZ, 2, TOK, HD)), "z", split_axis=0, concat_axis=0, tiled=True
    )
    left = shifted(own, "x", 1, NX)
    right = shifted(own, "x", -1, NX)
    half = NZ // 2
    far_left = shifted(left[:half], "x", 1, NX)
    far_right = shifted(right[half:], "x", -1, NX)

    state = [shape_of((ROWS, HD), f32)] * 3
    pair = 4 * ROWS * SLAB * HD
    top, total, mixed, pick = pl.pallas_call(
        own_kernel,
        in_specs=[smem(), vmem(), vmem(), vmem()],
        out_specs=[vmem()] * 4,
        out_shape=state + [shape_of((SEND, PICK), bf16)],
        compiler_params=params(),
        cost_estimate=pl.CostEstimate(
            flops=pair, bytes_accessed=5 * 2**20, transcendentals=ROWS * SLAB
        ),
        name="own_slab",
    )(place, queries, own, kept_slot[None])
    top, total, mixed = pl.pallas_call(
        next_kernel,
        in_specs=[smem()] + [vmem()] * 6,
        out_specs=[vmem()] * 3,
        out_shape=state,
        compiler_params=params(),
        cost_estimate=pl.CostEstimate(
            flops=2 * pair, bytes_accessed=5 * 2**20, transcendentals=2 * ROWS * SLAB
        ),
        name="next_slabs",
    )(place, queries, left, right, top, total, mixed)
    context, send = pl.pallas_call(
        last_kernel,
        in_specs=[smem()] + [vmem()] * 12,
        out_specs=[vmem()] * 2,
        out_shape=[shape_of((TOK, GROUP * HD), bf16), shape_of((SEND, HD), bf16)],
        scratch_shapes=[pltpu.VMEM((ROWS, HD), f32)] * 3 + [pltpu.VMEM((SHARDS, HD), f32)],
        compiler_params=params(),
        cost_estimate=pl.CostEstimate(
            flops=3 * pair, bytes_accessed=6 * 2**20, transcendentals=5 * ROWS * SLAB
        ),
        name="last_slab",
    )(
        place, queries, far_left, far_right, own, left, right, text_columns, slot_columns, pick,
        top, total, mixed,
    )
    got = lax.all_to_all(
        send.reshape(SHARDS, SUB, HD), ("x", "z"), split_axis=0, concat_axis=0, tiled=True
    ).reshape(SEND, HD)
    rows, pay = pl.pallas_call(
        place_kernel,
        in_specs=[vmem()],
        out_specs=[vmem()] * 2,
        out_shape=[shape_of((GROUP * KEEP, HD), f32), shape_of((PAY, HD), f32)],
        compiler_params=params(),
        name="place_rows",
    )(got)
    pay = pay + shifted(pay, "core", 1, 2)
    pays = [pay] + [shifted(pay, "y", step, 4) for step in (1, 2, 3)]
    mass, kept = pl.pallas_call(
        finish_kernel,
        in_specs=[vmem()] * 7,
        out_specs=[vmem()] * 2,
        out_shape=[shape_of((1, TOK), f32), shape_of((KEEP, GROUP * HD), bf16)],
        compiler_params=params(),
        name="finish",
    )(*pays, rows, norm_gain[None], text_mask[None])
    return context, mass[0], kept


def solution(mesh):
    cut = Mesh(mesh.devices.reshape(NX, NZ, 4, 2), ("x", "z", "y", "core"))
    seq, tp = ("x", "z"), ("y", "core")
    placed = (P(seq, tp), P(seq, tp), P(seq, tp), P(seq), P(seq), P(tp))
    return jax.shard_map(
        on_device,
        mesh=cut,
        in_specs=placed,
        out_specs=(P(seq, tp), P(seq), P(seq, tp)),
        check_vma=False,
    )
```

time: 355 us -> 88.5 us (0.25)
  blocking collectives: 160 us -> 48.8 us
  waiting for transfers between devices: 114 us -> 10.8 us
  other arithmetic: 24.1 us -> 2.91 us
  matrix products: 18 us -> 0 us
  between operations: 14.8 us -> 0.75 us
  Pallas kernels: 0 us -> 8.78 us
  starting transfers between devices: 19.2 us -> 14.6 us
  local copies, waits for them, and re-layouts: 5.24 us -> 1.6 us
    unnamed x1 -> x0, blocking collectives: 115 us -> none
    all_gather x2 -> x0, waiting for transfers between devices: 109 us -> none  [the longest x1 54.7 us: on_device(): lax.all_gather(value_rows, 'seq', axis=0, tiled=True)]
    all_to_all x0 -> x2, blocking collectives: none -> 48.8 us  [the longest x1 24.8 us: on_device(): lax.all_to_all(jnp.broadcast_to(both[None], (NZ, 2, TOK, HD)), 'z', split...]
    psum x1 -> x0, blocking collectives: 44.7 us -> none  [on_device(): head_mass = lax.psum(mass_mine, 'tp')]
    reduce_sum x4 -> x0, other arithmetic: 19.4 us -> none  [the longest x1 9.41 us: on_device(): summed = jnp.sum(probability, axis=(0, 1))]
    all_to_all x2 -> x0, starting transfers between devices: 19.1 us -> none  [the longest x1 11.9 us: on_device(): lax.all_to_all(send_slots, 'seq', split_axis=0, concat_axis=0, tiled=True)]
    dot_general x4 -> x0, matrix products: 18 us -> none  [the longest x1 9.36 us: on_device(): jnp.einsum('kgtr,rkd->tkgd', weights.astype(jnp.bfloat16), value_heads, p...]
    ppermute x0 -> x8, starting transfers between devices: none -> 14.6 us  [shifted(): lax.ppermute(value, axis, [(i, (i + step) % count) for i in range(count)])]
  transfers between devices with their start and end apart: 4 -> 8, of which waited for: 3 -> 4; matrix products, arithmetic and copies ran while one was open for 10% -> 2% of each run, Pallas kernels for 0% -> 4%
where the time goes in v1:
time: 88.5 us; the launch traced here: 88.2 us
  blocking collectives  48.8 us (55%)
  starting transfers between devices  14.6 us (16%)
  waiting for transfers between devices  10.8 us (12%)
  Pallas kernels  8.78 us (10%)
  other arithmetic  2.91 us (3%)
  local copies, waits for them, and re-layouts  1.6 us (2%)
    all_to_all x1, blocking collectives, on_device(): lax.all_to_all(jnp.broadcast_to(both[None], (NZ, 2, TOK, HD)), 'z', split...  24.8 us
    all_to_all x1, blocking collectives, on_device(): lax.all_to_all(send.reshape(SHARDS, SUB, HD), ('x', 'z'), split_axis=0, c...  24 us
    ppermute x8, starting transfers between devices, shifted(): lax.ppermute(value, axis, [(i, (i + step) % count) for i in range(count)])  14.6 us
    ppermute x8, waiting for transfers between devices, shifted(): lax.ppermute(value, axis, [(i, (i + step) % count) for i in range(count)])  10.8 us
    pallas_call x1, Pallas kernels, on_device(): pl.pallas_call(last_kernel, in_specs=[smem()] + [vmem()] * 12, out_specs=...  3.93 us
    pallas_call x1, Pallas kernels, on_device(): pl.pallas_call(own_kernel, in_specs=[smem(), vmem(), vmem(), vmem()], out...  3.14 us
  transfers between devices with their start and end apart: 8, of which 4 were waited for; matrix products, arithmetic and copies ran while one was open for 2% of the time, Pallas kernels for 4%

profile of v1, /device:TPU:1, one launch (start us, length us, event | category | flops | bytes accessed | tf_op | source)
XLA Modules:
  0.0 88.2 jit_solution(3233268491246853083)
XLA Ops:
  0.6 0.0 copy-start.1
  0.6 0.0 copy-start.3
  0.7 0.8 pad_maximum_fusion
  1.5 0.1 broadcast_in_dim.12
  1.6 24.8 %all_to_all.10.slab_ref.own_ref = bf16[8,2,128,128]{3,2,1,0:T(8,128)(2,1)S(1)} all-to-all(bf16[8,2,128,128]{3,2,1,0:T(8,128)(2,1)S(1)} %broadcast_in_dim.12), channel_id=1, replica_groups=mesh['x'=4,'z'=8,'y'=4,'core'=2] {'z'}, dimensions={0} | all-to-all | bytes 1048576 | tf_op jit(solution)/shard_map/all_to_all | solution.py:300
  26.4 1.2 %collective-permute-start = (bf16[8,2,128,128]{3,2,1,0:T(8,128)(2,1)S(1)}, bf16[8,2,128,128]{3,2,1,0:T(8,128)(2,1)S(1)}, u32[]{:S(2)}, u32[]{:S(2)}) collective-permute-start(bf16[8,2,128,128]{3,2,1,0:T(8,128)(2,1)S(1)} %all_to_all.10.slab_ref.own_ref), channel_id=1, source_target_pairs={{0,64},{64,128},{128,192},{192,0},{1,65},{65,129},{129,193},{193,1... | collective-permute-start | bytes 1572872 | tf_op jit(solution)/shard_map/ppermute | solution.py:288
  27.6 1.5 %collective-permute-start.2 = (bf16[8,2,128,128]{3,2,1,0:T(8,128)(2,1)S(1)}, bf16[8,2,128,128]{3,2,1,0:T(8,128)(2,1)S(1)}, u32[]{:S(2)}, u32[]{:S(2)}) collective-permute-start(bf16[8,2,128,128]{3,2,1,0:T(8,128)(2,1)S(1)} %all_to_all.10.slab_ref.own_ref), channel_id=1, source_target_pairs={{0,192},{64,0},{128,64},{192,128},{1,193},{65,1},{129,65},{193,129... | collective-permute-start | bytes 1572872 | tf_op jit(solution)/shard_map/ppermute | solution.py:288
  29.1 1.4 %fusion = (f32[128]{0:T(128)S(1)}, s32[]{:T(128)}) fusion(s32[128]{0:T(128)} %param.9), kind=kLoop, calls=%fused_computation.2 | loop fusion | flops 255 | bytes 1028 | tf_op jit(solution)/shard_map/convert_element_type | solution.py:296
  30.4 8.1 %collective-permute-done.left_ref = bf16[8,2,128,128]{3,2,1,0:T(8,128)(2,1)S(1)} collective-permute-done((bf16[8,2,128,128]{3,2,1,0:T(8,128)(2,1)S(1)}, bf16[8,2,128,128]{3,2,1,0:T(8,128)(2,1)S(1)}, u32[]{:S(2)}, u32[]{:S(2)}) %collective-permute-start) | collective-permute-done | bytes 524320 | tf_op jit(solution)/shard_map/ppermute | solution.py:288
  38.6 0.1 collective-permute-start.1
  38.7 0.0 collective-permute-done.2.right_ref
  38.7 2.7 %collective-permute-start.3 = (bf16[4,2,128,128]{3,2,1,0:T(8,128)(2,1)S(1)}, bf16[4,2,128,128]{3,2,1,0:T(8,128)(2,1)S(1)}, u32[]{:S(2)}, u32[]{:S(2)}) collective-permute-start(bf16[4,2,128,128]{3,2,1,0:T(8,128)(2,1)S(1)} %slice.9), channel_id=1, source_target_pairs={{0,192},{64,0},{128,64},{192,128},{1,193},{65,1},{129,65},{193,129... | collective-permute-start | bytes 786440 | tf_op jit(solution)/shard_map/ppermute | solution.py:288
  41.4 0.7 pad_add_fusion.place_ref
  42.2 0.0 copy-done.1
  42.2 0.0 copy-done.3
  42.2 3.1 %own_slab.1 = (f32[1024,128]{1,0:T(8,128)S(1)}, f32[1024,128]{1,0:T(8,128)S(1)}, f32[1024,128]{1,0:T(8,128)S(1)}, bf16[768,1280]{1,0:T(8,128)(2,1)S(1)}) custom-call(s32[3]{0:T(128)S(1)} %pad_add_fusion.place_ref, bf16[128,1024]{1,0:T(8,128)(2,1)S(1)} %copy-done.3, bf16[8,2,128,128]{3,2,1,0:T(8,128)(2,1)S(1)} %all_to_all.10.slab_ref.own_ref, ...), custom_call_target="tpu_custom_call" | custom-call | flops 536870912 | bytes 5242880 | tf_op jit(solution)/shard_map/own_slab/pallas_call | solution.py:311
  45.3 0.0 copy-start.4
  45.3 1.3 %copy-done.4 = bf16[768,1280]{1,0:T(8,128)(2,1)} copy-done((bf16[768,1280]{1,0:T(8,128)(2,1)}, bf16[768,1280]{1,0:T(8,128)(2,1)S(1)}, u32[]{:S(2)}) %copy-start.4) | copy-done | bytes 1966104
  46.6 0.6 next_slabs.1
  47.3 0.0 collective-permute-done.1.far_left_ref
  47.3 0.0 collective-permute-done.3.far_right_ref
  47.3 0.1 broadcast_in_dim.13.text_ref
  47.4 0.1 broadcast_in_dim.14.slots_ref
  47.4 0.0 copy-start
  47.5 0.0 copy-start.2
  47.5 3.9 %last_slab.1 = (bf16[128,1024]{1,0:T(8,128)(2,1)}, bf16[768,128]{1,0:T(8,128)(2,1)S(1)}) custom-call(s32[3]{0:T(128)S(1)} %pad_add_fusion.place_ref, bf16[128,1024]{1,0:T(8,128)(2,1)S(1)} %copy-done.3, bf16[4,2,128,128]{3,2,1,0:T(8,128)(2,1)S(1)} %collective-permute-done.1.far_left_ref, bf16[4,2,128,128]{3,2,1,0:T(8,128)(2,1)S(1)} %collective-permute-done.3.far_right_ref, ...), custom_call_target="tpu_custom_call" | custom-call | flops 1610612736 | bytes 6291456 | tf_op jit(solution)/shard_map/last_slab/pallas_call | solution.py:333
  51.4 24.0 %all_to_all.11 = bf16[32,24,128]{2,1,0:T(8,128)(2,1)S(1)} all-to-all(bf16[32,24,128]{2,1,0:T(8,128)(2,1)S(1)} %bitcast.12), channel_id=1, replica_groups=mesh['x'=4,'z'=8,'y'=4,'core'=2] {'x','z'}, dimensions={0} | all-to-all | bytes 393216 | tf_op jit(solution)/shard_map/all_to_all | solution.py:348
  75.4 0.4 place_rows.1
  75.8 4.2 %collective-permute-start.4 = (f32[40,128]{1,0:T(8,128)S(1)}, f32[40,128]{1,0:T(8,128)S(1)}, u32[]{:S(2)}, u32[]{:S(2)}) collective-permute-start(f32[40,128]{1,0:T(8,128)S(1)} %get-tuple-element.25), channel_id=1, source_target_pairs={{0,1},{1,0},{2,3},{3,2},{4,5},{5,4},{6,7},{7,6},{8,9},{9,8},{10,11... | collective-permute-start | bytes 61448 | tf_op jit(solution)/shard_map/ppermute | solution.py:288
  79.9 0.8 collective-permute-done.4
  80.8 1.3 %collective-permute-start.5 = (f32[40,128]{1,0:T(8,128)S(1)}, f32[40,128]{1,0:T(8,128)S(1)}, u32[]{:S(2)}, u32[]{:S(2)}) collective-permute-start(f32[40,128]{1,0:T(8,128)S(1)} %add.3.a_ref), channel_id=1, source_target_pairs={{0,2},{2,4},{4,6},{6,0},{1,3},{3,5},{5,7},{7,1},{8,10},{10,12},{12... | collective-permute-start | bytes 61448 | tf_op jit(solution)/shard_map/ppermute | solution.py:288
  82.1 2.6 %collective-permute-start.6 = (f32[40,128]{1,0:T(8,128)S(1)}, f32[40,128]{1,0:T(8,128)S(1)}, u32[]{:S(2)}, u32[]{:S(2)}) collective-permute-start(f32[40,128]{1,0:T(8,128)S(1)} %add.3.a_ref), channel_id=1, source_target_pairs={{0,4},{2,6},{4,0},{6,2},{1,5},{3,7},{5,1},{7,3},{8,12},{10,14},{12... | collective-permute-start | bytes 61448 | tf_op jit(solution)/shard_map/ppermute | solution.py:288
  84.7 1.1 %collective-permute-start.7 = (f32[40,128]{1,0:T(8,128)S(1)}, f32[40,128]{1,0:T(8,128)S(1)}, u32[]{:S(2)}, u32[]{:S(2)}) collective-permute-start(f32[40,128]{1,0:T(8,128)S(1)} %add.3.a_ref), channel_id=1, source_target_pairs={{0,6},{2,0},{4,2},{6,4},{1,7},{3,1},{5,3},{7,5},{8,14},{10,8},{12,... | collective-permute-start | bytes 61448 | tf_op jit(solution)/shard_map/ppermute | solution.py:288
  85.8 0.0 collective-permute-done.5.b_ref
  85.8 0.4 collective-permute-done.6.c_ref
  86.2 1.4 %collective-permute-done.7.d_ref = f32[40,128]{1,0:T(8,128)S(1)} collective-permute-done((f32[40,128]{1,0:T(8,128)S(1)}, f32[40,128]{1,0:T(8,128)S(1)}, u32[]{:S(2)}, u32[]{:S(2)}) %collective-permute-start.7) | collective-permute-done | bytes 20512 | tf_op jit(solution)/shard_map/ppermute | solution.py:288
  87.6 0.0 copy-done
  87.6 0.0 copy-done.2
  87.6 0.7 finish.1
  (3 shorter events, 0.0 us)
Async XLA Ops:
  0.6 41.5 %copy-start.1 = (s32[128]{0:T(128)S(1)}, s32[128]{0:T(128)}, u32[]{:S(2)}) copy-start(s32[128]{0:T(128)} %param.10) | copy-start | bytes 1540
  0.6 41.5 %copy-start.3 = (bf16[128,1024]{1,0:T(8,128)(2,1)S(1)}, bf16[128,1024]{1,0:T(8,128)(2,1)}, u32[]{:S(2)}) copy-start(bf16[128,1024]{1,0:T(8,128)(2,1)} %q_ref.5) | copy-start | bytes 786436
  26.4 12.2 %collective-permute-start = (bf16[8,2,128,128]{3,2,1,0:T(8,128)(2,1)S(1)}, bf16[8,2,128,128]{3,2,1,0:T(8,128)(2,1)S(1)}, u32[]{:S(2)}, u32[]{:S(2)}) collective-permute-start(bf16[8,2,128,128]{3,2,1,0:T(8,128)(2,1)S(1)} %all_to_all.10.slab_ref.own_ref), channel_id=1, source_target_pairs={{0,64},{64,128},{128,192},{192,0},{1,65},{65,129},{129,193},{193,1... | collective-permute-start | bytes 1572872 | tf_op jit(solution)/shard_map/ppermute | solution.py:288
  27.6 11.1 %collective-permute-start.2 = (bf16[8,2,128,128]{3,2,1,0:T(8,128)(2,1)S(1)}, bf16[8,2,128,128]{3,2,1,0:T(8,128)(2,1)S(1)}, u32[]{:S(2)}, u32[]{:S(2)}) collective-permute-start(bf16[8,2,128,128]{3,2,1,0:T(8,128)(2,1)S(1)} %all_to_all.10.slab_ref.own_ref), channel_id=1, source_target_pairs={{0,192},{64,0},{128,64},{192,128},{1,193},{65,1},{129,65},{193,129... | collective-permute-start | bytes 1572872 | tf_op jit(solution)/shard_map/ppermute | solution.py:288
  38.6 8.7 %collective-permute-start.1 = (bf16[4,2,128,128]{3,2,1,0:T(8,128)(2,1)S(1)}, bf16[4,2,128,128]{3,2,1,0:T(8,128)(2,1)S(1)}, u32[]{:S(2)}, u32[]{:S(2)}) collective-permute-start(bf16[4,2,128,128]{3,2,1,0:T(8,128)(2,1)S(1)} %slice.8), channel_id=1, source_target_pairs={{0,64},{64,128},{128,192},{192,0},{1,65},{65,129},{129,193},{193,1... | collective-permute-start | bytes 786440 | tf_op jit(solution)/shard_map/ppermute | solution.py:288
  38.7 8.6 %collective-permute-start.3 = (bf16[4,2,128,128]{3,2,1,0:T(8,128)(2,1)S(1)}, bf16[4,2,128,128]{3,2,1,0:T(8,128)(2,1)S(1)}, u32[]{:S(2)}, u32[]{:S(2)}) collective-permute-start(bf16[4,2,128,128]{3,2,1,0:T(8,128)(2,1)S(1)} %slice.9), channel_id=1, source_target_pairs={{0,192},{64,0},{128,64},{192,128},{1,193},{65,1},{129,65},{193,129... | collective-permute-start | bytes 786440 | tf_op jit(solution)/shard_map/ppermute | solution.py:288
  45.3 1.3 %copy-start.4 = (bf16[768,1280]{1,0:T(8,128)(2,1)}, bf16[768,1280]{1,0:T(8,128)(2,1)S(1)}, u32[]{:S(2)}) copy-start(bf16[768,1280]{1,0:T(8,128)(2,1)S(1)} %get-tuple-element.16.pick_ref) | copy-start | bytes 5898244
  47.4 40.1 %copy-start = (f32[1024]{0:T(1024)S(1)}, f32[1024]{0:T(1024)}, u32[]{:S(2)}) copy-start(f32[1024]{0:T(1024)} %param.11) | copy-start | bytes 12292
  47.5 40.1 %copy-start.2 = (s32[128]{0:T(128)S(1)}, s32[128]{0:T(128)}, u32[]{:S(2)}) copy-start(s32[128]{0:T(128)} %param.9) | copy-start | bytes 1540
  75.8 5.0 %collective-permute-start.4 = (f32[40,128]{1,0:T(8,128)S(1)}, f32[40,128]{1,0:T(8,128)S(1)}, u32[]{:S(2)}, u32[]{:S(2)}) collective-permute-start(f32[40,128]{1,0:T(8,128)S(1)} %get-tuple-element.25), channel_id=1, source_target_pairs={{0,1},{1,0},{2,3},{3,2},{4,5},{5,4},{6,7},{7,6},{8,9},{9,8},{10,11... | collective-permute-start | bytes 61448 | tf_op jit(solution)/shard_map/ppermute | solution.py:288
  80.8 5.0 %collective-permute-start.5 = (f32[40,128]{1,0:T(8,128)S(1)}, f32[40,128]{1,0:T(8,128)S(1)}, u32[]{:S(2)}, u32[]{:S(2)}) collective-permute-start(f32[40,128]{1,0:T(8,128)S(1)} %add.3.a_ref), channel_id=1, source_target_pairs={{0,2},{2,4},{4,6},{6,0},{1,3},{3,5},{5,7},{7,1},{8,10},{10,12},{12... | collective-permute-start | bytes 61448 | tf_op jit(solution)/shard_map/ppermute | solution.py:288
  82.1 4.1 %collective-permute-start.6 = (f32[40,128]{1,0:T(8,128)S(1)}, f32[40,128]{1,0:T(8,128)S(1)}, u32[]{:S(2)}, u32[]{:S(2)}) collective-permute-start(f32[40,128]{1,0:T(8,128)S(1)} %add.3.a_ref), channel_id=1, source_target_pairs={{0,4},{2,6},{4,0},{6,2},{1,5},{3,7},{5,1},{7,3},{8,12},{10,14},{12... | collective-permute-start | bytes 61448 | tf_op jit(solution)/shard_map/ppermute | solution.py:288
  84.7 2.9 %collective-permute-start.7 = (f32[40,128]{1,0:T(8,128)S(1)}, f32[40,128]{1,0:T(8,128)S(1)}, u32[]{:S(2)}, u32[]{:S(2)}) collective-permute-start(f32[40,128]{1,0:T(8,128)S(1)} %add.3.a_ref), channel_id=1, source_target_pairs={{0,6},{2,0},{4,2},{6,4},{1,7},{3,1},{5,3},{7,5},{8,14},{10,8},{12,... | collective-permute-start | bytes 61448 | tf_op jit(solution)/shard_map/ppermute | solution.py:288

commit v2 on v1

v2 whole, which is shorter than its diff:
```python
import math

import jax
import jax.numpy as jnp
from jax import lax
from jax.experimental import pallas as pl
from jax.experimental.pallas import tpu as pltpu
from jax.sharding import Mesh, PartitionSpec as P

HD = 128
D = 8192
TOK = 128
GROUP = 8
ROWS = GROUP * TOK
NX = 4
NZ = 8
SHARDS = NX * NZ
KEEP = 32
SUB = 24
SEND = SHARDS * SUB
PICK = ROWS + 2 * TOK
PAY = 8 + KEEP
SLAB = NZ * TOK
FACTOR = math.log2(math.e) / math.sqrt(HD)
LOW = -1e30
NT = (((1,), (1,)), ((), ()))
TN = (((0,), (0,)), ((), ()))
VMEM_BYTES = 40 * 1024 * 1024


def smem():
    return pl.BlockSpec(memory_space=pltpu.SMEM)


def vmem():
    return pl.BlockSpec(memory_space=pltpu.VMEM)


def params():
    return pltpu.CompilerParams(vmem_limit_bytes=VMEM_BYTES)


def wide(column):
    return jnp.broadcast_to(column, (column.shape[0], 128))


def tiled(array, count):
    return jnp.concatenate([array] * count, axis=1)


def keys_of(ref):
    return ref[:, 0].reshape(-1, HD)


def values_of(ref):
    value = ref[:, 1].reshape(-1, HD)
    return jnp.concatenate([value, jnp.ones_like(value)], axis=1)


def flash(query, key, value, old, weights_ref, rows, allowed=None):
    count = key.shape[0] // TOK
    scores = lax.dot_general(query, key, NT, preferred_element_type=jnp.float32)
    if allowed is not None:
        scores = jnp.where(allowed, scores, LOW)
    best = scores[:, 0:TOK]
    for i in range(1, count):
        best = jnp.maximum(best, scores[:, i * TOK : (i + 1) * TOK])
    top = wide(jnp.max(best, axis=1, keepdims=True))
    if old is not None:
        top = jnp.maximum(old[0], top)
    weights = jnp.exp2((scores - tiled(top, count)) * FACTOR).astype(jnp.bfloat16)
    weights_ref[rows] = weights
    both = jnp.dot(weights, value, preferred_element_type=jnp.float32)
    mixed, total = both[:, :HD], both[:, HD:]
    if old is not None:
        shrink = jnp.exp2((old[0] - top) * FACTOR)
        total = total + old[1] * shrink
        mixed = mixed + old[2] * shrink
    return top, total, mixed


def flash_heads(q_ref, key, value, state, weights_ref, fresh=False, allowed=None):
    for h in range(GROUP):
        rows = slice(h * TOK, (h + 1) * TOK)
        query = q_ref[:, h * HD : (h + 1) * HD]
        old = None if fresh else tuple(ref[rows] for ref in state)
        for ref, part in zip(state, flash(query, key, value, old, weights_ref, rows, allowed)):
            ref[rows] = part


def own_kernel(place_ref, q_ref, slab_ref, top_ref, total_ref, mixed_ref, weights_ref):
    token = lax.broadcasted_iota(jnp.int32, (TOK, SLAB), 0)
    key = lax.broadcasted_iota(jnp.int32, (TOK, SLAB), 1)
    flash_heads(
        q_ref,
        keys_of(slab_ref),
        values_of(slab_ref),
        (top_ref, total_ref, mixed_ref),
        weights_ref,
        fresh=True,
        allowed=key - token <= place_ref[1] * TOK,
    )


def pick_kernel(slot_row_ref, pick_ref):
    slot_row = slot_row_ref[...]
    target_row = jnp.where(slot_row >= 0, slot_row >> 5, -1)
    target_col = jnp.transpose(jnp.broadcast_to(target_row, (TOK, TOK)))
    first = lax.broadcasted_iota(jnp.int32, (TOK, TOK), 0)
    second = lax.broadcasted_iota(jnp.int32, (TOK, TOK), 1)
    earlier = jnp.where((target_col == target_row) & (first < second), 1, 0)
    rank = jnp.sum(earlier, axis=0, keepdims=True)
    placed = jnp.where(target_row >= 0, target_row * 2 + rank, -1)[None]
    shape = (SHARDS, SUB, TOK)
    to = lax.broadcasted_iota(jnp.int32, shape, 0)
    sub = lax.broadcasted_iota(jnp.int32, shape, 1)
    lane = lax.broadcasted_iota(jnp.int32, shape, 2)
    head = jnp.where(sub < 16, sub & 7, -1)
    same = placed == to * 2 + (sub >> 3)

    def put(at, hit):
        picked = jnp.where(hit, 1.0, 0.0).reshape(SEND, TOK)
        pick_ref[:, at : at + TOK] = picked.astype(jnp.bfloat16)

    for h in range(GROUP):
        put(h * TOK, same & (head == h))
    put(ROWS, (placed == to * 2 + (sub - 18)) & ((sub == 18) | (sub == 19)))
    put(ROWS + TOK, lane == jnp.where(sub == 16, to, jnp.where(sub == 17, to + SHARDS, -1)))


def next_kernel(
    place_ref,
    q_ref,
    left_ref,
    right_ref,
    top_in,
    total_in,
    mixed_in,
    top_ref,
    total_ref,
    mixed_ref,
    top_left_ref,
    weights_left_ref,
    weights_right_ref,
):
    x = place_ref[0]
    state = (top_ref, total_ref, mixed_ref)
    for ref, old in zip(state, (top_in, total_in, mixed_in)):
        ref[...] = old[...]

    @pl.when(x > 0)
    def _():
        flash_heads(q_ref, keys_of(left_ref), values_of(left_ref), state, weights_left_ref)

    top_left_ref[...] = top_ref[...]

    @pl.when(x == NX - 1)
    def _():
        flash_heads(q_ref, keys_of(right_ref), values_of(right_ref), state, weights_right_ref)


def last_kernel(
    place_ref,
    q_ref,
    far_left_ref,
    far_right_ref,
    text_ref,
    slots_ref,
    pick_ref,
    top_in,
    total_in,
    mixed_in,
    top_own_ref,
    top_left_ref,
    weights_own_ref,
    weights_left_ref,
    weights_right_ref,
    context_ref,
    send_ref,
    top_ref,
    total_ref,
    mixed_ref,
    weights_far_ref,
    mass_ref,
):
    x = place_ref[0]
    state = (top_ref, total_ref, mixed_ref)
    for ref, old in zip(state, (top_in, total_in, mixed_in)):
        ref[...] = old[...]
    mass_ref[...] = jnp.zeros_like(mass_ref)

    @pl.when(x >= 2)
    def _():
        key = jnp.concatenate([keys_of(far_left_ref), keys_of(far_right_ref)], axis=0)
        value = jnp.concatenate([values_of(far_left_ref), values_of(far_right_ref)], axis=0)
        flash_heads(q_ref, key, value, state, weights_far_ref)

    context = (mixed_ref[...] / total_ref[...]).astype(jnp.bfloat16)
    for h in range(GROUP):
        context_ref[:, h * HD : (h + 1) * HD] = context[h * TOK : (h + 1) * TOK]

    text = text_ref[...].astype(jnp.float32)

    @pl.when(place_ref[2] > 0)
    def _():
        eye = lax.broadcasted_iota(jnp.int32, (TOK, TOK), 0) == lax.broadcasted_iota(
            jnp.int32, (TOK, TOK), 1
        )

        def mass_of(top_then_ref, weights_ref, at):
            shares = []
            for h in range(GROUP):
                rows = slice(h * TOK, (h + 1) * TOK)
                share = jnp.exp2((top_then_ref[rows] - top_ref[rows]) * FACTOR) / total_ref[rows]
                share = jnp.sum(jnp.where(eye, share, 0.0), axis=0, keepdims=True)
                shares.append(share * text)
            share = jnp.concatenate(shares, axis=1)
            high = share.astype(jnp.bfloat16).astype(jnp.float32)
            low = share - high
            both = jnp.concatenate(
                [jnp.broadcast_to(high, (8, ROWS)), jnp.broadcast_to(low, (8, ROWS))], axis=0
            ).astype(jnp.bfloat16)
            added = jnp.dot(both, weights_ref[...], preferred_element_type=jnp.float32)
            added = added[0:1] + added[8:9]
            shift = lax.rem(at, NX) * NZ
            for i in range(NZ):
                mass_ref[pl.ds(shift + i, 1), :] = added[:, i * TOK : (i + 1) * TOK]

        mass_of(top_own_ref, weights_own_ref, x)

        @pl.when(x > 0)
        def _():
            mass_of(top_left_ref, weights_left_ref, x + NX - 1)

        @pl.when(x == NX - 1)
        def _():
            mass_of(top_in, weights_right_ref, x + 1)

        @pl.when(x >= 2)
        def _():
            mass_of(top_ref, weights_far_ref, x + 2)

    mass = mass_ref[...]
    high = mass.astype(jnp.bfloat16).astype(jnp.float32)
    low = mass - high
    both = jnp.concatenate([high, low, jnp.zeros((TOK - 2 * SHARDS, HD), jnp.float32)], axis=0)
    slots = slots_ref[...]
    slots = jnp.where(slots >= 0, (slots & (KEEP - 1)) + 1, 0).astype(jnp.float32)
    source = jnp.concatenate(
        [context, slots.astype(jnp.bfloat16), both.astype(jnp.bfloat16)], axis=0
    )
    send_ref[...] = jnp.dot(pick_ref[...], source, preferred_element_type=jnp.float32).astype(
        jnp.bfloat16
    )


def place_kernel(got_ref, rows_ref, pay_ref):
    got = got_ref[...].astype(jnp.float32).reshape(SHARDS, SUB, HD)
    mass = jnp.sum(got[:, 16:17, :] + got[:, 17:18, :], axis=0)
    slots = jnp.concatenate(
        [
            jnp.broadcast_to(got[:, 18:19, :], (SHARDS, 8, HD)),
            jnp.broadcast_to(got[:, 19:20, :], (SHARDS, 8, HD)),
            jnp.zeros((SHARDS, 8, HD), jnp.float32),
        ],
        axis=1,
    ).astype(jnp.int32)
    shape = (SHARDS, SUB, HD)
    head = lax.broadcasted_iota(jnp.int32, shape, 1) & 7
    lane = lax.broadcasted_iota(jnp.int32, shape, 2)
    parts = []
    for half in range(2):
        hit = (slots == (lane & (KEEP - 1)) + 1) & (head == (lane >> 5) + 4 * half)
        parts.append(jnp.where(hit, 1.0, 0.0).reshape(SEND, HD))
    put = jnp.concatenate(parts, axis=1).astype(jnp.bfloat16)
    rows = lax.dot_general(put, got_ref[...], TN, preferred_element_type=jnp.float32)
    rows_ref[...] = rows
    squares = jnp.sum((rows * rows).reshape(GROUP, KEEP, HD), axis=0)
    squares = jnp.sum(squares, axis=1, keepdims=True)
    pay_ref[...] = jnp.concatenate([jnp.broadcast_to(mass, (8, HD)), wide(squares)], axis=0)


def finish_kernel(a_ref, b_ref, c_ref, d_ref, rows_ref, gain_ref, text_ref, mass_ref, kept_ref):
    pay = (a_ref[...] + b_ref[...]) + (c_ref[...] + d_ref[...])
    mass_ref[...] = pay[0:1] * (1.0 - text_ref[...].astype(jnp.float32))
    factor = lax.rsqrt(pay[8:] / D + 1e-06)
    for h in range(GROUP):
        columns = slice(h * HD, (h + 1) * HD)
        kept_ref[:, columns] = (
            rows_ref[h * KEEP : (h + 1) * KEEP] * factor * gain_ref[:, columns]
        ).astype(jnp.bfloat16)


def shape_of(shape, dtype):
    return jax.ShapeDtypeStruct(shape, dtype)


def shifted(value, axis, step, count):
    return lax.ppermute(value, axis, [(i, (i + step) % count) for i in range(count)])


def cost(flops):
    return pl.CostEstimate(flops=flops, bytes_accessed=2**10, transcendentals=0)


def on_device(queries, key_rows, value_rows, text_mask, kept_slot, norm_gain):
    f32, bf16 = jnp.float32, jnp.bfloat16
    x = lax.axis_index("x")
    z = lax.axis_index("z")
    place = jnp.stack([x, z, jnp.max(text_mask)]).astype(jnp.int32)
    slot_columns = jnp.broadcast_to(kept_slot[:, None], (TOK, HD))

    both = jnp.stack([key_rows, value_rows])
    own = lax.all_to_all(
        jnp.broadcast_to(both[None], (NZ, 2, TOK, HD)), "z", split_axis=0, concat_axis=0, tiled=True
    )
    left = shifted(own, "x", 1, NX)
    right = shifted(own, "x", -1, NX)
    state = [shape_of((ROWS, HD), f32)] * 3
    kept_weights = shape_of((ROWS, SLAB), bf16)
    pick = pl.pallas_call(
        pick_kernel,
        in_specs=[vmem()],
        out_specs=vmem(),
        out_shape=shape_of((SEND, PICK), bf16),
        compiler_params=params(),
        cost_estimate=cost(5 * 10**8),
        name="pick",
    )(kept_slot[None])
    top_own, total, mixed, weights_own = pl.pallas_call(
        own_kernel,
        in_specs=[smem(), vmem(), vmem()],
        out_specs=[vmem()] * 4,
        out_shape=state + [kept_weights],
        compiler_params=params(),
        cost_estimate=cost(2 * 10**9),
        name="own_slab",
    )(place, queries, own)
    left, right, top_own, pick = lax.optimization_barrier((left, right, top_own, pick))
    half = NZ // 2
    far_left = shifted(left[:half], "x", 1, NX)
    far_right = shifted(right[half:], "x", -1, NX)
    top, total, mixed, top_left, weights_left, weights_right = pl.pallas_call(
        next_kernel,
        in_specs=[smem()] + [vmem()] * 6,
        out_specs=[vmem()] * 6,
        out_shape=state + [state[0]] + [kept_weights] * 2,
        compiler_params=params(),
        cost_estimate=cost(4 * 10**9),
        name="next_slabs",
    )(place, queries, left, right, top_own, total, mixed)
    context, send = pl.pallas_call(
        last_kernel,
        in_specs=[smem()] + [vmem()] * 14,
        out_specs=[vmem()] * 2,
        out_shape=[shape_of((TOK, GROUP * HD), bf16), shape_of((SEND, HD), bf16)],
        scratch_shapes=[pltpu.VMEM((ROWS, HD), f32)] * 3
        + [pltpu.VMEM((ROWS, SLAB), bf16), pltpu.VMEM((SHARDS, HD), f32)],
        compiler_params=params(),
        cost_estimate=cost(4 * 10**9),
        name="last_slab",
    )(
        place, queries, far_left, far_right, text_mask[None], slot_columns, pick,
        top, total, mixed, top_own, top_left, weights_own, weights_left, weights_right,
    )
    got = lax.all_to_all(
        send.reshape(SHARDS, SUB, HD), ("x", "z"), split_axis=0, concat_axis=0, tiled=True
    ).reshape(SEND, HD)
    rows, pay = pl.pallas_call(
        place_kernel,
        in_specs=[vmem()],
        out_specs=[vmem()] * 2,
        out_shape=[shape_of((GROUP * KEEP, HD), f32), shape_of((PAY, HD), f32)],
        compiler_params=params(),
        name="place_rows",
    )(got)
    pay = pay + shifted(pay, "core", 1, 2)
    pays = [pay] + [shifted(pay, "y", step, 4) for step in (1, 2, 3)]
    mass, kept = pl.pallas_call(
        finish_kernel,
        in_specs=[vmem()] * 7,
        out_specs=[vmem()] * 2,
        out_shape=[shape_of((1, TOK), f32), shape_of((KEEP, GROUP * HD), bf16)],
        compiler_params=params(),
        name="finish",
    )(*pays, rows, norm_gain[None], text_mask[None])
    return context, mass[0], kept


def solution(mesh):
    cut = Mesh(mesh.devices.reshape(NX, NZ, 4, 2), ("x", "z", "y", "core"))
    seq, tp = ("x", "z"), ("y", "core")
    placed = (P(seq, tp), P(seq, tp), P(seq, tp), P(seq), P(seq), P(tp))
    return jax.shard_map(
        on_device,
        mesh=cut,
        in_specs=placed,
        out_specs=(P(seq, tp), P(seq), P(seq, tp)),
        check_vma=False,
    )
```

time: 88.5 us -> 78.6 us (0.89)
  blocking collectives: 48.8 us -> 42.2 us
  Pallas kernels: 8.78 us -> 6.54 us
  waiting for transfers between devices: 10.8 us -> 9.66 us
  starting transfers between devices: 14.6 us -> 15.6 us
    all_to_all x1, blocking collectives: 24 us -> 17.4 us  [on_device(): lax.all_to_all(send.reshape(SHARDS, SUB, HD), ('x', 'z'), split_axis=0, c...]
    pallas_call x2 -> x3, Pallas kernels: 7.08 us -> 4.8 us  [the longest x1 2.35 us: on_device(): pl.pallas_call(own_kernel, in_specs=[smem(), vmem(), vmem()], out_specs=[...]
    convert_element_type x1 -> x0, other arithmetic: 1.37 us -> none  [on_device(): text_columns = jnp.broadcast_to(text_mask[:, None], (TOK, HD)).astype(f32)]
    reduce_max x0 -> x1, other arithmetic: none -> 1.29 us  [on_device(): place = jnp.stack([x, z, jnp.max(text_mask)]).astype(jnp.int32)]
    ppermute x8, waiting for transfers between devices: 10.8 us -> 9.66 us  [shifted(): lax.ppermute(value, axis, [(i, (i + step) % count) for i in range(count)])]
    ppermute x8, starting transfers between devices: 14.6 us -> 15.6 us  [shifted(): lax.ppermute(value, axis, [(i, (i + step) % count) for i in range(count)])]
  transfers between devices with their start and end apart: 8 -> 8, of which waited for: 4 -> 5; matrix products, arithmetic and copies ran while one was open for 2% -> 3% of each run, Pallas kernels for 4% -> 4%
where the time goes in v2:
time: 78.6 us; the launch traced here: 78.4 us
  blocking collectives  42.2 us (54%)
  starting transfers between devices  15.6 us (20%)
  waiting for transfers between devices  9.66 us (12%)
  Pallas kernels  6.54 us (8%)
  other arithmetic  2.84 us (4%)
  local copies, waits for them, and re-layouts  0.87 us (1%)
    all_to_all x1, blocking collectives, on_device(): lax.all_to_all(jnp.broadcast_to(both[None], (NZ, 2, TOK, HD)), 'z', split...  24.8 us
    all_to_all x1, blocking collectives, on_device(): lax.all_to_all(send.reshape(SHARDS, SUB, HD), ('x', 'z'), split_axis=0, c...  17.4 us
    ppermute x8, starting transfers between devices, shifted(): lax.ppermute(value, axis, [(i, (i + step) % count) for i in range(count)])  15.6 us
    ppermute x8, waiting for transfers between devices, shifted(): lax.ppermute(value, axis, [(i, (i + step) % count) for i in range(count)])  9.66 us
    pallas_call x1, Pallas kernels, on_device(): pl.pallas_call(own_kernel, in_specs=[smem(), vmem(), vmem()], out_specs=[...  2.35 us
    pallas_call x1, Pallas kernels, on_device(): pl.pallas_call(last_kernel, in_specs=[smem()] + [vmem()] * 14, out_specs=...  2.01 us
  transfers between devices with their start and end apart: 8, of which 5 were waited for; matrix products, arithmetic and copies ran while one was open for 3% of the time, Pallas kernels for 4%

profile of v2, /device:TPU:1, one launch (start us, length us, event | category | flops | bytes accessed | tf_op | source)
XLA Modules:
  0.0 78.4 jit_solution(5913238216809972368)
XLA Ops:
  0.6 0.0 copy-start.3
  0.6 0.8 %pad_maximum_fusion = bf16[2,128,128]{2,1,0:T(8,128)(2,1)S(1)} fusion(bf16[1,128,128]{2,1,0:T(8,128)(2,1)} %bitcast.17, bf16[1,128,128]{2,1,0:T(8,128)(2,1)} %bitcast.18), kind=kLoop, calls=%fused_computation | loop fusion | flops 32768 | bytes 131072 | tf_op jit(solution)/shard_map/stack | solution.py:313
  1.5 0.1 broadcast_in_dim.10
  1.6 24.8 %all_to_all.10.slab_ref = bf16[8,2,128,128]{3,2,1,0:T(8,128)(2,1)S(1)} all-to-all(bf16[8,2,128,128]{3,2,1,0:T(8,128)(2,1)S(1)} %broadcast_in_dim.10), channel_id=1, replica_groups=mesh['x'=4,'z'=8,'y'=4,'core'=2] {'z'}, dimensions={0} | all-to-all | bytes 1048576 | tf_op jit(solution)/shard_map/all_to_all | solution.py:314
  26.4 1.2 %collective-permute-start = (bf16[8,2,128,128]{3,2,1,0:T(8,128)(2,1)S(1)}, bf16[8,2,128,128]{3,2,1,0:T(8,128)(2,1)S(1)}, u32[]{:S(2)}, u32[]{:S(2)}) collective-permute-start(bf16[8,2,128,128]{3,2,1,0:T(8,128)(2,1)S(1)} %all_to_all.10.slab_ref), channel_id=1, source_target_pairs={{0,64},{64,128},{128,192},{192,0},{1,65},{65,129},{129,193},{193,1... | collective-permute-start | bytes 1572872 | tf_op jit(solution)/shard_map/ppermute | solution.py:299
  27.6 1.5 %collective-permute-start.1 = (bf16[8,2,128,128]{3,2,1,0:T(8,128)(2,1)S(1)}, bf16[8,2,128,128]{3,2,1,0:T(8,128)(2,1)S(1)}, u32[]{:S(2)}, u32[]{:S(2)}) collective-permute-start(bf16[8,2,128,128]{3,2,1,0:T(8,128)(2,1)S(1)} %all_to_all.10.slab_ref), channel_id=1, source_target_pairs={{0,192},{64,0},{128,64},{192,128},{1,193},{65,1},{129,65},{193,129... | collective-permute-start | bytes 1572872 | tf_op jit(solution)/shard_map/ppermute | solution.py:299
  29.0 1.3 %reduce_max.9 = s32[]{:T(128)} reduce(s32[128]{0:T(128)} %param.9, s32[]{:T(128)} %constant.11.clone.1), dimensions={0}, to_apply=%region_0.0 | reduce | flops 127 | bytes 520 | tf_op jit(solution)/shard_map/reduce_max | solution.py:310
  30.3 0.0 copy-start.1
  30.3 0.7 copy-done.1
  31.0 0.4 pick.1.pick_ref
  31.4 0.7 pad_add_fusion.place_ref
  32.2 0.0 copy-done.3
  32.2 2.4 %own_slab.1 = (f32[1024,128]{1,0:T(8,128)S(1)}, f32[1024,128]{1,0:T(8,128)S(1)}, f32[1024,128]{1,0:T(8,128)S(1)}, bf16[1024,1024]{1,0:T(8,128)(2,1)S(1)}) custom-call(s32[3]{0:T(128)S(1)} %pad_add_fusion.place_ref, bf16[128,1024]{1,0:T(8,128)(2,1)S(1)} %copy-done.3, bf16[8,2,128,128]{3,2,1,0:T(8,128)(2,1)S(1)} %all_to_all.10.slab_ref), custom_call_target="tpu_custom_call" | custom-call | flops 2000000000 | bytes 1024 | tf_op jit(solution)/shard_map/own_slab/pallas_call | solution.py:330
  34.5 4.0 %collective-permute-done.left_ref = bf16[8,2,128,128]{3,2,1,0:T(8,128)(2,1)S(1)} collective-permute-done((bf16[8,2,128,128]{3,2,1,0:T(8,128)(2,1)S(1)}, bf16[8,2,128,128]{3,2,1,0:T(8,128)(2,1)S(1)}, u32[]{:S(2)}, u32[]{:S(2)}) %collective-permute-start) | collective-permute-done | bytes 524320 | tf_op jit(solution)/shard_map/ppermute | solution.py:299
  38.5 0.0 collective-permute-done.1.right_ref
  38.6 1.0 %collective-permute-start.2 = (bf16[4,2,128,128]{3,2,1,0:T(8,128)(2,1)S(1)}, bf16[4,2,128,128]{3,2,1,0:T(8,128)(2,1)S(1)}, u32[]{:S(2)}, u32[]{:S(2)}) collective-permute-start(bf16[4,2,128,128]{3,2,1,0:T(8,128)(2,1)S(1)} %slice.6), channel_id=1, source_target_pairs={{0,64},{64,128},{128,192},{192,0},{1,65},{65,129},{129,193},{193,1... | collective-permute-start | bytes 786440 | tf_op jit(solution)/shard_map/ppermute | solution.py:299
  39.6 1.8 %collective-permute-start.3 = (bf16[4,2,128,128]{3,2,1,0:T(8,128)(2,1)S(1)}, bf16[4,2,128,128]{3,2,1,0:T(8,128)(2,1)S(1)}, u32[]{:S(2)}, u32[]{:S(2)}) collective-permute-start(bf16[4,2,128,128]{3,2,1,0:T(8,128)(2,1)S(1)} %slice.7), channel_id=1, source_target_pairs={{0,192},{64,0},{128,64},{192,128},{1,193},{65,1},{129,65},{193,129... | collective-permute-start | bytes 786440 | tf_op jit(solution)/shard_map/ppermute | solution.py:299
  41.4 0.0 copy-start.2
  41.4 0.7 next_slabs.1
  42.1 3.0 %collective-permute-done.2.far_left_ref = bf16[4,2,128,128]{3,2,1,0:T(8,128)(2,1)S(1)} collective-permute-done((bf16[4,2,128,128]{3,2,1,0:T(8,128)(2,1)S(1)}, bf16[4,2,128,128]{3,2,1,0:T(8,128)(2,1)S(1)}, u32[]{:S(2)}, u32[]{:S(2)}) %collective-permute-start.2) | collective-permute-done | bytes 262176 | tf_op jit(solution)/shard_map/ppermute | solution.py:299
  45.1 0.0 collective-permute-done.3.far_right_ref
  45.1 0.1 broadcast_in_dim.25.slots_ref
  45.2 0.0 copy-done.2
  45.2 0.0 copy-start
  45.2 2.0 %last_slab.1 = (bf16[128,1024]{1,0:T(8,128)(2,1)}, bf16[768,128]{1,0:T(8,128)(2,1)S(1)}) custom-call(s32[3]{0:T(128)S(1)} %pad_add_fusion.place_ref, bf16[128,1024]{1,0:T(8,128)(2,1)S(1)} %copy-done.3, bf16[4,2,128,128]{3,2,1,0:T(8,128)(2,1)S(1)} %collective-permute-done.2.far_left_ref, bf16[4,2,128,128]{3,2,1,0:T(8,128)(2,1)S(1)} %collective-permute-done.3.far_right_ref, ...), custom_call_target="tpu_custom_call" | custom-call | flops 4000000000 | bytes 1024 | tf_op jit(solution)/shard_map/last_slab/pallas_call | solution.py:352
  47.2 17.4 %all_to_all.11 = bf16[32,24,128]{2,1,0:T(8,128)(2,1)S(1)} all-to-all(bf16[32,24,128]{2,1,0:T(8,128)(2,1)S(1)} %bitcast.12), channel_id=1, replica_groups=mesh['x'=4,'z'=8,'y'=4,'core'=2] {'x','z'}, dimensions={0} | all-to-all | bytes 393216 | tf_op jit(solution)/shard_map/all_to_all | solution.py:366
  64.6 0.4 place_rows.1
  65.0 5.1 %collective-permute-start.4 = (f32[40,128]{1,0:T(8,128)S(1)}, f32[40,128]{1,0:T(8,128)S(1)}, u32[]{:S(2)}, u32[]{:S(2)}) collective-permute-start(f32[40,128]{1,0:T(8,128)S(1)} %get-tuple-element.39), channel_id=1, source_target_pairs={{0,1},{1,0},{2,3},{3,2},{4,5},{5,4},{6,7},{7,6},{8,9},{9,8},{10,11... | collective-permute-start | bytes 61448 | tf_op jit(solution)/shard_map/ppermute | solution.py:299
  70.0 0.8 %collective-permute-done.4 = f32[40,128]{1,0:T(8,128)S(1)} collective-permute-done((f32[40,128]{1,0:T(8,128)S(1)}, f32[40,128]{1,0:T(8,128)S(1)}, u32[]{:S(2)}, u32[]{:S(2)}) %collective-permute-start.4) | collective-permute-done | bytes 20512 | tf_op jit(solution)/shard_map/ppermute | solution.py:299
  70.9 1.3 %collective-permute-start.5 = (f32[40,128]{1,0:T(8,128)S(1)}, f32[40,128]{1,0:T(8,128)S(1)}, u32[]{:S(2)}, u32[]{:S(2)}) collective-permute-start(f32[40,128]{1,0:T(8,128)S(1)} %add.3.a_ref), channel_id=1, source_target_pairs={{0,2},{2,4},{4,6},{6,0},{1,3},{3,5},{5,7},{7,1},{8,10},{10,12},{12... | collective-permute-start | bytes 61448 | tf_op jit(solution)/shard_map/ppermute | solution.py:299
  72.2 2.6 %collective-permute-start.6 = (f32[40,128]{1,0:T(8,128)S(1)}, f32[40,128]{1,0:T(8,128)S(1)}, u32[]{:S(2)}, u32[]{:S(2)}) collective-permute-start(f32[40,128]{1,0:T(8,128)S(1)} %add.3.a_ref), channel_id=1, source_target_pairs={{0,4},{2,6},{4,0},{6,2},{1,5},{3,7},{5,1},{7,3},{8,12},{10,14},{12... | collective-permute-start | bytes 61448 | tf_op jit(solution)/shard_map/ppermute | solution.py:299
  74.8 1.1 %collective-permute-start.7 = (f32[40,128]{1,0:T(8,128)S(1)}, f32[40,128]{1,0:T(8,128)S(1)}, u32[]{:S(2)}, u32[]{:S(2)}) collective-permute-start(f32[40,128]{1,0:T(8,128)S(1)} %add.3.a_ref), channel_id=1, source_target_pairs={{0,6},{2,0},{4,2},{6,4},{1,7},{3,1},{5,3},{7,5},{8,14},{10,8},{12,... | collective-permute-start | bytes 61448 | tf_op jit(solution)/shard_map/ppermute | solution.py:299
  75.9 0.0 collective-permute-done.5.b_ref
  75.9 0.4 collective-permute-done.6.c_ref
  76.3 1.4 %collective-permute-done.7.d_ref = f32[40,128]{1,0:T(8,128)S(1)} collective-permute-done((f32[40,128]{1,0:T(8,128)S(1)}, f32[40,128]{1,0:T(8,128)S(1)}, u32[]{:S(2)}, u32[]{:S(2)}) %collective-permute-start.7) | collective-permute-done | bytes 20512 | tf_op jit(solution)/shard_map/ppermute | solution.py:299
  77.7 0.0 copy-done
  77.7 0.7 finish.1
  (3 shorter events, 0.0 us)
Async XLA Ops:
  0.6 31.5 %copy-start.3 = (bf16[128,1024]{1,0:T(8,128)(2,1)S(1)}, bf16[128,1024]{1,0:T(8,128)(2,1)}, u32[]{:S(2)}) copy-start(bf16[128,1024]{1,0:T(8,128)(2,1)} %q_ref.5) | copy-start | bytes 786436
  26.4 12.2 %collective-permute-start = (bf16[8,2,128,128]{3,2,1,0:T(8,128)(2,1)S(1)}, bf16[8,2,128,128]{3,2,1,0:T(8,128)(2,1)S(1)}, u32[]{:S(2)}, u32[]{:S(2)}) collective-permute-start(bf16[8,2,128,128]{3,2,1,0:T(8,128)(2,1)S(1)} %all_to_all.10.slab_ref), channel_id=1, source_target_pairs={{0,64},{64,128},{128,192},{192,0},{1,65},{65,129},{129,193},{193,1... | collective-permute-start | bytes 1572872 | tf_op jit(solution)/shard_map/ppermute | solution.py:299
  27.6 11.0 %collective-permute-start.1 = (bf16[8,2,128,128]{3,2,1,0:T(8,128)(2,1)S(1)}, bf16[8,2,128,128]{3,2,1,0:T(8,128)(2,1)S(1)}, u32[]{:S(2)}, u32[]{:S(2)}) collective-permute-start(bf16[8,2,128,128]{3,2,1,0:T(8,128)(2,1)S(1)} %all_to_all.10.slab_ref), channel_id=1, source_target_pairs={{0,192},{64,0},{128,64},{192,128},{1,193},{65,1},{129,65},{193,129... | collective-permute-start | bytes 1572872 | tf_op jit(solution)/shard_map/ppermute | solution.py:299
  30.3 0.7 copy-start.1
  38.6 6.5 %collective-permute-start.2 = (bf16[4,2,128,128]{3,2,1,0:T(8,128)(2,1)S(1)}, bf16[4,2,128,128]{3,2,1,0:T(8,128)(2,1)S(1)}, u32[]{:S(2)}, u32[]{:S(2)}) collective-permute-start(bf16[4,2,128,128]{3,2,1,0:T(8,128)(2,1)S(1)} %slice.6), channel_id=1, source_target_pairs={{0,64},{64,128},{128,192},{192,0},{1,65},{65,129},{129,193},{193,1... | collective-permute-start | bytes 786440 | tf_op jit(solution)/shard_map/ppermute | solution.py:299
  39.6 5.5 %collective-permute-start.3 = (bf16[4,2,128,128]{3,2,1,0:T(8,128)(2,1)S(1)}, bf16[4,2,128,128]{3,2,1,0:T(8,128)(2,1)S(1)}, u32[]{:S(2)}, u32[]{:S(2)}) collective-permute-start(bf16[4,2,128,128]{3,2,1,0:T(8,128)(2,1)S(1)} %slice.7), channel_id=1, source_target_pairs={{0,192},{64,0},{128,64},{192,128},{1,193},{65,1},{129,65},{193,129... | collective-permute-start | bytes 786440 | tf_op jit(solution)/shard_map/ppermute | solution.py:299
  41.4 3.7 %copy-start.2 = (s32[128]{0:T(128)S(1)}, s32[128]{0:T(128)}, u32[]{:S(2)}) copy-start(s32[128]{0:T(128)} %param.9) | copy-start | bytes 1540
  45.2 32.5 %copy-start = (f32[1024]{0:T(1024)S(1)}, f32[1024]{0:T(1024)}, u32[]{:S(2)}) copy-start(f32[1024]{0:T(1024)} %param.11) | copy-start | bytes 12292
  65.0 5.9 %collective-permute-start.4 = (f32[40,128]{1,0:T(8,128)S(1)}, f32[40,128]{1,0:T(8,128)S(1)}, u32[]{:S(2)}, u32[]{:S(2)}) collective-permute-start(f32[40,128]{1,0:T(8,128)S(1)} %get-tuple-element.39), channel_id=1, source_target_pairs={{0,1},{1,0},{2,3},{3,2},{4,5},{5,4},{6,7},{7,6},{8,9},{9,8},{10,11... | collective-permute-start | bytes 61448 | tf_op jit(solution)/shard_map/ppermute | solution.py:299
  70.9 5.0 %collective-permute-start.5 = (f32[40,128]{1,0:T(8,128)S(1)}, f32[40,128]{1,0:T(8,128)S(1)}, u32[]{:S(2)}, u32[]{:S(2)}) collective-permute-start(f32[40,128]{1,0:T(8,128)S(1)} %add.3.a_ref), channel_id=1, source_target_pairs={{0,2},{2,4},{4,6},{6,0},{1,3},{3,5},{5,7},{7,1},{8,10},{10,12},{12... | collective-permute-start | bytes 61448 | tf_op jit(solution)/shard_map/ppermute | solution.py:299
  72.2 4.1 %collective-permute-start.6 = (f32[40,128]{1,0:T(8,128)S(1)}, f32[40,128]{1,0:T(8,128)S(1)}, u32[]{:S(2)}, u32[]{:S(2)}) collective-permute-start(f32[40,128]{1,0:T(8,128)S(1)} %add.3.a_ref), channel_id=1, source_target_pairs={{0,4},{2,6},{4,0},{6,2},{1,5},{3,7},{5,1},{7,3},{8,12},{10,14},{12... | collective-permute-start | bytes 61448 | tf_op jit(solution)/shard_map/ppermute | solution.py:299
  74.8 2.9 %collective-permute-start.7 = (f32[40,128]{1,0:T(8,128)S(1)}, f32[40,128]{1,0:T(8,128)S(1)}, u32[]{:S(2)}, u32[]{:S(2)}) collective-permute-start(f32[40,128]{1,0:T(8,128)S(1)} %add.3.a_ref), channel_id=1, source_target_pairs={{0,6},{2,0},{4,2},{6,4},{1,7},{3,1},{5,3},{7,5},{8,14},{10,8},{12,... | collective-permute-start | bytes 61448 | tf_op jit(solution)/shard_map/ppermute | solution.py:299

commit v3 on v2

v3 whole, which is shorter than its diff:
```python
import math

import jax
import jax.numpy as jnp
from jax import lax
from jax.experimental import pallas as pl
from jax.experimental.pallas import tpu as pltpu
from jax.sharding import Mesh, PartitionSpec as P

HD = 128
D = 8192
TOK = 128
GROUP = 8
ROWS = GROUP * TOK
NX = 4
NZ = 8
SHARDS = NX * NZ
KEEP = 32
SUB = 24
SEND = SHARDS * SUB
EIGHT = SHARDS * 8
TP = 8
SLAB = NZ * TOK
FACTOR = math.log2(math.e) / math.sqrt(HD)
LOW = -1e30
NT = (((1,), (1,)), ((), ()))
TN = (((0,), (0,)), ((), ()))
VMEM_BYTES = 40 * 1024 * 1024


def smem():
    return pl.BlockSpec(memory_space=pltpu.SMEM)


def vmem():
    return pl.BlockSpec(memory_space=pltpu.VMEM)


def params():
    return pltpu.CompilerParams(vmem_limit_bytes=VMEM_BYTES)


def wide(column):
    return jnp.broadcast_to(column, (column.shape[0], 128))


def tiled(array, count):
    return jnp.concatenate([array] * count, axis=1)


def diagonal(rows=TOK):
    return lax.broadcasted_iota(jnp.int32, (rows, TOK), 0) == lax.broadcasted_iota(
        jnp.int32, (rows, TOK), 1
    )


def row_of(column, eye):
    return jnp.sum(jnp.where(eye, column, 0.0), axis=0, keepdims=True)


def rows_of(ref, eye):
    return jnp.concatenate(
        [row_of(ref[h * TOK : (h + 1) * TOK], eye) for h in range(GROUP)], axis=0
    )


def keys_of(same_ref, other_ref):
    return jnp.concatenate([ref[:, 0].reshape(-1, HD) for ref in (same_ref, other_ref)], axis=0)


def values_of(same_ref, other_ref):
    value = jnp.concatenate(
        [ref[:, 1].reshape(-1, HD) for ref in (same_ref, other_ref)], axis=0
    )
    return jnp.concatenate([value, jnp.ones_like(value)], axis=1)


def shard_of(chunk, z):
    parity = z & 1
    return 2 * (chunk & 3) + jnp.where(chunk < 4, parity, 1 - parity)


def flash(query, key, value, old, weights_ref, rows, allowed=None):
    count = key.shape[0] // TOK
    scores = lax.dot_general(query, key, NT, preferred_element_type=jnp.float32)
    if allowed is not None:
        scores = jnp.where(allowed, scores, LOW)
    best = scores[:, 0:TOK]
    for i in range(1, count):
        best = jnp.maximum(best, scores[:, i * TOK : (i + 1) * TOK])
    top = wide(jnp.max(best, axis=1, keepdims=True))
    if old is not None:
        top = jnp.maximum(old[0], top)
    weights = jnp.exp2((scores - tiled(top, count)) * FACTOR).astype(jnp.bfloat16)
    weights_ref[rows] = weights
    both = jnp.dot(weights, value, preferred_element_type=jnp.float32)
    mixed, total = both[:, :HD], both[:, HD:]
    if old is not None:
        shrink = jnp.exp2((old[0] - top) * FACTOR)
        total = total + old[1] * shrink
        mixed = mixed + old[2] * shrink
    return top, total, mixed


def flash_heads(q_ref, key, value, state, weights_ref, fresh=False, allowed=None):
    for h in range(GROUP):
        rows = slice(h * TOK, (h + 1) * TOK)
        query = q_ref[:, h * HD : (h + 1) * HD]
        old = None if fresh else tuple(ref[rows] for ref in state)
        for ref, part in zip(state, flash(query, key, value, old, weights_ref, rows, allowed)):
            ref[rows] = part


def own_kernel(
    place_ref,
    q_ref,
    same_ref,
    other_ref,
    top_ref,
    total_ref,
    mixed_ref,
    level_ref,
    weights_ref,
):
    z = place_ref[1]
    token = lax.broadcasted_iota(jnp.int32, (TOK, SLAB), 0)
    lane = lax.broadcasted_iota(jnp.int32, (TOK, SLAB), 1)
    key = shard_of(lane >> 7, z) * TOK + (lane & (TOK - 1))
    flash_heads(
        q_ref,
        keys_of(same_ref, other_ref),
        values_of(same_ref, other_ref),
        (top_ref, total_ref, mixed_ref),
        weights_ref,
        fresh=True,
        allowed=key - token <= z * TOK,
    )
    level_ref[...] = rows_of(top_ref, diagonal())


def pick_kernel(slot_row_ref, rows_ref, rest_ref):
    slot_row = slot_row_ref[...]
    target_row = jnp.where(slot_row >= 0, slot_row >> 5, -1)
    target_col = jnp.transpose(jnp.broadcast_to(target_row, (TOK, TOK)))
    first = lax.broadcasted_iota(jnp.int32, (TOK, TOK), 0)
    second = lax.broadcasted_iota(jnp.int32, (TOK, TOK), 1)
    earlier = jnp.where((target_col == target_row) & (first < second), 1, 0)
    rank = jnp.sum(earlier, axis=0, keepdims=True)
    placed = jnp.where(target_row >= 0, target_row * 2 + rank, -1)[None]
    shape = (SHARDS, 8, TOK)
    to = lax.broadcasted_iota(jnp.int32, shape, 0)
    sub = lax.broadcasted_iota(jnp.int32, shape, 1)
    lane = lax.broadcasted_iota(jnp.int32, shape, 2)

    def one_hot(hit):
        return jnp.where(hit, 1.0, 0.0).reshape(EIGHT, TOK).astype(jnp.bfloat16)

    same = placed == to * 2 + (sub >> 2)
    for h in range(4):
        rows_ref[:, h * TOK : (h + 1) * TOK] = one_hot(same & ((sub & 3) == h))
    rest_ref[:, :TOK] = one_hot((placed == to * 2 + (sub - 2)) & ((sub == 2) | (sub == 3)))
    rest_ref[:, TOK:] = one_hot(lane == jnp.where(sub == 0, to, jnp.where(sub == 1, to + SHARDS, -1)))


def next_kernel(
    place_ref,
    q_ref,
    left_same_ref,
    left_other_ref,
    right_same_ref,
    right_other_ref,
    top_in,
    total_in,
    mixed_in,
    top_ref,
    total_ref,
    mixed_ref,
    level_left_ref,
    level_right_ref,
    weights_left_ref,
    weights_right_ref,
):
    x = place_ref[0]
    eye = diagonal()
    state = (top_ref, total_ref, mixed_ref)
    for ref, old in zip(state, (top_in, total_in, mixed_in)):
        ref[...] = old[...]

    @pl.when(x > 0)
    def _():
        pair = (left_same_ref, left_other_ref)
        flash_heads(q_ref, keys_of(*pair), values_of(*pair), state, weights_left_ref)

    level_left_ref[...] = rows_of(top_ref, eye)

    @pl.when(x == NX - 1)
    def _():
        pair = (right_same_ref, right_other_ref)
        flash_heads(q_ref, keys_of(*pair), values_of(*pair), state, weights_right_ref)

    level_right_ref[...] = rows_of(top_ref, eye)


def last_kernel(
    place_ref,
    q_ref,
    far_same_ref,
    far_other_ref,
    text_ref,
    slots_ref,
    pick_rows_ref,
    pick_rest_ref,
    top_in,
    total_in,
    mixed_in,
    level_own_ref,
    level_left_ref,
    level_right_ref,
    weights_own_ref,
    weights_left_ref,
    weights_right_ref,
    context_ref,
    send_ref,
    top_ref,
    total_ref,
    mixed_ref,
    weights_far_ref,
    mass_ref,
):
    x = place_ref[0]
    state = (top_ref, total_ref, mixed_ref)
    for ref, old in zip(state, (top_in, total_in, mixed_in)):
        ref[...] = old[...]
    mass_ref[...] = jnp.zeros_like(mass_ref)

    @pl.when(x >= 2)
    def _():
        pair = (far_same_ref, far_other_ref)
        flash_heads(q_ref, keys_of(*pair), values_of(*pair), state, weights_far_ref)

    context = (mixed_ref[...] / total_ref[...]).astype(jnp.bfloat16)
    for h in range(GROUP):
        context_ref[:, h * HD : (h + 1) * HD] = context[h * TOK : (h + 1) * TOK]

    @pl.when(place_ref[2] > 0)
    def _():
        eye = diagonal()
        level = rows_of(top_ref, eye)
        part = text_ref[...].astype(jnp.float32) / rows_of(total_ref, eye)

        def mass_of(level_then, weights_ref, at):
            share = jnp.exp2((level_then - level) * FACTOR) * part
            share = jnp.concatenate([share[h : h + 1] for h in range(GROUP)], axis=1)
            high = share.astype(jnp.bfloat16).astype(jnp.float32)
            low = share - high
            both = jnp.concatenate(
                [jnp.broadcast_to(high, (8, ROWS)), jnp.broadcast_to(low, (8, ROWS))], axis=0
            ).astype(jnp.bfloat16)
            added = jnp.dot(both, weights_ref[...], preferred_element_type=jnp.float32)
            added = added[0:1] + added[8:9]
            shift = lax.rem(at, NX) * NZ
            for i in range(NZ):
                to = shift + shard_of(i, place_ref[1])
                mass_ref[pl.ds(to, 1), :] = added[:, i * TOK : (i + 1) * TOK]

        mass_of(level_own_ref[...], weights_own_ref, x)

        @pl.when(x > 0)
        def _():
            mass_of(level_left_ref[...], weights_left_ref, x + NX - 1)

        @pl.when(x == NX - 1)
        def _():
            mass_of(level_right_ref[...], weights_right_ref, x + 1)

        @pl.when(x >= 2)
        def _():
            mass_of(level, weights_far_ref, x + 2)

    half = ROWS // 2
    sides = jnp.concatenate([context[:half], context[half:]], axis=1)
    sides = jnp.dot(pick_rows_ref[...], sides, preferred_element_type=jnp.float32)
    mass = mass_ref[...]
    high = mass.astype(jnp.bfloat16).astype(jnp.float32)
    low = mass - high
    slots = slots_ref[...]
    slots = jnp.where(slots >= 0, (slots & (KEEP - 1)) + 1, 0).astype(jnp.float32)
    rest = jnp.concatenate(
        [slots, high, low, jnp.zeros((TOK - 2 * SHARDS, HD), jnp.float32)], axis=0
    )
    rest = jnp.dot(
        pick_rest_ref[...], rest.astype(jnp.bfloat16), preferred_element_type=jnp.float32
    )
    parts = [part.reshape(SHARDS, 8, HD) for part in (sides[:, :HD], sides[:, HD:], rest)]
    send = jnp.concatenate(parts, axis=1).reshape(SEND, HD)
    send_ref[...] = send.astype(jnp.bfloat16)


def place_kernel(got_ref, rows_ref, pay_ref):
    got = got_ref[...].astype(jnp.float32).reshape(SHARDS, SUB, HD)
    mass = jnp.sum(got[:, 16:17, :] + got[:, 17:18, :], axis=0)
    slots = jnp.concatenate(
        [
            jnp.broadcast_to(got[:, 18:19, :], (SHARDS, 4, HD)),
            jnp.broadcast_to(got[:, 19:20, :], (SHARDS, 4, HD)),
        ],
        axis=1,
    ).astype(jnp.int32)
    shape = (SHARDS, 8, HD)
    head = lax.broadcasted_iota(jnp.int32, shape, 1) & 3
    lane = lax.broadcasted_iota(jnp.int32, shape, 2)
    hit = (slots == (lane & (KEEP - 1)) + 1) & (head == lane >> 5)
    put = jnp.where(hit, 1.0, 0.0).reshape(EIGHT, HD).astype(jnp.bfloat16)
    sides = jnp.concatenate(
        [got[:, 0:8].reshape(EIGHT, HD), got[:, 8:16].reshape(EIGHT, HD)], axis=1
    ).astype(jnp.bfloat16)
    rows = lax.dot_general(put, sides, TN, preferred_element_type=jnp.float32)
    rows_ref[...] = rows
    squares = jnp.sum((rows * rows).reshape(4, KEEP, 2 * HD), axis=0)
    squares = jnp.sum(squares, axis=1, keepdims=True)
    squares = row_of(wide(squares), diagonal(KEEP))
    pay = jnp.concatenate([mass, squares, jnp.zeros((6, HD), jnp.float32)], axis=0)
    pay_ref[...] = jnp.broadcast_to(pay[None], (TP, 8, HD))


def finish_kernel(pay_ref, rows_ref, gain_ref, text_ref, mass_ref, kept_ref):
    pay = jnp.sum(pay_ref[...], axis=0)
    mass_ref[...] = pay[0:1] * (1.0 - text_ref[...].astype(jnp.float32))
    squares = jnp.where(diagonal(KEEP), jnp.broadcast_to(pay[1:2], (KEEP, HD)), 0.0)
    factor = lax.rsqrt(wide(jnp.sum(squares, axis=1, keepdims=True)) / D + 1e-06)
    for h in range(GROUP):
        columns = slice(h * HD, (h + 1) * HD)
        rows = slice((h & 3) * KEEP, ((h & 3) + 1) * KEEP)
        side = slice((h >> 2) * HD, ((h >> 2) + 1) * HD)
        kept_ref[:, columns] = (rows_ref[rows, side] * factor * gain_ref[:, columns]).astype(
            jnp.bfloat16
        )


def shape_of(shape, dtype):
    return jax.ShapeDtypeStruct(shape, dtype)


def shifted(value, axis, step, count):
    return lax.ppermute(value, axis, [(i, (i + step) % count) for i in range(count)])


def cost(flops):
    return pl.CostEstimate(flops=flops, bytes_accessed=2**10, transcendentals=0)


def on_device(queries, key_rows, value_rows, text_mask, kept_slot, norm_gain):
    f32, bf16 = jnp.float32, jnp.bfloat16
    x = lax.axis_index("x")
    z = lax.axis_index(("zh", "zl"))
    place = jnp.stack([x, z, jnp.max(text_mask)]).astype(jnp.int32)
    slot_columns = jnp.broadcast_to(kept_slot[:, None], (TOK, HD))

    both = jnp.stack([key_rows, value_rows])
    same = lax.all_to_all(
        jnp.broadcast_to(both[None], (NZ // 2, 2, TOK, HD)),
        "zh",
        split_axis=0,
        concat_axis=0,
        tiled=True,
    )
    other = shifted(same, "zl", 1, 2)
    left = [shifted(part, "x", 1, NX) for part in (same, other)]
    right = [shifted(part, "x", -1, NX) for part in (same, other)]
    far = [shifted(left[0], "x", 1, NX), shifted(right[1], "x", -1, NX)]
    state = [shape_of((ROWS, HD), f32)] * 3
    kept_weights = shape_of((ROWS, SLAB), bf16)
    level = shape_of((GROUP, TOK), f32)
    pick = pl.pallas_call(
        pick_kernel,
        in_specs=[vmem()],
        out_specs=[vmem()] * 2,
        out_shape=[shape_of((EIGHT, 4 * TOK), bf16), shape_of((EIGHT, 2 * TOK), bf16)],
        compiler_params=params(),
        cost_estimate=cost(5 * 10**8),
        name="pick",
    )(kept_slot[None])
    top, total, mixed, level_own, weights_own = pl.pallas_call(
        own_kernel,
        in_specs=[smem()] + [vmem()] * 3,
        out_specs=[vmem()] * 5,
        out_shape=state + [level, kept_weights],
        compiler_params=params(),
        cost_estimate=cost(2 * 10**9),
        name="own_slab",
    )(place, queries, same, other)
    top, total, mixed, level_left, level_right, weights_left, weights_right = pl.pallas_call(
        next_kernel,
        in_specs=[smem()] + [vmem()] * 8,
        out_specs=[vmem()] * 7,
        out_shape=state + [level] * 2 + [kept_weights] * 2,
        compiler_params=params(),
        cost_estimate=cost(4 * 10**9),
        name="next_slabs",
    )(place, queries, *left, *right, top, total, mixed)
    context, send = pl.pallas_call(
        last_kernel,
        in_specs=[smem()] + [vmem()] * 16,
        out_specs=[vmem()] * 2,
        out_shape=[shape_of((TOK, GROUP * HD), bf16), shape_of((SEND, HD), bf16)],
        scratch_shapes=[pltpu.VMEM((ROWS, HD), f32)] * 3
        + [pltpu.VMEM((ROWS, SLAB), bf16), pltpu.VMEM((SHARDS, HD), f32)],
        compiler_params=params(),
        cost_estimate=cost(4 * 10**9),
        name="last_slab",
    )(
        place, queries, *far, text_mask[None], slot_columns, *pick,
        top, total, mixed, level_own, level_left, level_right,
        weights_own, weights_left, weights_right,
    )
    got = lax.all_to_all(
        send.reshape(SHARDS, SUB, HD), ("x", "zh", "zl"), split_axis=0, concat_axis=0, tiled=True
    ).reshape(SEND, HD)
    rows, pay = pl.pallas_call(
        place_kernel,
        in_specs=[vmem()],
        out_specs=[vmem()] * 2,
        out_shape=[shape_of((4 * KEEP, 2 * HD), f32), shape_of((TP, 8, HD), f32)],
        compiler_params=params(),
        name="place_rows",
    )(got)
    pay = lax.all_to_all(pay, ("y", "core"), split_axis=0, concat_axis=0, tiled=True)
    mass, kept = pl.pallas_call(
        finish_kernel,
        in_specs=[vmem()] * 4,
        out_specs=[vmem()] * 2,
        out_shape=[shape_of((1, TOK), f32), shape_of((KEEP, GROUP * HD), bf16)],
        compiler_params=params(),
        name="finish",
    )(pay, rows, norm_gain[None], text_mask[None])
    return context, mass[0], kept


def solution(mesh):
    cut = Mesh(mesh.devices.reshape(NX, NZ // 2, 2, 4, 2), ("x", "zh", "zl", "y", "core"))
    seq, tp = ("x", "zh", "zl"), ("y", "core")
    placed = (P(seq, tp), P(seq, tp), P(seq, tp), P(seq), P(seq), P(tp))
    return jax.shard_map(
        on_device,
        mesh=cut,
        in_specs=placed,
        out_specs=(P(seq, tp), P(seq), P(seq, tp)),
        check_vma=False,
    )
```

time: 78.6 us -> 77 us (0.980)
  blocking collectives: 42.2 us -> 51.5 us
  starting transfers between devices: 15.6 us -> 9.29 us
  waiting for transfers between devices: 9.66 us -> 5.16 us
    all_to_all x2 -> x3, blocking collectives: 42.2 us -> 51.5 us  [the longest x1 20.1 us: on_device(): lax.all_to_all(send.reshape(SHARDS, SUB, HD), ('x', 'zh', 'zl'), split_ax...]
    ppermute x8 -> x7, starting transfers between devices: 15.6 us -> 9.29 us  [shifted(): lax.ppermute(value, axis, [(i, (i + step) % count) for i in range(count)])]
    ppermute x8 -> x7, waiting for transfers between devices: 9.66 us -> 5.16 us  [shifted(): lax.ppermute(value, axis, [(i, (i + step) % count) for i in range(count)])]
  transfers between devices with their start and end apart: 8 -> 7, of which waited for: 5 -> 4; matrix products, arithmetic and copies ran while one was open for 3% -> 3% of each run, Pallas kernels for 4% -> 4%
where the time goes in v3:
time: 77 us; the launch traced here: 76.8 us
  blocking collectives  51.5 us (67%)
  starting transfers between devices  9.29 us (12%)
  Pallas kernels  6.52 us (8%)
  waiting for transfers between devices  5.16 us (7%)
  other arithmetic  2.84 us (4%)
  local copies, waits for them, and re-layouts  0.79 us (1%)
    all_to_all x1, blocking collectives, on_device(): lax.all_to_all(send.reshape(SHARDS, SUB, HD), ('x', 'zh', 'zl'), split_ax...  20.1 us
    all_to_all x1, blocking collectives, on_device(): lax.all_to_all(jnp.broadcast_to(both[None], (NZ // 2, 2, TOK, HD)), 'zh',...  17.9 us
    all_to_all x1, blocking collectives, on_device(): lax.all_to_all(pay, ('y', 'core'), split_axis=0, concat_axis=0, tiled=True)  13.5 us
    ppermute x7, starting transfers between devices, shifted(): lax.ppermute(value, axis, [(i, (i + step) % count) for i in range(count)])  9.29 us
    ppermute x7, waiting for transfers between devices, shifted(): lax.ppermute(value, axis, [(i, (i + step) % count) for i in range(count)])  5.16 us
    pallas_call x1, Pallas kernels, on_device(): pl.pallas_call(own_kernel, in_specs=[smem()] + [vmem()] * 3, out_specs=[v...  2.33 us
    pallas_call x1, Pallas kernels, on_device(): pl.pallas_call(last_kernel, in_specs=[smem()] + [vmem()] * 16, out_specs=...  2.2 us
  transfers between devices with their start and end apart: 7, of which 4 were waited for; matrix products, arithmetic and copies ran while one was open for 3% of the time, Pallas kernels for 4%

profile of v3, /device:TPU:1, one launch (start us, length us, event | category | flops | bytes accessed | tf_op | source)
XLA Modules:
  0.0 76.8 jit_solution(17876186094271867127)
XLA Ops:
  0.6 0.0 copy-start.4
  0.6 0.8 %pad_maximum_fusion = bf16[2,128,128]{2,1,0:T(8,128)(2,1)S(1)} fusion(bf16[1,128,128]{2,1,0:T(8,128)(2,1)} %bitcast.17, bf16[1,128,128]{2,1,0:T(8,128)(2,1)} %bitcast.18), kind=kLoop, calls=%fused_computation | loop fusion | flops 32768 | bytes 131072 | tf_op jit(solution)/shard_map/stack | solution.py:359
  1.5 17.9 %all_to_all.15.same_ref = bf16[4,2,128,128]{3,2,1,0:T(8,128)(2,1)S(1)} all-to-all(bf16[4,2,128,128]{3,2,1,0:T(8,128)(2,1)S(1)} %broadcast_in_dim.10), channel_id=1, replica_groups=mesh['x'=4,'zh'=4,'zl'=2,'y'=4,'core'=2] {'zh'}, dimensions={0} | all-to-all | bytes 524288 | tf_op jit(solution)/shard_map/all_to_all | solution.py:360
  19.4 1.2 %collective-permute-start.2 = (bf16[4,2,128,128]{3,2,1,0:T(8,128)(2,1)S(1)}, bf16[4,2,128,128]{3,2,1,0:T(8,128)(2,1)S(1)}, u32[]{:S(2)}, u32[]{:S(2)}) collective-permute-start(bf16[4,2,128,128]{3,2,1,0:T(8,128)(2,1)S(1)} %all_to_all.15.same_ref), channel_id=1, source_target_pairs={{0,8},{8,0},{1,9},{9,1},{2,10},{10,2},{3,11},{11,3},{4,12},{12,4},... | collective-permute-start | bytes 786440 | tf_op jit(solution)/shard_map/ppermute | solution.py:345
  20.6 1.2 %collective-permute-start = (bf16[4,2,128,128]{3,2,1,0:T(8,128)(2,1)S(1)}, bf16[4,2,128,128]{3,2,1,0:T(8,128)(2,1)S(1)}, u32[]{:S(2)}, u32[]{:S(2)}) collective-permute-start(bf16[4,2,128,128]{3,2,1,0:T(8,128)(2,1)S(1)} %all_to_all.15.same_ref), channel_id=1, source_target_pairs={{0,64},{64,128},{128,192},{192,0},{1,65},{65,129},{129,193},{193,1... | collective-permute-start | bytes 786440 | tf_op jit(solution)/shard_map/ppermute | solution.py:345
  21.8 1.3 %reduce_max.9 = s32[]{:T(128)} reduce(s32[128]{0:T(128)} %param.9, s32[]{:T(128)} %constant.18.clone.1), dimensions={0}, to_apply=%region_0.0 | reduce | flops 127 | bytes 520 | tf_op jit(solution)/shard_map/reduce_max | solution.py:356
  23.1 1.5 %collective-permute-start.6 = (bf16[4,2,128,128]{3,2,1,0:T(8,128)(2,1)S(1)}, bf16[4,2,128,128]{3,2,1,0:T(8,128)(2,1)S(1)}, u32[]{:S(2)}, u32[]{:S(2)}) collective-permute-start(bf16[4,2,128,128]{3,2,1,0:T(8,128)(2,1)S(1)} %all_to_all.15.same_ref), channel_id=1, source_target_pairs={{0,192},{64,0},{128,64},{192,128},{1,193},{65,1},{129,65},{193,129... | collective-permute-start | bytes 786440 | tf_op jit(solution)/shard_map/ppermute | solution.py:345
  24.5 0.1 collective-permute-done.2.other_ref
  24.6 2.5 %collective-permute-start.3 = (bf16[4,2,128,128]{3,2,1,0:T(8,128)(2,1)S(1)}, bf16[4,2,128,128]{3,2,1,0:T(8,128)(2,1)S(1)}, u32[]{:S(2)}, u32[]{:S(2)}) collective-permute-start(bf16[4,2,128,128]{3,2,1,0:T(8,128)(2,1)S(1)} %collective-permute-done.2.other_ref), channel_id=1, source_target_pairs={{0,192},{64,0},{128,64},{192,128},{1,193},{65,1},{129,65},{193,129... | collective-permute-start | bytes 786440 | tf_op jit(solution)/shard_map/ppermute | solution.py:345
  27.1 0.0 collective-permute-start.5
  27.1 0.7 pad_add_fusion.place_ref
  27.8 0.0 copy-start.1
  27.8 0.7 copy-done.1
  28.5 0.2 pick.1
  28.6 0.0 collective-permute-done.left_same_ref
  28.7 0.3 collective-permute-start.1
  28.9 0.0 copy-done.4
  28.9 2.3 %own_slab.1 = (f32[1024,128]{1,0:T(8,128)S(1)}, f32[1024,128]{1,0:T(8,128)S(1)}, f32[1024,128]{1,0:T(8,128)S(1)}, f32[8,128]{1,0:T(8,128)S(1)}, bf16[1024,1024]{1,0:T(8,128)(2,1)S(1)}) custom-call(s32[3]{0:T(128)S(1)} %pad_add_fusion.place_ref, bf16[128,1024]{1,0:T(8,128)(2,1)S(1)} %copy-done.4, bf16[4,2,128,128]{3,2,1,0:T(8,128)(2,1)S(1)} %all_to_all.15.same_ref, ...), custom_call_target="tpu_custom_call" | custom-call | flops 2000000000 | bytes 1024 | tf_op jit(solution)/shard_map/own_slab/pallas_call | solution.py:383
  31.3 2.2 %collective-permute-done.3.right_other_ref = bf16[4,2,128,128]{3,2,1,0:T(8,128)(2,1)S(1)} collective-permute-done((bf16[4,2,128,128]{3,2,1,0:T(8,128)(2,1)S(1)}, bf16[4,2,128,128]{3,2,1,0:T(8,128)(2,1)S(1)}, u32[]{:S(2)}, u32[]{:S(2)}) %collective-permute-start.3) | collective-permute-done | bytes 262176 | tf_op jit(solution)/shard_map/ppermute | solution.py:345
  33.4 2.7 %collective-permute-start.4 = (bf16[4,2,128,128]{3,2,1,0:T(8,128)(2,1)S(1)}, bf16[4,2,128,128]{3,2,1,0:T(8,128)(2,1)S(1)}, u32[]{:S(2)}, u32[]{:S(2)}) collective-permute-start(bf16[4,2,128,128]{3,2,1,0:T(8,128)(2,1)S(1)} %collective-permute-done.3.right_other_ref), channel_id=1, source_target_pairs={{0,192},{64,0},{128,64},{192,128},{1,193},{65,1},{129,65},{193,129... | collective-permute-start | bytes 786440 | tf_op jit(solution)/shard_map/ppermute | solution.py:345
  36.1 0.0 collective-permute-done.6.right_same_ref
  36.1 0.0 collective-permute-done.5.left_other_ref
  36.1 0.0 copy-start.2
  36.1 0.0 copy-start.3
  36.1 0.7 next_slabs.1
  36.9 0.4 collective-permute-done.1.far_same_ref
  37.3 2.5 %collective-permute-done.4.far_other_ref = bf16[4,2,128,128]{3,2,1,0:T(8,128)(2,1)S(1)} collective-permute-done((bf16[4,2,128,128]{3,2,1,0:T(8,128)(2,1)S(1)}, bf16[4,2,128,128]{3,2,1,0:T(8,128)(2,1)S(1)}, u32[]{:S(2)}, u32[]{:S(2)}) %collective-permute-start.4) | collective-permute-done | bytes 262176 | tf_op jit(solution)/shard_map/ppermute | solution.py:345
  39.8 0.0 copy-done.2
  39.8 0.1 broadcast_in_dim.24.slots_ref
  39.9 0.0 copy-done.3
  39.9 0.0 copy-start
  39.9 2.2 %last_slab.1 = (bf16[128,1024]{1,0:T(8,128)(2,1)}, bf16[768,128]{1,0:T(8,128)(2,1)S(1)}) custom-call(s32[3]{0:T(128)S(1)} %pad_add_fusion.place_ref, bf16[128,1024]{1,0:T(8,128)(2,1)S(1)} %copy-done.4, bf16[4,2,128,128]{3,2,1,0:T(8,128)(2,1)S(1)} %collective-permute-done.1.far_same_ref, bf16[4,2,128,128]{3,2,1,0:T(8,128)(2,1)S(1)} %collective-permute-done.4.far_other_ref, ...), custom_call_target="tpu_custom_call" | custom-call | flops 4000000000 | bytes 1024 | tf_op jit(solution)/shard_map/last_slab/pallas_call | solution.py:401
  42.1 20.1 %all_to_all.16 = bf16[32,24,128]{2,1,0:T(8,128)(2,1)S(1)} all-to-all(bf16[32,24,128]{2,1,0:T(8,128)(2,1)S(1)} %bitcast.12), channel_id=1, replica_groups=mesh['x'=4,'zh'=4,'zl'=2,'y'=4,'core'=2] {'x','zh','zl'}, dimensions={0} | all-to-all | bytes 393216 | tf_op jit(solution)/shard_map/all_to_all | solution.py:416
  62.2 0.3 place_rows.1
  62.6 13.5 %all_to_all.17.pay_ref = f32[8,8,128]{2,1,0:T(8,128)S(1)} all-to-all(f32[8,8,128]{2,1,0:T(8,128)S(1)} %get-tuple-element.39), channel_id=1, replica_groups=mesh['x'=4,'zh'=4,'zl'=2,'y'=4,'core'=2] {'y','core'}, dimensions={0} | all-to-all | bytes 65536 | tf_op jit(solution)/shard_map/all_to_all | solution.py:427
  76.1 0.0 copy-done
  76.1 0.7 finish.1
  (1 shorter events, 0.0 us)
Async XLA Ops:
  0.6 28.3 %copy-start.4 = (bf16[128,1024]{1,0:T(8,128)(2,1)S(1)}, bf16[128,1024]{1,0:T(8,128)(2,1)}, u32[]{:S(2)}) copy-start(bf16[128,1024]{1,0:T(8,128)(2,1)} %q_ref.5) | copy-start | bytes 786436
  19.4 5.2 %collective-permute-start.2 = (bf16[4,2,128,128]{3,2,1,0:T(8,128)(2,1)S(1)}, bf16[4,2,128,128]{3,2,1,0:T(8,128)(2,1)S(1)}, u32[]{:S(2)}, u32[]{:S(2)}) collective-permute-start(bf16[4,2,128,128]{3,2,1,0:T(8,128)(2,1)S(1)} %all_to_all.15.same_ref), channel_id=1, source_target_pairs={{0,8},{8,0},{1,9},{9,1},{2,10},{10,2},{3,11},{11,3},{4,12},{12,4},... | collective-permute-start | bytes 786440 | tf_op jit(solution)/shard_map/ppermute | solution.py:345
  20.6 8.1 %collective-permute-start = (bf16[4,2,128,128]{3,2,1,0:T(8,128)(2,1)S(1)}, bf16[4,2,128,128]{3,2,1,0:T(8,128)(2,1)S(1)}, u32[]{:S(2)}, u32[]{:S(2)}) collective-permute-start(bf16[4,2,128,128]{3,2,1,0:T(8,128)(2,1)S(1)} %all_to_all.15.same_ref), channel_id=1, source_target_pairs={{0,64},{64,128},{128,192},{192,0},{1,65},{65,129},{129,193},{193,1... | collective-permute-start | bytes 786440 | tf_op jit(solution)/shard_map/ppermute | solution.py:345
  23.1 13.1 %collective-permute-start.6 = (bf16[4,2,128,128]{3,2,1,0:T(8,128)(2,1)S(1)}, bf16[4,2,128,128]{3,2,1,0:T(8,128)(2,1)S(1)}, u32[]{:S(2)}, u32[]{:S(2)}) collective-permute-start(bf16[4,2,128,128]{3,2,1,0:T(8,128)(2,1)S(1)} %all_to_all.15.same_ref), channel_id=1, source_target_pairs={{0,192},{64,0},{128,64},{192,128},{1,193},{65,1},{129,65},{193,129... | collective-permute-start | bytes 786440 | tf_op jit(solution)/shard_map/ppermute | solution.py:345
  24.6 8.8 %collective-permute-start.3 = (bf16[4,2,128,128]{3,2,1,0:T(8,128)(2,1)S(1)}, bf16[4,2,128,128]{3,2,1,0:T(8,128)(2,1)S(1)}, u32[]{:S(2)}, u32[]{:S(2)}) collective-permute-start(bf16[4,2,128,128]{3,2,1,0:T(8,128)(2,1)S(1)} %collective-permute-done.2.other_ref), channel_id=1, source_target_pairs={{0,192},{64,0},{128,64},{192,128},{1,193},{65,1},{129,65},{193,129... | collective-permute-start | bytes 786440 | tf_op jit(solution)/shard_map/ppermute | solution.py:345
  27.1 9.0 %collective-permute-start.5 = (bf16[4,2,128,128]{3,2,1,0:T(8,128)(2,1)S(1)}, bf16[4,2,128,128]{3,2,1,0:T(8,128)(2,1)S(1)}, u32[]{:S(2)}, u32[]{:S(2)}) collective-permute-start(bf16[4,2,128,128]{3,2,1,0:T(8,128)(2,1)S(1)} %collective-permute-done.2.other_ref), channel_id=1, source_target_pairs={{0,64},{64,128},{128,192},{192,0},{1,65},{65,129},{129,193},{193,1... | collective-permute-start | bytes 786440 | tf_op jit(solution)/shard_map/ppermute | solution.py:345
  27.8 0.7 copy-start.1
  28.7 8.6 %collective-permute-start.1 = (bf16[4,2,128,128]{3,2,1,0:T(8,128)(2,1)S(1)}, bf16[4,2,128,128]{3,2,1,0:T(8,128)(2,1)S(1)}, u32[]{:S(2)}, u32[]{:S(2)}) collective-permute-start(bf16[4,2,128,128]{3,2,1,0:T(8,128)(2,1)S(1)} %collective-permute-done.left_same_ref), channel_id=1, source_target_pairs={{0,64},{64,128},{128,192},{192,0},{1,65},{65,129},{129,193},{193,1... | collective-permute-start | bytes 786440 | tf_op jit(solution)/shard_map/ppermute | solution.py:345
  33.4 6.4 %collective-permute-start.4 = (bf16[4,2,128,128]{3,2,1,0:T(8,128)(2,1)S(1)}, bf16[4,2,128,128]{3,2,1,0:T(8,128)(2,1)S(1)}, u32[]{:S(2)}, u32[]{:S(2)}) collective-permute-start(bf16[4,2,128,128]{3,2,1,0:T(8,128)(2,1)S(1)} %collective-permute-done.3.right_other_ref), channel_id=1, source_target_pairs={{0,192},{64,0},{128,64},{192,128},{1,193},{65,1},{129,65},{193,129... | collective-permute-start | bytes 786440 | tf_op jit(solution)/shard_map/ppermute | solution.py:345
  36.1 3.7 %copy-start.2 = (s32[128]{0:T(128)S(1)}, s32[128]{0:T(128)}, u32[]{:S(2)}) copy-start(s32[128]{0:T(128)} %param.10) | copy-start | bytes 1540
  36.1 3.8 %copy-start.3 = (s32[128]{0:T(128)S(1)}, s32[128]{0:T(128)}, u32[]{:S(2)}) copy-start(s32[128]{0:T(128)} %param.9) | copy-start | bytes 1540
  39.9 36.2 %copy-start = (f32[1024]{0:T(1024)S(1)}, f32[1024]{0:T(1024)}, u32[]{:S(2)}) copy-start(f32[1024]{0:T(1024)} %param.11) | copy-start | bytes 12292

commit v4 on v3

v4 whole, which is shorter than its diff:
```python
import math

import jax
import jax.numpy as jnp
from jax import lax
from jax.experimental import pallas as pl
from jax.experimental.pallas import tpu as pltpu
from jax.sharding import Mesh, PartitionSpec as P

HD = 128
D = 8192
TOK = 128
GROUP = 8
ROWS = GROUP * TOK
NX = 4
NZ = 8
SHARDS = NX * NZ
KEEP = 32
SUB = 24
SEND = SHARDS * SUB
EIGHT = SHARDS * 8
TP = 8
PART = NZ * TOK // 2
FACTOR = math.log2(math.e) / math.sqrt(HD)
LOW = -1e30
NT = (((1,), (1,)), ((), ()))
TN = (((0,), (0,)), ((), ()))
VMEM_BYTES = 40 * 1024 * 1024


def vmem():
    return pl.BlockSpec(memory_space=pltpu.VMEM)


def params():
    return pltpu.CompilerParams(vmem_limit_bytes=VMEM_BYTES)


def wide(column):
    return jnp.broadcast_to(column, (column.shape[0], 128))


def tiled(array, count):
    return jnp.concatenate([array] * count, axis=1)


def position():
    return lax.axis_index("x"), lax.axis_index("zh") * 2 + lax.axis_index("zl")


def diagonal(rows=TOK):
    return lax.broadcasted_iota(jnp.int32, (rows, TOK), 0) == lax.broadcasted_iota(
        jnp.int32, (rows, TOK), 1
    )


def row_of(column, eye):
    return jnp.sum(jnp.where(eye, column, 0.0), axis=0, keepdims=True)


def rows_of(ref, eye):
    return jnp.concatenate(
        [row_of(ref[h * TOK : (h + 1) * TOK], eye) for h in range(GROUP)], axis=0
    )


def keys_of(*refs):
    return jnp.concatenate([ref[:, 0].reshape(-1, HD) for ref in refs], axis=0)


def values_of(*refs):
    value = jnp.concatenate([ref[:, 1].reshape(-1, HD) for ref in refs], axis=0)
    return jnp.concatenate([value, jnp.ones_like(value)], axis=1)


def shard_of(chunk, z):
    parity = z & 1
    return 2 * (chunk & 3) + jnp.where(chunk < 4, parity, 1 - parity)


def flash(query, key, value, old, weights_ref, rows, allowed=None):
    count = key.shape[0] // TOK
    scores = lax.dot_general(query, key, NT, preferred_element_type=jnp.float32)
    if allowed is not None:
        scores = jnp.where(allowed, scores, LOW)
    best = scores[:, 0:TOK]
    for i in range(1, count):
        best = jnp.maximum(best, scores[:, i * TOK : (i + 1) * TOK])
    top = wide(jnp.max(best, axis=1, keepdims=True))
    if old is not None:
        top = jnp.maximum(old[0], top)
    weights = jnp.exp2((scores - tiled(top, count)) * FACTOR).astype(jnp.bfloat16)
    weights_ref[rows] = weights
    both = jnp.dot(weights, value, preferred_element_type=jnp.float32)
    mixed, total = both[:, :HD], both[:, HD:]
    if old is not None:
        shrink = jnp.exp2((old[0] - top) * FACTOR)
        total = total + old[1] * shrink
        mixed = mixed + old[2] * shrink
    return top, total, mixed


def flash_heads(q_ref, pair, old_state, state, weights_ref, allowed=None):
    key = keys_of(*pair)
    value = values_of(*pair)
    for h in range(GROUP):
        rows = slice(h * TOK, (h + 1) * TOK)
        query = q_ref[:, h * HD : (h + 1) * HD]
        old = None if old_state is None else tuple(ref[rows] for ref in old_state)
        for ref, part in zip(state, flash(query, key, value, old, weights_ref, rows, allowed)):
            ref[rows] = part


def copy_state(old_state, state):
    for ref, old in zip(state, old_state):
        ref[...] = old[...]


def own_part(first, q_ref, keys_ref, old_state, state, level_ref, weights_ref):
    z = position()[1]
    token = lax.broadcasted_iota(jnp.int32, (TOK, PART), 0)
    lane = lax.broadcasted_iota(jnp.int32, (TOK, PART), 1)
    key = shard_of(first + (lane >> 7), z) * TOK + (lane & (TOK - 1))
    flash_heads(q_ref, (keys_ref,), old_state, state, weights_ref, key - token <= z * TOK)
    level_ref[...] = rows_of(state[0], diagonal())


def sides(q_ref, left_ref, right_ref, state, level_refs, weights_refs):
    x = position()[0]
    eye = diagonal()

    @pl.when(x > 0)
    def _():
        flash_heads(q_ref, (left_ref,), state, state, weights_refs[0])

    level_refs[0][...] = rows_of(state[0], eye)

    @pl.when(x == NX - 1)
    def _():
        flash_heads(q_ref, (right_ref,), state, state, weights_refs[1])

    level_refs[1][...] = rows_of(state[0], eye)


def first_kernel(q_ref, keys_ref, slot_row_ref, text_ref, *refs):
    state, (level_ref, weights_ref), picked, text_out_ref = refs[:3], refs[3:5], refs[5:8], refs[8]
    text_out_ref[...] = jnp.broadcast_to(text_ref[...].astype(jnp.float32), (8, TOK))
    own_part(0, q_ref, keys_ref, None, state, level_ref, weights_ref)
    pick(slot_row_ref, *picked)


def second_kernel(q_ref, keys_ref, left_ref, right_ref, *refs):
    old_state, state, levels, weights = refs[:3], refs[3:6], refs[6:9], refs[9:]
    own_part(NZ // 2, q_ref, keys_ref, old_state, state, levels[0], weights[0])
    sides(q_ref, left_ref, right_ref, state, levels[1:], weights[1:])


def third_kernel(q_ref, left_ref, right_ref, far_0_ref, far_1_ref, *refs):
    old_state, state, levels, weights = refs[:3], refs[3:6], refs[6:9], refs[9:]
    copy_state(old_state, state)
    sides(q_ref, left_ref, right_ref, state, levels, weights)

    @pl.when(position()[0] >= 2)
    def _():
        flash_heads(q_ref, (far_0_ref, far_1_ref), state, state, weights[2])

    levels[2][...] = rows_of(state[0], diagonal())


def pick(slot_row_ref, rows_ref, rest_ref, slots_ref):
    slot_row = slot_row_ref[...]
    slot_col = jnp.transpose(jnp.broadcast_to(slot_row, (TOK, TOK)))
    slots = jnp.where(slot_col >= 0, (slot_col & (KEEP - 1)) + 1, 0)
    slots_ref[...] = slots.astype(jnp.float32).astype(jnp.bfloat16)
    target_row = jnp.where(slot_row >= 0, slot_row >> 5, -1)
    target_col = jnp.where(slot_col >= 0, slot_col >> 5, -1)
    first = lax.broadcasted_iota(jnp.int32, (TOK, TOK), 0)
    second = lax.broadcasted_iota(jnp.int32, (TOK, TOK), 1)
    earlier = jnp.where((target_col == target_row) & (first < second), 1, 0)
    rank = jnp.sum(earlier, axis=0, keepdims=True)
    placed = jnp.where(target_row >= 0, target_row * 2 + rank, -1)[None]
    shape = (SHARDS, 8, TOK)
    to = lax.broadcasted_iota(jnp.int32, shape, 0)
    sub = lax.broadcasted_iota(jnp.int32, shape, 1)
    lane = lax.broadcasted_iota(jnp.int32, shape, 2)

    def one_hot(hit):
        return jnp.where(hit, 1.0, 0.0).reshape(EIGHT, TOK).astype(jnp.bfloat16)

    same = placed == to * 2 + (sub >> 2)
    for h in range(4):
        rows_ref[:, h * TOK : (h + 1) * TOK] = one_hot(same & ((sub & 3) == h))
    rest_ref[:, :TOK] = one_hot((placed == to * 2 + (sub - 2)) & ((sub == 2) | (sub == 3)))
    rest_ref[:, TOK:] = one_hot(lane == jnp.where(sub == 0, to, jnp.where(sub == 1, to + SHARDS, -1)))


def last_kernel(
    q_ref,
    far_2_ref,
    far_3_ref,
    text_ref,
    pick_rows_ref,
    pick_rest_ref,
    slots_ref,
    top_in,
    total_in,
    mixed_in,
    *refs,
):
    levels, weights = refs[:7], refs[7:14]
    context_ref, send_ref, top_ref, total_ref, mixed_ref, weights_last_ref, mass_ref = refs[14:]
    x, z = position()
    old_state = (top_in, total_in, mixed_in)
    state = (top_ref, total_ref, mixed_ref)
    mass_ref[...] = jnp.zeros_like(mass_ref)

    @pl.when(x >= 2)
    def _():
        flash_heads(q_ref, (far_2_ref, far_3_ref), old_state, state, weights_last_ref)

    @pl.when(x < 2)
    def _():
        copy_state(old_state, state)

    context = (mixed_ref[...] / total_ref[...]).astype(jnp.bfloat16)
    for h in range(GROUP):
        context_ref[:, h * HD : (h + 1) * HD] = context[h * TOK : (h + 1) * TOK]

    text = text_ref[...]

    @pl.when(jnp.max(text) > 0.0)
    def _():
        eye = diagonal()
        level = rows_of(top_ref, eye)
        part = text / rows_of(total_ref, eye)

        def mass_of(level_then, weights_ref, at, first=0):
            share = jnp.exp2((level_then - level) * FACTOR) * part
            share = jnp.concatenate([share[h : h + 1] for h in range(GROUP)], axis=1)
            high = share.astype(jnp.bfloat16).astype(jnp.float32)
            low = share - high
            both = jnp.concatenate(
                [jnp.broadcast_to(high, (8, ROWS)), jnp.broadcast_to(low, (8, ROWS))], axis=0
            ).astype(jnp.bfloat16)
            added = jnp.dot(both, weights_ref[...], preferred_element_type=jnp.float32)
            added = added[0:1] + added[8:9]
            shift = lax.rem(at, NX) * NZ
            for i in range(weights_ref.shape[1] // TOK):
                to = shift + shard_of(first + i, z)
                mass_ref[pl.ds(to, 1), :] = added[:, i * TOK : (i + 1) * TOK]

        own, own_other, left, right, left_other, right_other, far = [
            (level_ref[...], weights_ref) for level_ref, weights_ref in zip(levels, weights)
        ]
        mass_of(*own, x)
        mass_of(*own_other, x, NZ // 2)

        @pl.when(x > 0)
        def _():
            mass_of(*left, x + NX - 1)
            mass_of(*left_other, x + NX - 1, NZ // 2)

        @pl.when(x == NX - 1)
        def _():
            mass_of(*right, x + 1)
            mass_of(*right_other, x + 1, NZ // 2)

        @pl.when(x >= 2)
        def _():
            mass_of(*far, x + 2)
            mass_of(level, weights_last_ref, x + 2, NZ // 2)

    half = ROWS // 2
    sides = jnp.concatenate([context[:half], context[half:]], axis=1)
    sides = jnp.dot(pick_rows_ref[...], sides, preferred_element_type=jnp.float32)
    mass = mass_ref[...]
    high = mass.astype(jnp.bfloat16).astype(jnp.float32)
    low = mass - high
    rest = jnp.concatenate([high, low, jnp.zeros((TOK - 2 * SHARDS, HD), jnp.float32)], axis=0)
    rest = jnp.concatenate([slots_ref[...], rest.astype(jnp.bfloat16)], axis=0)
    rest = jnp.dot(pick_rest_ref[...], rest, preferred_element_type=jnp.float32)
    parts = [part.reshape(SHARDS, 8, HD) for part in (sides[:, :HD], sides[:, HD:], rest)]
    send = jnp.concatenate(parts, axis=1).reshape(SEND, HD)
    send_ref[...] = send.astype(jnp.bfloat16)


def place_kernel(got_ref, rows_ref, pay_ref):
    got = got_ref[...].astype(jnp.float32).reshape(SHARDS, SUB, HD)
    mass = jnp.sum(got[:, 16:17, :] + got[:, 17:18, :], axis=0)
    slots = jnp.concatenate(
        [
            jnp.broadcast_to(got[:, 18:19, :], (SHARDS, 4, HD)),
            jnp.broadcast_to(got[:, 19:20, :], (SHARDS, 4, HD)),
        ],
        axis=1,
    ).astype(jnp.int32)
    shape = (SHARDS, 8, HD)
    head = lax.broadcasted_iota(jnp.int32, shape, 1) & 3
    lane = lax.broadcasted_iota(jnp.int32, shape, 2)
    hit = (slots == (lane & (KEEP - 1)) + 1) & (head == lane >> 5)
    put = jnp.where(hit, 1.0, 0.0).reshape(EIGHT, HD).astype(jnp.bfloat16)
    sides = jnp.concatenate(
        [got[:, 0:8].reshape(EIGHT, HD), got[:, 8:16].reshape(EIGHT, HD)], axis=1
    ).astype(jnp.bfloat16)
    rows = lax.dot_general(put, sides, TN, preferred_element_type=jnp.float32)
    rows_ref[...] = rows
    squares = jnp.sum((rows * rows).reshape(4, KEEP, 2 * HD), axis=0)
    squares = jnp.sum(squares, axis=1, keepdims=True)
    squares = row_of(wide(squares), diagonal(KEEP))
    pay = jnp.concatenate([mass, squares, jnp.zeros((6, HD), jnp.float32)], axis=0)
    pay_ref[...] = jnp.broadcast_to(pay[None], (TP, 8, HD))


def finish_kernel(pay_ref, rows_ref, gain_ref, text_ref, mass_ref, kept_ref):
    pay = jnp.sum(pay_ref[...], axis=0)
    mass_ref[...] = pay[0:1] * (1.0 - text_ref[...].astype(jnp.float32))
    squares = jnp.where(diagonal(KEEP), jnp.broadcast_to(pay[1:2], (KEEP, HD)), 0.0)
    factor = lax.rsqrt(wide(jnp.sum(squares, axis=1, keepdims=True)) / D + 1e-06)
    for h in range(GROUP):
        columns = slice(h * HD, (h + 1) * HD)
        rows = slice((h & 3) * KEEP, ((h & 3) + 1) * KEEP)
        side = slice((h >> 2) * HD, ((h >> 2) + 1) * HD)
        kept_ref[:, columns] = (rows_ref[rows, side] * factor * gain_ref[:, columns]).astype(
            jnp.bfloat16
        )


def shape_of(shape, dtype):
    return jax.ShapeDtypeStruct(shape, dtype)


def shifted(value, axis, step, count):
    return lax.ppermute(value, axis, [(i, (i + step) % count) for i in range(count)])


def cost(flops):
    return pl.CostEstimate(flops=flops, bytes_accessed=2**10, transcendentals=0)


def on_device(queries, key_rows, value_rows, text_mask, kept_slot, norm_gain):
    f32, bf16 = jnp.float32, jnp.bfloat16
    both = jnp.stack([key_rows, value_rows])
    same = lax.all_to_all(
        jnp.broadcast_to(both[None], (NZ // 2, 2, TOK, HD)),
        "zh",
        split_axis=0,
        concat_axis=0,
        tiled=True,
    )
    other = shifted(same, "zl", 1, 2)
    state = [shape_of((ROWS, HD), f32)] * 3
    level = shape_of((GROUP, TOK), f32)
    weights = shape_of((ROWS, PART), bf16)

    def kernel(body, name, inputs, out_shape, scratch=()):
        return pl.pallas_call(
            body,
            in_specs=[vmem()] * len(inputs),
            out_specs=[vmem()] * len(out_shape),
            out_shape=out_shape,
            scratch_shapes=list(scratch),
            compiler_params=params(),
            cost_estimate=cost(10**9),
            name=name,
        )(*inputs)

    *now, level_own, weights_own, pick_rows, pick_rest, slots, text = kernel(
        first_kernel,
        "first",
        [queries, same, kept_slot[None], text_mask[None]],
        state
        + [level, weights]
        + [shape_of((EIGHT, 4 * TOK), bf16), shape_of((EIGHT, 2 * TOK), bf16)]
        + [shape_of((TOK, HD), bf16), shape_of((8, TOK), f32)],
    )
    other, now[0] = lax.optimization_barrier((other, now[0]))
    left = [shifted(part, "x", 1, NX) for part in (same, other)]
    right = [shifted(part, "x", -1, NX) for part in (same, other)]
    outs = kernel(
        second_kernel,
        "second",
        [queries, other, left[0], right[0], *now],
        state + [level] * 3 + [weights] * 3,
    )
    now, levels, kept = list(outs[:3]), [level_own, *outs[3:6]], [weights_own, *outs[6:]]
    left[1], right[1], now[0] = lax.optimization_barrier((left[1], right[1], now[0]))
    half = NZ // 4
    far = []
    for i in range(2):
        far.append(shifted(left[i][:half], "x", 1, NX))
        far.append(shifted(right[i][half:], "x", -1, NX))
    outs = kernel(
        third_kernel,
        "third",
        [queries, left[1], right[1], *far[:2], *now],
        state + [level] * 3 + [weights] * 3,
    )
    now, levels, kept = outs[:3], [*levels, *outs[3:6]], [*kept, *outs[6:]]
    context, send = kernel(
        last_kernel,
        "last",
        [queries, *far[2:], text, pick_rows, pick_rest, slots, *now, *levels, *kept],
        [shape_of((TOK, GROUP * HD), bf16), shape_of((SEND, HD), bf16)],
        [pltpu.VMEM((ROWS, HD), f32)] * 3
        + [pltpu.VMEM((ROWS, PART), bf16), pltpu.VMEM((SHARDS, HD), f32)],
    )
    got = lax.all_to_all(
        send.reshape(SHARDS, SUB, HD), ("x", "zh", "zl"), split_axis=0, concat_axis=0, tiled=True
    ).reshape(SEND, HD)
    rows, pay = pl.pallas_call(
        place_kernel,
        in_specs=[vmem()],
        out_specs=[vmem()] * 2,
        out_shape=[shape_of((4 * KEEP, 2 * HD), f32), shape_of((TP, 8, HD), f32)],
        compiler_params=params(),
        name="place_rows",
    )(got)
    pay = lax.all_to_all(pay, ("y", "core"), split_axis=0, concat_axis=0, tiled=True)
    mass, kept = pl.pallas_call(
        finish_kernel,
        in_specs=[vmem()] * 4,
        out_specs=[vmem()] * 2,
        out_shape=[shape_of((1, TOK), f32), shape_of((KEEP, GROUP * HD), bf16)],
        compiler_params=params(),
        name="finish",
    )(pay, rows, norm_gain[None], text_mask[None])
    return context, mass[0], kept


def solution(mesh):
    cut = Mesh(mesh.devices.reshape(NX, NZ // 2, 2, 4, 2), ("x", "zh", "zl", "y", "core"))
    seq, tp = ("x", "zh", "zl"), ("y", "core")
    placed = (P(seq, tp), P(seq, tp), P(seq, tp), P(seq), P(seq), P(tp))
    return jax.shard_map(
        on_device,
        mesh=cut,
        in_specs=placed,
        out_specs=(P(seq, tp), P(seq), P(seq, tp)),
        check_vma=False,
    )
```

time: 77 us -> 75 us (0.974)
  starting transfers between devices: 9.29 us -> 12.3 us
  other arithmetic: 2.84 us -> 0.78 us
  blocking collectives: 51.5 us -> 49.5 us
  Pallas kernels: 6.52 us -> 5.35 us
    all_to_all x1, blocking collectives: 20.1 us -> 16.9 us  [on_device(): lax.all_to_all(send.reshape(SHARDS, SUB, HD), ('x', 'zh', 'zl'), split_ax...]
    ppermute x7 -> x9, starting transfers between devices: 9.29 us -> 12.3 us  [shifted(): lax.ppermute(value, axis, [(i, (i + step) % count) for i in range(count)])]
    reduce_max x1 -> x0, other arithmetic: 1.29 us -> none  [on_device(): place = jnp.stack([x, z, jnp.max(text_mask)]).astype(jnp.int32)]
    pallas_call x4, Pallas kernels: 5.47 us -> 4.29 us  [kernel(): pl.pallas_call(body, in_specs=[vmem()] * len(inputs), out_specs=[vmem()]...]
    all_to_all x1, blocking collectives: 13.5 us -> 14.6 us  [on_device(): lax.all_to_all(pay, ('y', 'core'), split_axis=0, concat_axis=0, tiled=True)]
    ppermute x7 -> x9, waiting for transfers between devices: 5.16 us -> 5.32 us  [shifted(): lax.ppermute(value, axis, [(i, (i + step) % count) for i in range(count)])]
  transfers between devices with their start and end apart: 7 -> 9, of which waited for: 4 -> 4; matrix products, arithmetic and copies ran while one was open for 3% -> 0% of each run, Pallas kernels for 4% -> 4%
where the time goes in v4:
time: 75 us; the launch traced here: 74.7 us
  blocking collectives  49.5 us (66%)
  starting transfers between devices  12.3 us (16%)
  Pallas kernels  5.35 us (7%)
  waiting for transfers between devices  5.32 us (7%)
  other arithmetic  0.78 us (1%)
  local copies, waits for them, and re-layouts  0.75 us (1%)
    all_to_all x1, blocking collectives, on_device(): lax.all_to_all(jnp.broadcast_to(both[None], (NZ // 2, 2, TOK, HD)), 'zh',...  18 us
    all_to_all x1, blocking collectives, on_device(): lax.all_to_all(send.reshape(SHARDS, SUB, HD), ('x', 'zh', 'zl'), split_ax...  16.9 us
    all_to_all x1, blocking collectives, on_device(): lax.all_to_all(pay, ('y', 'core'), split_axis=0, concat_axis=0, tiled=True)  14.6 us
    ppermute x9, starting transfers between devices, shifted(): lax.ppermute(value, axis, [(i, (i + step) % count) for i in range(count)])  12.3 us
    ppermute x9, waiting for transfers between devices, shifted(): lax.ppermute(value, axis, [(i, (i + step) % count) for i in range(count)])  5.32 us
    pallas_call x4, Pallas kernels, kernel(): pl.pallas_call(body, in_specs=[vmem()] * len(inputs), out_specs=[vmem()]...  4.29 us
  transfers between devices with their start and end apart: 9, of which 4 were waited for; matrix products, arithmetic and copies ran while one was open for 0% of the time, Pallas kernels for 4%

profile of v4, /device:TPU:1, one launch (start us, length us, event | category | flops | bytes accessed | tf_op | source)
XLA Modules:
  0.0 74.7 jit_solution(16112628765457641368)
XLA Ops:
  0.6 0.8 %pad_maximum_fusion = bf16[2,128,128]{2,1,0:T(8,128)(2,1)S(1)} fusion(bf16[1,128,128]{2,1,0:T(8,128)(2,1)} %bitcast.14, bf16[1,128,128]{2,1,0:T(8,128)(2,1)} %bitcast.15), kind=kLoop, calls=%fused_computation | loop fusion | flops 32768 | bytes 131072 | tf_op jit(solution)/shard_map/stack | solution.py:342
  1.5 0.0 copy-start
  1.5 18.0 %all_to_all.15.keys_ref = bf16[4,2,128,128]{3,2,1,0:T(8,128)(2,1)S(1)} all-to-all(bf16[4,2,128,128]{3,2,1,0:T(8,128)(2,1)S(1)} %broadcast_in_dim.16), channel_id=1, replica_groups=mesh['x'=4,'zh'=4,'zl'=2,'y'=4,'core'=2] {'zh'}, dimensions={0} | all-to-all | bytes 524288 | tf_op jit(solution)/shard_map/all_to_all | solution.py:343
  19.5 1.2 %collective-permute-start = (bf16[4,2,128,128]{3,2,1,0:T(8,128)(2,1)S(1)}, bf16[4,2,128,128]{3,2,1,0:T(8,128)(2,1)S(1)}, u32[]{:S(2)}, u32[]{:S(2)}) collective-permute-start(bf16[4,2,128,128]{3,2,1,0:T(8,128)(2,1)S(1)} %all_to_all.15.keys_ref), channel_id=1, source_target_pairs={{0,8},{8,0},{1,9},{9,1},{2,10},{10,2},{3,11},{11,3},{4,12},{12,4},... | collective-permute-start | bytes 786440 | tf_op jit(solution)/shard_map/ppermute | solution.py:333
  20.6 1.2 %collective-permute-start.3 = (bf16[4,2,128,128]{3,2,1,0:T(8,128)(2,1)S(1)}, bf16[4,2,128,128]{3,2,1,0:T(8,128)(2,1)S(1)}, u32[]{:S(2)}, u32[]{:S(2)}) collective-permute-start(bf16[4,2,128,128]{3,2,1,0:T(8,128)(2,1)S(1)} %all_to_all.15.keys_ref), channel_id=1, source_target_pairs={{0,64},{64,128},{128,192},{192,0},{1,65},{65,129},{129,193},{193,1... | collective-permute-start | bytes 786440 | tf_op jit(solution)/shard_map/ppermute | solution.py:333
  21.9 1.5 %collective-permute-start.4 = (bf16[4,2,128,128]{3,2,1,0:T(8,128)(2,1)S(1)}, bf16[4,2,128,128]{3,2,1,0:T(8,128)(2,1)S(1)}, u32[]{:S(2)}, u32[]{:S(2)}) collective-permute-start(bf16[4,2,128,128]{3,2,1,0:T(8,128)(2,1)S(1)} %all_to_all.15.keys_ref), channel_id=1, source_target_pairs={{0,192},{64,0},{128,64},{192,128},{1,193},{65,1},{129,65},{193,129... | collective-permute-start | bytes 786440 | tf_op jit(solution)/shard_map/ppermute | solution.py:333
  23.3 0.0 copy-start.2
  23.3 0.0 copy-start.3
  23.3 0.0 copy-done
  23.3 0.6 copy-done.2
  24.0 0.0 copy-done.3
  24.0 1.1 %first.1 = (f32[1024,128]{1,0:T(8,128)S(1)}, f32[1024,128]{1,0:T(8,128)S(1)}, f32[1024,128]{1,0:T(8,128)S(1)}, f32[8,128]{1,0:T(8,128)S(1)}, bf16[1024,512]{1,0:...) custom-call(bf16[128,1024]{1,0:T(8,128)(2,1)S(1)} %copy-done, ...), custom_call_target="tpu_custom_call" | custom-call | flops 1000000000 | bytes 1024 | tf_op jit(solution)/shard_map/first/pallas_call | solution.py:356
  25.1 0.0 collective-permute-done.keys_ref
  25.1 0.8 %collective-permute-start.1 = (bf16[4,2,128,128]{3,2,1,0:T(8,128)(2,1)S(1)}, bf16[4,2,128,128]{3,2,1,0:T(8,128)(2,1)S(1)}, u32[]{:S(2)}, u32[]{:S(2)}) collective-permute-start(bf16[4,2,128,128]{3,2,1,0:T(8,128)(2,1)S(1)} %collective-permute-done.keys_ref), channel_id=1, source_target_pairs={{0,64},{64,128},{128,192},{192,0},{1,65},{65,129},{129,193},{193,1... | collective-permute-start | bytes 786440 | tf_op jit(solution)/shard_map/ppermute | solution.py:333
  25.9 2.0 %collective-permute-start.2 = (bf16[4,2,128,128]{3,2,1,0:T(8,128)(2,1)S(1)}, bf16[4,2,128,128]{3,2,1,0:T(8,128)(2,1)S(1)}, u32[]{:S(2)}, u32[]{:S(2)}) collective-permute-start(bf16[4,2,128,128]{3,2,1,0:T(8,128)(2,1)S(1)} %collective-permute-done.keys_ref), channel_id=1, source_target_pairs={{0,192},{64,0},{128,64},{192,128},{1,193},{65,1},{129,65},{193,129... | collective-permute-start | bytes 786440 | tf_op jit(solution)/shard_map/ppermute | solution.py:333
  27.9 0.0 collective-permute-done.3.left_ref
  27.9 0.1 collective-permute-start.7
  28.0 0.0 collective-permute-done.4.right_ref
  28.0 2.7 %collective-permute-start.8 = (bf16[2,2,128,128]{3,2,1,0:T(8,128)(2,1)S(1)}, bf16[2,2,128,128]{3,2,1,0:T(8,128)(2,1)S(1)}, u32[]{:S(2)}, u32[]{:S(2)}) collective-permute-start(bf16[2,2,128,128]{3,2,1,0:T(8,128)(2,1)S(1)} %slice.17), channel_id=1, source_target_pairs={{0,192},{64,0},{128,64},{192,128},{1,193},{65,1},{129,65},{193,129... | collective-permute-start | bytes 393224 | tf_op jit(solution)/shard_map/ppermute | solution.py:333
  30.7 1.3 %second.1 = (f32[1024,128]{1,0:T(8,128)S(1)}, f32[1024,128]{1,0:T(8,128)S(1)}, f32[1024,128]{1,0:T(8,128)S(1)}, f32[8,128]{1,0:T(8,128)S(1)}, f32[8,128]{1,0:T(8...) custom-call(bf16[128,1024]{1,0:T(8,128)(2,1)S(1)} %copy-done, ...), custom_call_target="tpu_custom_call" | custom-call | flops 1000000000 | bytes 1024 | tf_op jit(solution)/shard_map/second/pallas_call | solution.py:356
  32.0 1.6 %collective-permute-done.1.left_ref = bf16[4,2,128,128]{3,2,1,0:T(8,128)(2,1)S(1)} collective-permute-done((bf16[4,2,128,128]{3,2,1,0:T(8,128)(2,1)S(1)}, bf16[4,2,128,128]{3,2,1,0:T(8,128)(2,1)S(1)}, u32[]{:S(2)}, u32[]{:S(2)}) %collective-permute-start.1) | collective-permute-done | bytes 262176 | tf_op jit(solution)/shard_map/ppermute | solution.py:333
  33.5 0.3 collective-permute-done.2.right_ref
  33.8 1.3 %collective-permute-start.5 = (bf16[2,2,128,128]{3,2,1,0:T(8,128)(2,1)S(1)}, bf16[2,2,128,128]{3,2,1,0:T(8,128)(2,1)S(1)}, u32[]{:S(2)}, u32[]{:S(2)}) collective-permute-start(bf16[2,2,128,128]{3,2,1,0:T(8,128)(2,1)S(1)} %slice.12), channel_id=1, source_target_pairs={{0,64},{64,128},{128,192},{192,0},{1,65},{65,129},{129,193},{193,1... | collective-permute-start | bytes 393224 | tf_op jit(solution)/shard_map/ppermute | solution.py:333
  35.1 1.6 %collective-permute-start.6 = (bf16[2,2,128,128]{3,2,1,0:T(8,128)(2,1)S(1)}, bf16[2,2,128,128]{3,2,1,0:T(8,128)(2,1)S(1)}, u32[]{:S(2)}, u32[]{:S(2)}) collective-permute-start(bf16[2,2,128,128]{3,2,1,0:T(8,128)(2,1)S(1)} %slice.13), channel_id=1, source_target_pairs={{0,192},{64,0},{128,64},{192,128},{1,193},{65,1},{129,65},{193,129... | collective-permute-start | bytes 393224 | tf_op jit(solution)/shard_map/ppermute | solution.py:333
  36.7 0.0 collective-permute-done.7.far_0_ref
  36.7 0.0 collective-permute-done.8.far_1_ref
  36.7 0.4 third.1
  37.1 3.0 %collective-permute-done.5.far_2_ref = bf16[2,2,128,128]{3,2,1,0:T(8,128)(2,1)S(1)} collective-permute-done((bf16[2,2,128,128]{3,2,1,0:T(8,128)(2,1)S(1)}, bf16[2,2,128,128]{3,2,1,0:T(8,128)(2,1)S(1)}, u32[]{:S(2)}, u32[]{:S(2)}) %collective-permute-start.5) | collective-permute-done | bytes 131104 | tf_op jit(solution)/shard_map/ppermute | solution.py:333
  40.1 0.5 collective-permute-done.6.far_3_ref
  40.6 1.5 %last.1 = (bf16[128,1024]{1,0:T(8,128)(2,1)}, bf16[768,128]{1,0:T(8,128)(2,1)S(1)}) custom-call(bf16[128,1024]{1,0:T(8,128)(2,1)S(1)} %copy-done, bf16[2,2,128,128]{3,2,1,0:T(8,128)(2,1)S(1)} %collective-permute-done.5.far_2_ref, bf16[2,2,128,128]{3,2,1,0:T(8,128)(2,1)S(1)} %collective-permute-done.6.far_3_ref, f32[8,128]{1,0:T(8,128)S(1)} %get-tuple-element.49.text_ref, ...), custom_call_target="tpu_custom_call" | custom-call | flops 1000000000 | bytes 1024 | tf_op jit(solution)/shard_map/last/pallas_call | solution.py:356
  42.1 16.9 %all_to_all.16 = bf16[32,24,128]{2,1,0:T(8,128)(2,1)S(1)} all-to-all(bf16[32,24,128]{2,1,0:T(8,128)(2,1)S(1)} %bitcast.9), channel_id=1, replica_groups=mesh['x'=4,'zh'=4,'zl'=2,'y'=4,'core'=2] {'x','zh','zl'}, dimensions={0} | all-to-all | bytes 393216 | tf_op jit(solution)/shard_map/all_to_all | solution.py:407
  59.0 0.3 place_rows.1
  59.3 0.0 copy-start.1
  59.3 14.6 %all_to_all.17.pay_ref = f32[8,8,128]{2,1,0:T(8,128)S(1)} all-to-all(f32[8,8,128]{2,1,0:T(8,128)S(1)} %get-tuple-element.75), channel_id=1, replica_groups=mesh['x'=4,'zh'=4,'zl'=2,'y'=4,'core'=2] {'y','core'}, dimensions={0} | all-to-all | bytes 65536 | tf_op jit(solution)/shard_map/all_to_all | solution.py:418
  74.0 0.0 copy-done.1
  74.0 0.7 finish.1
  (5 shorter events, 0.1 us)
Async XLA Ops:
  1.5 21.9 %copy-start = (bf16[128,1024]{1,0:T(8,128)(2,1)S(1)}, bf16[128,1024]{1,0:T(8,128)(2,1)}, u32[]{:S(2)}) copy-start(bf16[128,1024]{1,0:T(8,128)(2,1)} %q_ref.7) | copy-start | bytes 786436
  19.5 5.6 %collective-permute-start = (bf16[4,2,128,128]{3,2,1,0:T(8,128)(2,1)S(1)}, bf16[4,2,128,128]{3,2,1,0:T(8,128)(2,1)S(1)}, u32[]{:S(2)}, u32[]{:S(2)}) collective-permute-start(bf16[4,2,128,128]{3,2,1,0:T(8,128)(2,1)S(1)} %all_to_all.15.keys_ref), channel_id=1, source_target_pairs={{0,8},{8,0},{1,9},{9,1},{2,10},{10,2},{3,11},{11,3},{4,12},{12,4},... | collective-permute-start | bytes 786440 | tf_op jit(solution)/shard_map/ppermute | solution.py:333
  20.6 7.2 %collective-permute-start.3 = (bf16[4,2,128,128]{3,2,1,0:T(8,128)(2,1)S(1)}, bf16[4,2,128,128]{3,2,1,0:T(8,128)(2,1)S(1)}, u32[]{:S(2)}, u32[]{:S(2)}) collective-permute-start(bf16[4,2,128,128]{3,2,1,0:T(8,128)(2,1)S(1)} %all_to_all.15.keys_ref), channel_id=1, source_target_pairs={{0,64},{64,128},{128,192},{192,0},{1,65},{65,129},{129,193},{193,1... | collective-permute-start | bytes 786440 | tf_op jit(solution)/shard_map/ppermute | solution.py:333
  21.9 6.1 %collective-permute-start.4 = (bf16[4,2,128,128]{3,2,1,0:T(8,128)(2,1)S(1)}, bf16[4,2,128,128]{3,2,1,0:T(8,128)(2,1)S(1)}, u32[]{:S(2)}, u32[]{:S(2)}) collective-permute-start(bf16[4,2,128,128]{3,2,1,0:T(8,128)(2,1)S(1)} %all_to_all.15.keys_ref), channel_id=1, source_target_pairs={{0,192},{64,0},{128,64},{192,128},{1,193},{65,1},{129,65},{193,129... | collective-permute-start | bytes 786440 | tf_op jit(solution)/shard_map/ppermute | solution.py:333
  23.3 0.7 copy-start.2
  23.3 0.7 copy-start.3
  25.1 8.4 %collective-permute-start.1 = (bf16[4,2,128,128]{3,2,1,0:T(8,128)(2,1)S(1)}, bf16[4,2,128,128]{3,2,1,0:T(8,128)(2,1)S(1)}, u32[]{:S(2)}, u32[]{:S(2)}) collective-permute-start(bf16[4,2,128,128]{3,2,1,0:T(8,128)(2,1)S(1)} %collective-permute-done.keys_ref), channel_id=1, source_target_pairs={{0,64},{64,128},{128,192},{192,0},{1,65},{65,129},{129,193},{193,1... | collective-permute-start | bytes 786440 | tf_op jit(solution)/shard_map/ppermute | solution.py:333
  25.9 7.9 %collective-permute-start.2 = (bf16[4,2,128,128]{3,2,1,0:T(8,128)(2,1)S(1)}, bf16[4,2,128,128]{3,2,1,0:T(8,128)(2,1)S(1)}, u32[]{:S(2)}, u32[]{:S(2)}) collective-permute-start(bf16[4,2,128,128]{3,2,1,0:T(8,128)(2,1)S(1)} %collective-permute-done.keys_ref), channel_id=1, source_target_pairs={{0,192},{64,0},{128,64},{192,128},{1,193},{65,1},{129,65},{193,129... | collective-permute-start | bytes 786440 | tf_op jit(solution)/shard_map/ppermute | solution.py:333
  27.9 8.8 %collective-permute-start.7 = (bf16[2,2,128,128]{3,2,1,0:T(8,128)(2,1)S(1)}, bf16[2,2,128,128]{3,2,1,0:T(8,128)(2,1)S(1)}, u32[]{:S(2)}, u32[]{:S(2)}) collective-permute-start(bf16[2,2,128,128]{3,2,1,0:T(8,128)(2,1)S(1)} %slice.16), channel_id=1, source_target_pairs={{0,64},{64,128},{128,192},{192,0},{1,65},{65,129},{129,193},{193,1... | collective-permute-start | bytes 393224 | tf_op jit(solution)/shard_map/ppermute | solution.py:333
  28.0 8.7 %collective-permute-start.8 = (bf16[2,2,128,128]{3,2,1,0:T(8,128)(2,1)S(1)}, bf16[2,2,128,128]{3,2,1,0:T(8,128)(2,1)S(1)}, u32[]{:S(2)}, u32[]{:S(2)}) collective-permute-start(bf16[2,2,128,128]{3,2,1,0:T(8,128)(2,1)S(1)} %slice.17), channel_id=1, source_target_pairs={{0,192},{64,0},{128,64},{192,128},{1,193},{65,1},{129,65},{193,129... | collective-permute-start | bytes 393224 | tf_op jit(solution)/shard_map/ppermute | solution.py:333
  33.8 6.3 %collective-permute-start.5 = (bf16[2,2,128,128]{3,2,1,0:T(8,128)(2,1)S(1)}, bf16[2,2,128,128]{3,2,1,0:T(8,128)(2,1)S(1)}, u32[]{:S(2)}, u32[]{:S(2)}) collective-permute-start(bf16[2,2,128,128]{3,2,1,0:T(8,128)(2,1)S(1)} %slice.12), channel_id=1, source_target_pairs={{0,64},{64,128},{128,192},{192,0},{1,65},{65,129},{129,193},{193,1... | collective-permute-start | bytes 393224 | tf_op jit(solution)/shard_map/ppermute | solution.py:333
  35.1 5.5 %collective-permute-start.6 = (bf16[2,2,128,128]{3,2,1,0:T(8,128)(2,1)S(1)}, bf16[2,2,128,128]{3,2,1,0:T(8,128)(2,1)S(1)}, u32[]{:S(2)}, u32[]{:S(2)}) collective-permute-start(bf16[2,2,128,128]{3,2,1,0:T(8,128)(2,1)S(1)} %slice.13), channel_id=1, source_target_pairs={{0,192},{64,0},{128,64},{192,128},{1,193},{65,1},{129,65},{193,129... | collective-permute-start | bytes 393224 | tf_op jit(solution)/shard_map/ppermute | solution.py:333
  59.3 14.7 %copy-start.1 = (f32[1024]{0:T(1024)S(1)}, f32[1024]{0:T(1024)}, u32[]{:S(2)}) copy-start(f32[1024]{0:T(1024)} %param.11) | copy-start | bytes 12292

commit v5 on v4

--- a/solution.py
+++ b/solution.py
@@ -20,7 +20,8 @@
 SEND = SHARDS * SUB
 EIGHT = SHARDS * 8
 TP = 8
-PART = NZ * TOK // 2
+NEAR = (0, -2, 2, 4)
+REST = (1, -1, 3, 5)
 FACTOR = math.log2(math.e) / math.sqrt(HD)
 LOW = -1e30
 NT = (((1,), (1,)), ((), ()))
@@ -73,9 +74,8 @@
     return jnp.concatenate([value, jnp.ones_like(value)], axis=1)
 
 
-def shard_of(chunk, z):
-    parity = z & 1
-    return 2 * (chunk & 3) + jnp.where(chunk < 4, parity, 1 - parity)
+def shard_of(z, offset):
+    return (z + offset) & (NZ - 1)
 
 
 def flash(query, key, value, old, weights_ref, rows, allowed=None):
@@ -116,12 +116,14 @@
         ref[...] = old[...]
 
 
-def own_part(first, q_ref, keys_ref, old_state, state, level_ref, weights_ref):
+def own_part(offsets, q_ref, keys_ref, old_state, state, level_ref, weights_ref):
     z = position()[1]
-    token = lax.broadcasted_iota(jnp.int32, (TOK, PART), 0)
-    lane = lax.broadcasted_iota(jnp.int32, (TOK, PART), 1)
-    key = shard_of(first + (lane >> 7), z) * TOK + (lane & (TOK - 1))
-    flash_heads(q_ref, (keys_ref,), old_state, state, weights_ref, key - token <= z * TOK)
+    token = lax.broadcasted_iota(jnp.int32, (TOK, TOK), 0)
+    lane = lax.broadcasted_iota(jnp.int32, (TOK, TOK), 1)
+    allowed = jnp.concatenate(
+        [lane - token <= (z - shard_of(z, offset)) * TOK for offset in offsets], axis=1
+    )
+    flash_heads(q_ref, (keys_ref,), old_state, state, weights_ref, allowed)
     level_ref[...] = rows_of(state[0], diagonal())
 
 
@@ -145,13 +147,13 @@
 def first_kernel(q_ref, keys_ref, slot_row_ref, text_ref, *refs):
     state, (level_ref, weights_ref), picked, text_out_ref = refs[:3], refs[3:5], refs[5:8], refs[8]
     text_out_ref[...] = jnp.broadcast_to(text_ref[...].astype(jnp.float32), (8, TOK))
-    own_part(0, q_ref, keys_ref, None, state, level_ref, weights_ref)
+    own_part(NEAR, q_ref, keys_ref, None, state, level_ref, weights_ref)
     pick(slot_row_ref, *picked)
 
 
 def second_kernel(q_ref, keys_ref, left_ref, right_ref, *refs):
     old_state, state, levels, weights = refs[:3], refs[3:6], refs[6:9], refs[9:]
-    own_part(NZ // 2, q_ref, keys_ref, old_state, state, levels[0], weights[0])
+    own_part(REST, q_ref, keys_ref, old_state, state, levels[0], weights[0])
     sides(q_ref, left_ref, right_ref, state, levels[1:], weights[1:])
 
 
@@ -234,7 +236,7 @@
         level = rows_of(top_ref, eye)
         part = text / rows_of(total_ref, eye)
 
-        def mass_of(level_then, weights_ref, at, first=0):
+        def mass_of(level_then, weights_ref, at, offsets=NEAR):
             share = jnp.exp2((level_then - level) * FACTOR) * part
             share = jnp.concatenate([share[h : h + 1] for h in range(GROUP)], axis=1)
             high = share.astype(jnp.bfloat16).astype(jnp.float32)
@@ -245,30 +247,30 @@
             added = jnp.dot(both, weights_ref[...], preferred_element_type=jnp.float32)
             added = added[0:1] + added[8:9]
             shift = lax.rem(at, NX) * NZ
-            for i in range(weights_ref.shape[1] // TOK):
-                to = shift + shard_of(first + i, z)
+            for i, offset in enumerate(offsets):
+                to = shift + shard_of(z, offset)
                 mass_ref[pl.ds(to, 1), :] = added[:, i * TOK : (i + 1) * TOK]
 
         own, own_other, left, right, left_other, right_other, far = [
             (level_ref[...], weights_ref) for level_ref, weights_ref in zip(levels, weights)
         ]
         mass_of(*own, x)
-        mass_of(*own_other, x, NZ // 2)
+        mass_of(*own_other, x, REST)
 
         @pl.when(x > 0)
         def _():
             mass_of(*left, x + NX - 1)
-            mass_of(*left_other, x + NX - 1, NZ // 2)
+            mass_of(*left_other, x + NX - 1, REST)
 
         @pl.when(x == NX - 1)
         def _():
             mass_of(*right, x + 1)
-            mass_of(*right_other, x + 1, NZ // 2)
+            mass_of(*right_other, x + 1, REST)
 
         @pl.when(x >= 2)
         def _():
             mass_of(*far, x + 2)
-            mass_of(level, weights_last_ref, x + 2, NZ // 2)
+            mass_of(level, weights_last_ref, x + 2, REST)
 
     half = ROWS // 2
     sides = jnp.concatenate([context[:half], context[half:]], axis=1)
@@ -340,17 +342,13 @@
 def on_device(queries, key_rows, value_rows, text_mask, kept_slot, norm_gain):
     f32, bf16 = jnp.float32, jnp.bfloat16
     both = jnp.stack([key_rows, value_rows])
-    same = lax.all_to_all(
-        jnp.broadcast_to(both[None], (NZ // 2, 2, TOK, HD)),
-        "zh",
-        split_axis=0,
-        concat_axis=0,
-        tiled=True,
-    )
-    other = shifted(same, "zl", 1, 2)
+    over_z = ("zh", "zl")
+    same = jnp.stack([both] + [shifted(both, over_z, step, NZ) for step in (2, -2, 4)])
+    other = shifted(same, over_z, -1, NZ)
     state = [shape_of((ROWS, HD), f32)] * 3
     level = shape_of((GROUP, TOK), f32)
-    weights = shape_of((ROWS, PART), bf16)
+    near_weights = shape_of((ROWS, len(NEAR) * TOK), bf16)
+    rest_weights = shape_of((ROWS, len(REST) * TOK), bf16)
 
     def kernel(body, name, inputs, out_shape, scratch=()):
         return pl.pallas_call(
@@ -369,7 +367,7 @@
         "first",
         [queries, same, kept_slot[None], text_mask[None]],
         state
-        + [level, weights]
+        + [level, near_weights]
         + [shape_of((EIGHT, 4 * TOK), bf16), shape_of((EIGHT, 2 * TOK), bf16)]
         + [shape_of((TOK, HD), bf16), shape_of((8, TOK), f32)],
     )
@@ -380,11 +378,11 @@
         second_kernel,
         "second",
         [queries, other, left[0], right[0], *now],
-        state + [level] * 3 + [weights] * 3,
+        state + [level] * 3 + [rest_weights, near_weights, near_weights],
     )
     now, levels, kept = list(outs[:3]), [level_own, *outs[3:6]], [weights_own, *outs[6:]]
     left[1], right[1], now[0] = lax.optimization_barrier((left[1], right[1], now[0]))
-    half = NZ // 4
+    half = 2
     far = []
     for i in range(2):
         far.append(shifted(left[i][:half], "x", 1, NX))
@@ -393,7 +391,7 @@
         third_kernel,
         "third",
         [queries, left[1], right[1], *far[:2], *now],
-        state + [level] * 3 + [weights] * 3,
+        state + [level] * 3 + [rest_weights, rest_weights, near_weights],
     )
     now, levels, kept = outs[:3], [*levels, *outs[3:6]], [*kept, *outs[6:]]
     context, send = kernel(
@@ -402,7 +400,7 @@
         [queries, *far[2:], text, pick_rows, pick_rest, slots, *now, *levels, *kept],
         [shape_of((TOK, GROUP * HD), bf16), shape_of((SEND, HD), bf16)],
         [pltpu.VMEM((ROWS, HD), f32)] * 3
-        + [pltpu.VMEM((ROWS, PART), bf16), pltpu.VMEM((SHARDS, HD), f32)],
+        + [pltpu.VMEM((ROWS, len(REST) * TOK), bf16), pltpu.VMEM((SHARDS, HD), f32)],
     )
     got = lax.all_to_all(
         send.reshape(SHARDS, SUB, HD), ("x", "zh", "zl"), split_axis=0, concat_axis=0, tiled=True

time: 75 us -> 73.2 us (0.976)
  blocking collectives: 49.5 us -> 32.7 us
  starting transfers between devices: 12.3 us -> 24.7 us
  waiting for transfers between devices: 5.32 us -> 8.16 us
    all_to_all x1 -> x0, blocking collectives: 18 us -> none  [on_device(): lax.all_to_all(jnp.broadcast_to(both[None], (NZ // 2, 2, TOK, HD)), 'zh',...]
    ppermute x9 -> x12, starting transfers between devices: 12.3 us -> 24.7 us  [shifted(): lax.ppermute(value, axis, [(i, (i + step) % count) for i in range(count)])]
    ppermute x9 -> x12, waiting for transfers between devices: 5.32 us -> 8.16 us  [shifted(): lax.ppermute(value, axis, [(i, (i + step) % count) for i in range(count)])]
  transfers between devices with their start and end apart: 9 -> 12, of which waited for: 4 -> 5; matrix products, arithmetic and copies ran while one was open for 0% -> 0% of each run, Pallas kernels for 4% -> 4%
where the time goes in v5:
time: 73.2 us; the launch traced here: 73 us
  blocking collectives  32.7 us (45%)
  starting transfers between devices  24.7 us (34%)
  waiting for transfers between devices  8.16 us (11%)
  Pallas kernels  5.17 us (7%)
  other arithmetic  0.82 us (1%)
    ppermute x12, starting transfers between devices, shifted(): lax.ppermute(value, axis, [(i, (i + step) % count) for i in range(count)])  24.7 us
    all_to_all x1, blocking collectives, on_device(): lax.all_to_all(send.reshape(SHARDS, SUB, HD), ('x', 'zh', 'zl'), split_ax...  17.6 us
    all_to_all x1, blocking collectives, on_device(): lax.all_to_all(pay, ('y', 'core'), split_axis=0, concat_axis=0, tiled=True)  15.1 us
    ppermute x12, waiting for transfers between devices, shifted(): lax.ppermute(value, axis, [(i, (i + step) % count) for i in range(count)])  8.16 us
    pallas_call x4, Pallas kernels, kernel(): pl.pallas_call(body, in_specs=[vmem()] * len(inputs), out_specs=[vmem()]...  4.11 us
  transfers between devices with their start and end apart: 12, of which 5 were waited for; matrix products, arithmetic and copies ran while one was open for 0% of the time, Pallas kernels for 4%

profile of v5, /device:TPU:1, one launch (start us, length us, event | category | flops | bytes accessed | tf_op | source)
XLA Modules:
  0.0 73.0 jit_solution(6244397050983702053)
XLA Ops:
  0.6 0.8 %fusion = (bf16[1,2,128,128]{3,2,1,0:T(8,128)(2,1)S(1)}, bf16[2,128,128]{2,1,0:T(8,128)(2,1)S(1)}) fusion(bf16[1,128,128]{2,1,0:T(8,128)(2,1)} %bitcast.22, bf16[1,128,128]{2,1,0:T(8,128)(2,1)} %bitcast.23), kind=kLoop, calls=%fused_computation.2 | loop fusion | flops 32768 | bytes 196608 | tf_op jit(solution)/shard_map/stack | solution.py:346
  1.4 3.9 %collective-permute-start = (bf16[2,128,128]{2,1,0:T(8,128)(2,1)S(1)}, bf16[2,128,128]{2,1,0:T(8,128)(2,1)S(1)}, u32[]{:S(2)}, u32[]{:S(2)}) collective-permute-start(bf16[2,128,128]{2,1,0:T(8,128)(2,1)S(1)} %get-tuple-element.80), channel_id=1, source_target_pairs={{0,16},{8,24},{16,32},{24,40},{32,48},{40,56},{48,0},{56,8},{1,17}... | collective-permute-start | bytes 196616 | tf_op jit(solution)/shard_map/ppermute | solution.py:335
  5.3 3.1 %collective-permute-start.1 = (bf16[2,128,128]{2,1,0:T(8,128)(2,1)S(1)}, bf16[2,128,128]{2,1,0:T(8,128)(2,1)S(1)}, u32[]{:S(2)}, u32[]{:S(2)}) collective-permute-start(bf16[2,128,128]{2,1,0:T(8,128)(2,1)S(1)} %get-tuple-element.80), channel_id=1, source_target_pairs={{0,48},{8,56},{16,0},{24,8},{32,16},{40,24},{48,32},{56,40},{1,49}... | collective-permute-start | bytes 196616 | tf_op jit(solution)/shard_map/ppermute | solution.py:335
  8.4 4.4 %collective-permute-start.2 = (bf16[2,128,128]{2,1,0:T(8,128)(2,1)S(1)}, bf16[2,128,128]{2,1,0:T(8,128)(2,1)S(1)}, u32[]{:S(2)}, u32[]{:S(2)}) collective-permute-start(bf16[2,128,128]{2,1,0:T(8,128)(2,1)S(1)} %get-tuple-element.80), channel_id=1, source_target_pairs={{0,32},{8,40},{16,48},{24,56},{32,0},{40,8},{48,16},{56,24},{1,33}... | collective-permute-start | bytes 196616 | tf_op jit(solution)/shard_map/ppermute | solution.py:335
  12.8 0.0 collective-permute-done
  12.8 0.0 collective-permute-done.1
  12.8 2.7 %collective-permute-done.2 = bf16[2,128,128]{2,1,0:T(8,128)(2,1)S(1)} collective-permute-done((bf16[2,128,128]{2,1,0:T(8,128)(2,1)S(1)}, bf16[2,128,128]{2,1,0:T(8,128)(2,1)S(1)}, u32[]{:S(2)}, u32[]{:S(2)}) %collective-permute-start.2) | collective-permute-done | bytes 65568 | tf_op jit(solution)/shard_map/ppermute | solution.py:335
  15.5 0.0 copy-start
  15.5 2.1 %collective-permute-start.3 = (bf16[4,2,128,128]{3,2,1,0:T(8,128)(2,1)S(1)}, bf16[4,2,128,128]{3,2,1,0:T(8,128)(2,1)S(1)}, u32[]{:S(2)}, u32[]{:S(2)}) collective-permute-start(bf16[4,2,128,128]{3,2,1,0:T(8,128)(2,1)S(1)} %pad_maximum_fusion.keys_ref), channel_id=1, source_target_pairs={{0,56},{8,0},{16,8},{24,16},{32,24},{40,32},{48,40},{56,48},{1,57}... | collective-permute-start | bytes 786440 | tf_op jit(solution)/shard_map/ppermute | solution.py:335
  17.7 1.2 %collective-permute-start.6 = (bf16[4,2,128,128]{3,2,1,0:T(8,128)(2,1)S(1)}, bf16[4,2,128,128]{3,2,1,0:T(8,128)(2,1)S(1)}, u32[]{:S(2)}, u32[]{:S(2)}) collective-permute-start(bf16[4,2,128,128]{3,2,1,0:T(8,128)(2,1)S(1)} %pad_maximum_fusion.keys_ref), channel_id=1, source_target_pairs={{0,64},{64,128},{128,192},{192,0},{1,65},{65,129},{129,193},{193,1... | collective-permute-start | bytes 786440 | tf_op jit(solution)/shard_map/ppermute | solution.py:335
  18.9 1.5 %collective-permute-start.7 = (bf16[4,2,128,128]{3,2,1,0:T(8,128)(2,1)S(1)}, bf16[4,2,128,128]{3,2,1,0:T(8,128)(2,1)S(1)}, u32[]{:S(2)}, u32[]{:S(2)}) collective-permute-start(bf16[4,2,128,128]{3,2,1,0:T(8,128)(2,1)S(1)} %pad_maximum_fusion.keys_ref), channel_id=1, source_target_pairs={{0,192},{64,0},{128,64},{192,128},{1,193},{65,1},{129,65},{193,129... | collective-permute-start | bytes 786440 | tf_op jit(solution)/shard_map/ppermute | solution.py:335
  20.4 0.0 copy-start.2
  20.4 0.0 copy-start.3
  20.4 0.0 copy-done
  20.4 0.6 copy-done.2
  21.0 0.0 copy-done.3
  21.0 1.1 %first.1 = (f32[1024,128]{1,0:T(8,128)S(1)}, f32[1024,128]{1,0:T(8,128)S(1)}, f32[1024,128]{1,0:T(8,128)S(1)}, f32[8,128]{1,0:T(8,128)S(1)}, bf16[1024,512]{1,0:...) custom-call(bf16[128,1024]{1,0:T(8,128)(2,1)S(1)} %copy-done, ...), custom_call_target="tpu_custom_call" | custom-call | flops 1000000000 | bytes 1024 | tf_op jit(solution)/shard_map/first/pallas_call | solution.py:354
  22.1 2.0 %collective-permute-done.3.keys_ref = bf16[4,2,128,128]{3,2,1,0:T(8,128)(2,1)S(1)} collective-permute-done((bf16[4,2,128,128]{3,2,1,0:T(8,128)(2,1)S(1)}, bf16[4,2,128,128]{3,2,1,0:T(8,128)(2,1)S(1)}, u32[]{:S(2)}, u32[]{:S(2)}) %collective-permute-start.3) | collective-permute-done | bytes 262176 | tf_op jit(solution)/shard_map/ppermute | solution.py:335
  24.1 1.2 %collective-permute-start.4 = (bf16[4,2,128,128]{3,2,1,0:T(8,128)(2,1)S(1)}, bf16[4,2,128,128]{3,2,1,0:T(8,128)(2,1)S(1)}, u32[]{:S(2)}, u32[]{:S(2)}) collective-permute-start(bf16[4,2,128,128]{3,2,1,0:T(8,128)(2,1)S(1)} %collective-permute-done.3.keys_ref), channel_id=1, source_target_pairs={{0,64},{64,128},{128,192},{192,0},{1,65},{65,129},{129,193},{193,1... | collective-permute-start | bytes 786440 | tf_op jit(solution)/shard_map/ppermute | solution.py:335
  25.3 1.5 %collective-permute-start.5 = (bf16[4,2,128,128]{3,2,1,0:T(8,128)(2,1)S(1)}, bf16[4,2,128,128]{3,2,1,0:T(8,128)(2,1)S(1)}, u32[]{:S(2)}, u32[]{:S(2)}) collective-permute-start(bf16[4,2,128,128]{3,2,1,0:T(8,128)(2,1)S(1)} %collective-permute-done.3.keys_ref), channel_id=1, source_target_pairs={{0,192},{64,0},{128,64},{192,128},{1,193},{65,1},{129,65},{193,129... | collective-permute-start | bytes 786440 | tf_op jit(solution)/shard_map/ppermute | solution.py:335
  26.8 0.0 collective-permute-done.6.left_ref
  26.8 0.1 collective-permute-start.10
  26.9 0.0 collective-permute-done.7.right_ref
  26.9 2.7 %collective-permute-start.11 = (bf16[2,2,128,128]{3,2,1,0:T(8,128)(2,1)S(1)}, bf16[2,2,128,128]{3,2,1,0:T(8,128)(2,1)S(1)}, u32[]{:S(2)}, u32[]{:S(2)}) collective-permute-start(bf16[2,2,128,128]{3,2,1,0:T(8,128)(2,1)S(1)} %slice.17), channel_id=1, source_target_pairs={{0,192},{64,0},{128,64},{192,128},{1,193},{65,1},{129,65},{193,129... | collective-permute-start | bytes 393224 | tf_op jit(solution)/shard_map/ppermute | solution.py:335
  29.6 1.3 %second.1 = (f32[1024,128]{1,0:T(8,128)S(1)}, f32[1024,128]{1,0:T(8,128)S(1)}, f32[1024,128]{1,0:T(8,128)S(1)}, f32[8,128]{1,0:T(8,128)S(1)}, f32[8,128]{1,0:T(8...) custom-call(bf16[128,1024]{1,0:T(8,128)(2,1)S(1)} %copy-done, ...), custom_call_target="tpu_custom_call" | custom-call | flops 1000000000 | bytes 1024 | tf_op jit(solution)/shard_map/second/pallas_call | solution.py:354
  30.9 0.1 collective-permute-done.4.left_ref
  31.0 0.0 collective-permute-done.5.right_ref
  31.0 1.3 %collective-permute-start.8 = (bf16[2,2,128,128]{3,2,1,0:T(8,128)(2,1)S(1)}, bf16[2,2,128,128]{3,2,1,0:T(8,128)(2,1)S(1)}, u32[]{:S(2)}, u32[]{:S(2)}) collective-permute-start(bf16[2,2,128,128]{3,2,1,0:T(8,128)(2,1)S(1)} %slice.12), channel_id=1, source_target_pairs={{0,64},{64,128},{128,192},{192,0},{1,65},{65,129},{129,193},{193,1... | collective-permute-start | bytes 393224 | tf_op jit(solution)/shard_map/ppermute | solution.py:335
  32.3 1.7 %collective-permute-start.9 = (bf16[2,2,128,128]{3,2,1,0:T(8,128)(2,1)S(1)}, bf16[2,2,128,128]{3,2,1,0:T(8,128)(2,1)S(1)}, u32[]{:S(2)}, u32[]{:S(2)}) collective-permute-start(bf16[2,2,128,128]{3,2,1,0:T(8,128)(2,1)S(1)} %slice.13), channel_id=1, source_target_pairs={{0,192},{64,0},{128,64},{192,128},{1,193},{65,1},{129,65},{193,129... | collective-permute-start | bytes 393224 | tf_op jit(solution)/shard_map/ppermute | solution.py:335
  34.0 0.0 collective-permute-done.10.far_0_ref
  34.0 0.0 collective-permute-done.11.far_1_ref
  34.0 0.3 third.1
  34.3 3.3 %collective-permute-done.8.far_2_ref = bf16[2,2,128,128]{3,2,1,0:T(8,128)(2,1)S(1)} collective-permute-done((bf16[2,2,128,128]{3,2,1,0:T(8,128)(2,1)S(1)}, bf16[2,2,128,128]{3,2,1,0:T(8,128)(2,1)S(1)}, u32[]{:S(2)}, u32[]{:S(2)}) %collective-permute-start.8) | collective-permute-done | bytes 131104 | tf_op jit(solution)/shard_map/ppermute | solution.py:335
  37.6 0.1 collective-permute-done.9.far_3_ref
  37.7 1.5 %last.1 = (bf16[128,1024]{1,0:T(8,128)(2,1)}, bf16[768,128]{1,0:T(8,128)(2,1)S(1)}) custom-call(bf16[128,1024]{1,0:T(8,128)(2,1)S(1)} %copy-done, bf16[2,2,128,128]{3,2,1,0:T(8,128)(2,1)S(1)} %collective-permute-done.8.far_2_ref, bf16[2,2,128,128]{3,2,1,0:T(8,128)(2,1)S(1)} %collective-permute-done.9.far_3_ref, f32[8,128]{1,0:T(8,128)S(1)} %get-tuple-element.49.text_ref, ...), custom_call_target="tpu_custom_call" | custom-call | flops 1000000000 | bytes 1024 | tf_op jit(solution)/shard_map/last/pallas_call | solution.py:354
  39.2 17.6 %all_to_all.10 = bf16[32,24,128]{2,1,0:T(8,128)(2,1)S(1)} all-to-all(bf16[32,24,128]{2,1,0:T(8,128)(2,1)S(1)} %bitcast.14), channel_id=1, replica_groups=mesh['x'=4,'zh'=4,'zl'=2,'y'=4,'core'=2] {'x','zh','zl'}, dimensions={0} | all-to-all | bytes 393216 | tf_op jit(solution)/shard_map/all_to_all | solution.py:405
  56.8 0.3 place_rows.1
  57.1 0.0 copy-start.1
  57.1 15.1 %all_to_all.11.pay_ref = f32[8,8,128]{2,1,0:T(8,128)S(1)} all-to-all(f32[8,8,128]{2,1,0:T(8,128)S(1)} %get-tuple-element.75), channel_id=1, replica_groups=mesh['x'=4,'zh'=4,'zl'=2,'y'=4,'core'=2] {'y','core'}, dimensions={0} | all-to-all | bytes 65536 | tf_op jit(solution)/shard_map/all_to_all | solution.py:416
  72.2 0.0 copy-done.1
  72.2 0.7 %finish.1 = (f32[1,128]{1,0:T(1,128)}, bf16[32,1024]{1,0:T(8,128)(2,1)}) custom-call(f32[8,8,128]{2,1,0:T(8,128)S(1)} %all_to_all.11.pay_ref, f32[128,256]{1,0:T(8,128)S(1)} %get-tuple-element.76.rows_ref, f32[1,1024]{1,0:T(1,128)S(1)} %bitcast.15, s32[1,128]{1,0:T(1,128)S(1)} %bitcast.17), custom_call_target="tpu_custom_call" | custom-call | tf_op jit(solution)/shard_map/finish/pallas_call | solution.py:417
  (5 shorter events, 0.1 us)
Async XLA Ops:
  1.4 11.4 %collective-permute-start = (bf16[2,128,128]{2,1,0:T(8,128)(2,1)S(1)}, bf16[2,128,128]{2,1,0:T(8,128)(2,1)S(1)}, u32[]{:S(2)}, u32[]{:S(2)}) collective-permute-start(bf16[2,128,128]{2,1,0:T(8,128)(2,1)S(1)} %get-tuple-element.80), channel_id=1, source_target_pairs={{0,16},{8,24},{16,32},{24,40},{32,48},{40,56},{48,0},{56,8},{1,17}... | collective-permute-start | bytes 196616 | tf_op jit(solution)/shard_map/ppermute | solution.py:335
  5.3 7.5 %collective-permute-start.1 = (bf16[2,128,128]{2,1,0:T(8,128)(2,1)S(1)}, bf16[2,128,128]{2,1,0:T(8,128)(2,1)S(1)}, u32[]{:S(2)}, u32[]{:S(2)}) collective-permute-start(bf16[2,128,128]{2,1,0:T(8,128)(2,1)S(1)} %get-tuple-element.80), channel_id=1, source_target_pairs={{0,48},{8,56},{16,0},{24,8},{32,16},{40,24},{48,32},{56,40},{1,49}... | collective-permute-start | bytes 196616 | tf_op jit(solution)/shard_map/ppermute | solution.py:335
  8.4 7.1 %collective-permute-start.2 = (bf16[2,128,128]{2,1,0:T(8,128)(2,1)S(1)}, bf16[2,128,128]{2,1,0:T(8,128)(2,1)S(1)}, u32[]{:S(2)}, u32[]{:S(2)}) collective-permute-start(bf16[2,128,128]{2,1,0:T(8,128)(2,1)S(1)} %get-tuple-element.80), channel_id=1, source_target_pairs={{0,32},{8,40},{16,48},{24,56},{32,0},{40,8},{48,16},{56,24},{1,33}... | collective-permute-start | bytes 196616 | tf_op jit(solution)/shard_map/ppermute | solution.py:335
  15.5 4.9 %copy-start = (bf16[128,1024]{1,0:T(8,128)(2,1)S(1)}, bf16[128,1024]{1,0:T(8,128)(2,1)}, u32[]{:S(2)}) copy-start(bf16[128,1024]{1,0:T(8,128)(2,1)} %q_ref.7) | copy-start | bytes 786436
  15.5 8.6 %collective-permute-start.3 = (bf16[4,2,128,128]{3,2,1,0:T(8,128)(2,1)S(1)}, bf16[4,2,128,128]{3,2,1,0:T(8,128)(2,1)S(1)}, u32[]{:S(2)}, u32[]{:S(2)}) collective-permute-start(bf16[4,2,128,128]{3,2,1,0:T(8,128)(2,1)S(1)} %pad_maximum_fusion.keys_ref), channel_id=1, source_target_pairs={{0,56},{8,0},{16,8},{24,16},{32,24},{40,32},{48,40},{56,48},{1,57}... | collective-permute-start | bytes 786440 | tf_op jit(solution)/shard_map/ppermute | solution.py:335
  17.7 9.1 %collective-permute-start.6 = (bf16[4,2,128,128]{3,2,1,0:T(8,128)(2,1)S(1)}, bf16[4,2,128,128]{3,2,1,0:T(8,128)(2,1)S(1)}, u32[]{:S(2)}, u32[]{:S(2)}) collective-permute-start(bf16[4,2,128,128]{3,2,1,0:T(8,128)(2,1)S(1)} %pad_maximum_fusion.keys_ref), channel_id=1, source_target_pairs={{0,64},{64,128},{128,192},{192,0},{1,65},{65,129},{129,193},{193,1... | collective-permute-start | bytes 786440 | tf_op jit(solution)/shard_map/ppermute | solution.py:335
  18.9 8.0 %collective-permute-start.7 = (bf16[4,2,128,128]{3,2,1,0:T(8,128)(2,1)S(1)}, bf16[4,2,128,128]{3,2,1,0:T(8,128)(2,1)S(1)}, u32[]{:S(2)}, u32[]{:S(2)}) collective-permute-start(bf16[4,2,128,128]{3,2,1,0:T(8,128)(2,1)S(1)} %pad_maximum_fusion.keys_ref), channel_id=1, source_target_pairs={{0,192},{64,0},{128,64},{192,128},{1,193},{65,1},{129,65},{193,129... | collective-permute-start | bytes 786440 | tf_op jit(solution)/shard_map/ppermute | solution.py:335
  20.4 0.7 copy-start.2
  20.4 0.7 copy-start.3
  24.1 6.9 %collective-permute-start.4 = (bf16[4,2,128,128]{3,2,1,0:T(8,128)(2,1)S(1)}, bf16[4,2,128,128]{3,2,1,0:T(8,128)(2,1)S(1)}, u32[]{:S(2)}, u32[]{:S(2)}) collective-permute-start(bf16[4,2,128,128]{3,2,1,0:T(8,128)(2,1)S(1)} %collective-permute-done.3.keys_ref), channel_id=1, source_target_pairs={{0,64},{64,128},{128,192},{192,0},{1,65},{65,129},{129,193},{193,1... | collective-permute-start | bytes 786440 | tf_op jit(solution)/shard_map/ppermute | solution.py:335
  25.3 5.7 %collective-permute-start.5 = (bf16[4,2,128,128]{3,2,1,0:T(8,128)(2,1)S(1)}, bf16[4,2,128,128]{3,2,1,0:T(8,128)(2,1)S(1)}, u32[]{:S(2)}, u32[]{:S(2)}) collective-permute-start(bf16[4,2,128,128]{3,2,1,0:T(8,128)(2,1)S(1)} %collective-permute-done.3.keys_ref), channel_id=1, source_target_pairs={{0,192},{64,0},{128,64},{192,128},{1,193},{65,1},{129,65},{193,129... | collective-permute-start | bytes 786440 | tf_op jit(solution)/shard_map/ppermute | solution.py:335
  26.8 7.3 %collective-permute-start.10 = (bf16[2,2,128,128]{3,2,1,0:T(8,128)(2,1)S(1)}, bf16[2,2,128,128]{3,2,1,0:T(8,128)(2,1)S(1)}, u32[]{:S(2)}, u32[]{:S(2)}) collective-permute-start(bf16[2,2,128,128]{3,2,1,0:T(8,128)(2,1)S(1)} %slice.16), channel_id=1, source_target_pairs={{0,64},{64,128},{128,192},{192,0},{1,65},{65,129},{129,193},{193,1... | collective-permute-start | bytes 393224 | tf_op jit(solution)/shard_map/ppermute | solution.py:335
  26.9 7.1 %collective-permute-start.11 = (bf16[2,2,128,128]{3,2,1,0:T(8,128)(2,1)S(1)}, bf16[2,2,128,128]{3,2,1,0:T(8,128)(2,1)S(1)}, u32[]{:S(2)}, u32[]{:S(2)}) collective-permute-start(bf16[2,2,128,128]{3,2,1,0:T(8,128)(2,1)S(1)} %slice.17), channel_id=1, source_target_pairs={{0,192},{64,0},{128,64},{192,128},{1,193},{65,1},{129,65},{193,129... | collective-permute-start | bytes 393224 | tf_op jit(solution)/shard_map/ppermute | solution.py:335
  31.0 6.6 %collective-permute-start.8 = (bf16[2,2,128,128]{3,2,1,0:T(8,128)(2,1)S(1)}, bf16[2,2,128,128]{3,2,1,0:T(8,128)(2,1)S(1)}, u32[]{:S(2)}, u32[]{:S(2)}) collective-permute-start(bf16[2,2,128,128]{3,2,1,0:T(8,128)(2,1)S(1)} %slice.12), channel_id=1, source_target_pairs={{0,64},{64,128},{128,192},{192,0},{1,65},{65,129},{129,193},{193,1... | collective-permute-start | bytes 393224 | tf_op jit(solution)/shard_map/ppermute | solution.py:335
  32.3 5.4 %collective-permute-start.9 = (bf16[2,2,128,128]{3,2,1,0:T(8,128)(2,1)S(1)}, bf16[2,2,128,128]{3,2,1,0:T(8,128)(2,1)S(1)}, u32[]{:S(2)}, u32[]{:S(2)}) collective-permute-start(bf16[2,2,128,128]{3,2,1,0:T(8,128)(2,1)S(1)} %slice.13), channel_id=1, source_target_pairs={{0,192},{64,0},{128,64},{192,128},{1,193},{65,1},{129,65},{193,129... | collective-permute-start | bytes 393224 | tf_op jit(solution)/shard_map/ppermute | solution.py:335
  57.1 15.1 %copy-start.1 = (f32[1024]{0:T(1024)S(1)}, f32[1024]{0:T(1024)}, u32[]{:S(2)}) copy-start(f32[1024]{0:T(1024)} %param.11) | copy-start | bytes 12292

commit v6 on v5

--- a/solution.py
+++ b/solution.py
@@ -20,8 +20,8 @@
 SEND = SHARDS * SUB
 EIGHT = SHARDS * 8
 TP = 8
-NEAR = (0, -2, 2, 4)
-REST = (1, -1, 3, 5)
+NEAR = (0, 4, -2, 2)
+REST = (1, 5, -1, 3)
 FACTOR = math.log2(math.e) / math.sqrt(HD)
 LOW = -1e30
 NT = (((1,), (1,)), ((), ()))
@@ -343,7 +343,7 @@
     f32, bf16 = jnp.float32, jnp.bfloat16
     both = jnp.stack([key_rows, value_rows])
     over_z = ("zh", "zl")
-    same = jnp.stack([both] + [shifted(both, over_z, step, NZ) for step in (2, -2, 4)])
+    same = jnp.stack([both] + [shifted(both, over_z, step, NZ) for step in (4, 2, -2)])
     other = shifted(same, over_z, -1, NZ)
     state = [shape_of((ROWS, HD), f32)] * 3
     level = shape_of((GROUP, TOK), f32)

time: 73.2 us -> 72.7 us (level)
  starting transfers between devices: 24.7 us -> 26 us
  waiting for transfers between devices: 8.16 us -> 6.88 us
    ppermute x12, starting transfers between devices: 24.7 us -> 26 us  [shifted(): lax.ppermute(value, axis, [(i, (i + step) % count) for i in range(count)])]
    ppermute x12, waiting for transfers between devices: 8.16 us -> 6.88 us  [shifted(): lax.ppermute(value, axis, [(i, (i + step) % count) for i in range(count)])]
  transfers between devices with their start and end apart: 12 -> 12, of which waited for: 5 -> 4; matrix products, arithmetic and copies ran while one was open for 0% -> 0% of each run, Pallas kernels for 4% -> 4%
where the time goes in v6:
time: 72.7 us; the launch traced here: 72.5 us
  blocking collectives  32.1 us (44%)
  starting transfers between devices  26 us (36%)
  waiting for transfers between devices  6.88 us (9%)
  Pallas kernels  5.17 us (7%)
  other arithmetic  0.82 us (1%)
  between operations  0.73 us (1%)
    ppermute x12, starting transfers between devices, shifted(): lax.ppermute(value, axis, [(i, (i + step) % count) for i in range(count)])  26 us
    all_to_all x1, blocking collectives, on_device(): lax.all_to_all(send.reshape(SHARDS, SUB, HD), ('x', 'zh', 'zl'), split_ax...  17.2 us
    all_to_all x1, blocking collectives, on_device(): lax.all_to_all(pay, ('y', 'core'), split_axis=0, concat_axis=0, tiled=True)  14.9 us
    ppermute x12, waiting for transfers between devices, shifted(): lax.ppermute(value, axis, [(i, (i + step) % count) for i in range(count)])  6.88 us
    pallas_call x4, Pallas kernels, kernel(): pl.pallas_call(body, in_specs=[vmem()] * len(inputs), out_specs=[vmem()]...  4.12 us
  transfers between devices with their start and end apart: 12, of which 4 were waited for; matrix products, arithmetic and copies ran while one was open for 0% of the time, Pallas kernels for 4%

profile of v6, /device:TPU:1, one launch (start us, length us, event | category | flops | bytes accessed | tf_op | source)
XLA Modules:
  0.0 72.5 jit_solution(4362362593261821896)
XLA Ops:
  0.6 0.8 %fusion = (bf16[1,2,128,128]{3,2,1,0:T(8,128)(2,1)S(1)}, bf16[2,128,128]{2,1,0:T(8,128)(2,1)S(1)}) fusion(bf16[1,128,128]{2,1,0:T(8,128)(2,1)} %bitcast.22, bf16[1,128,128]{2,1,0:T(8,128)(2,1)} %bitcast.23), kind=kLoop, calls=%fused_computation.2 | loop fusion | flops 32768 | bytes 196608 | tf_op jit(solution)/shard_map/stack | solution.py:346
  1.4 7.8 %collective-permute-start = (bf16[2,128,128]{2,1,0:T(8,128)(2,1)S(1)}, bf16[2,128,128]{2,1,0:T(8,128)(2,1)S(1)}, u32[]{:S(2)}, u32[]{:S(2)}) collective-permute-start(bf16[2,128,128]{2,1,0:T(8,128)(2,1)S(1)} %get-tuple-element.80), channel_id=1, source_target_pairs={{0,32},{8,40},{16,48},{24,56},{32,0},{40,8},{48,16},{56,24},{1,33}... | collective-permute-start | bytes 196616 | tf_op jit(solution)/shard_map/ppermute | solution.py:335
  9.2 1.2 %collective-permute-start.1 = (bf16[2,128,128]{2,1,0:T(8,128)(2,1)S(1)}, bf16[2,128,128]{2,1,0:T(8,128)(2,1)S(1)}, u32[]{:S(2)}, u32[]{:S(2)}) collective-permute-start(bf16[2,128,128]{2,1,0:T(8,128)(2,1)S(1)} %get-tuple-element.80), channel_id=1, source_target_pairs={{0,16},{8,24},{16,32},{24,40},{32,48},{40,56},{48,0},{56,8},{1,17}... | collective-permute-start | bytes 196616 | tf_op jit(solution)/shard_map/ppermute | solution.py:335
  10.4 2.4 %collective-permute-start.2 = (bf16[2,128,128]{2,1,0:T(8,128)(2,1)S(1)}, bf16[2,128,128]{2,1,0:T(8,128)(2,1)S(1)}, u32[]{:S(2)}, u32[]{:S(2)}) collective-permute-start(bf16[2,128,128]{2,1,0:T(8,128)(2,1)S(1)} %get-tuple-element.80), channel_id=1, source_target_pairs={{0,48},{8,56},{16,0},{24,8},{32,16},{40,24},{48,32},{56,40},{1,49}... | collective-permute-start | bytes 196616 | tf_op jit(solution)/shard_map/ppermute | solution.py:335
  12.8 0.0 collective-permute-done
  12.8 2.4 %collective-permute-done.1 = bf16[2,128,128]{2,1,0:T(8,128)(2,1)S(1)} collective-permute-done((bf16[2,128,128]{2,1,0:T(8,128)(2,1)S(1)}, bf16[2,128,128]{2,1,0:T(8,128)(2,1)S(1)}, u32[]{:S(2)}, u32[]{:S(2)}) %collective-permute-start.1) | collective-permute-done | bytes 65568 | tf_op jit(solution)/shard_map/ppermute | solution.py:335
  15.2 0.0 collective-permute-done.2
  15.3 0.0 copy-start
  15.3 3.3 %collective-permute-start.3 = (bf16[4,2,128,128]{3,2,1,0:T(8,128)(2,1)S(1)}, bf16[4,2,128,128]{3,2,1,0:T(8,128)(2,1)S(1)}, u32[]{:S(2)}, u32[]{:S(2)}) collective-permute-start(bf16[4,2,128,128]{3,2,1,0:T(8,128)(2,1)S(1)} %pad_maximum_fusion.keys_ref), channel_id=1, source_target_pairs={{0,56},{8,0},{16,8},{24,16},{32,24},{40,32},{48,40},{56,48},{1,57}... | collective-permute-start | bytes 786440 | tf_op jit(solution)/shard_map/ppermute | solution.py:335
  18.6 1.2 %collective-permute-start.6 = (bf16[4,2,128,128]{3,2,1,0:T(8,128)(2,1)S(1)}, bf16[4,2,128,128]{3,2,1,0:T(8,128)(2,1)S(1)}, u32[]{:S(2)}, u32[]{:S(2)}) collective-permute-start(bf16[4,2,128,128]{3,2,1,0:T(8,128)(2,1)S(1)} %pad_maximum_fusion.keys_ref), channel_id=1, source_target_pairs={{0,64},{64,128},{128,192},{192,0},{1,65},{65,129},{129,193},{193,1... | collective-permute-start | bytes 786440 | tf_op jit(solution)/shard_map/ppermute | solution.py:335
  19.8 1.5 %collective-permute-start.7 = (bf16[4,2,128,128]{3,2,1,0:T(8,128)(2,1)S(1)}, bf16[4,2,128,128]{3,2,1,0:T(8,128)(2,1)S(1)}, u32[]{:S(2)}, u32[]{:S(2)}) collective-permute-start(bf16[4,2,128,128]{3,2,1,0:T(8,128)(2,1)S(1)} %pad_maximum_fusion.keys_ref), channel_id=1, source_target_pairs={{0,192},{64,0},{128,64},{192,128},{1,193},{65,1},{129,65},{193,129... | collective-permute-start | bytes 786440 | tf_op jit(solution)/shard_map/ppermute | solution.py:335
  21.3 0.0 copy-start.2
  21.3 0.0 copy-start.3
  21.3 0.0 copy-done
  21.3 0.6 copy-done.2
  22.0 0.0 copy-done.3
  22.0 1.1 %first.1 = (f32[1024,128]{1,0:T(8,128)S(1)}, f32[1024,128]{1,0:T(8,128)S(1)}, f32[1024,128]{1,0:T(8,128)S(1)}, f32[8,128]{1,0:T(8,128)S(1)}, bf16[1024,512]{1,0:...) custom-call(bf16[128,1024]{1,0:T(8,128)(2,1)S(1)} %copy-done, ...), custom_call_target="tpu_custom_call" | custom-call | flops 1000000000 | bytes 1024 | tf_op jit(solution)/shard_map/first/pallas_call | solution.py:354
  23.1 0.0 collective-permute-done.3.keys_ref
  23.1 0.7 %collective-permute-start.4 = (bf16[4,2,128,128]{3,2,1,0:T(8,128)(2,1)S(1)}, bf16[4,2,128,128]{3,2,1,0:T(8,128)(2,1)S(1)}, u32[]{:S(2)}, u32[]{:S(2)}) collective-permute-start(bf16[4,2,128,128]{3,2,1,0:T(8,128)(2,1)S(1)} %collective-permute-done.3.keys_ref), channel_id=1, source_target_pairs={{0,64},{64,128},{128,192},{192,0},{1,65},{65,129},{129,193},{193,1... | collective-permute-start | bytes 786440 | tf_op jit(solution)/shard_map/ppermute | solution.py:335
  23.8 2.0 %collective-permute-start.5 = (bf16[4,2,128,128]{3,2,1,0:T(8,128)(2,1)S(1)}, bf16[4,2,128,128]{3,2,1,0:T(8,128)(2,1)S(1)}, u32[]{:S(2)}, u32[]{:S(2)}) collective-permute-start(bf16[4,2,128,128]{3,2,1,0:T(8,128)(2,1)S(1)} %collective-permute-done.3.keys_ref), channel_id=1, source_target_pairs={{0,192},{64,0},{128,64},{192,128},{1,193},{65,1},{129,65},{193,129... | collective-permute-start | bytes 786440 | tf_op jit(solution)/shard_map/ppermute | solution.py:335
  25.8 0.0 collective-permute-done.6.left_ref
  25.9 0.1 collective-permute-start.10
  25.9 0.0 collective-permute-done.7.right_ref
  26.0 2.7 %collective-permute-start.11 = (bf16[2,2,128,128]{3,2,1,0:T(8,128)(2,1)S(1)}, bf16[2,2,128,128]{3,2,1,0:T(8,128)(2,1)S(1)}, u32[]{:S(2)}, u32[]{:S(2)}) collective-permute-start(bf16[2,2,128,128]{3,2,1,0:T(8,128)(2,1)S(1)} %slice.17), channel_id=1, source_target_pairs={{0,192},{64,0},{128,64},{192,128},{1,193},{65,1},{129,65},{193,129... | collective-permute-start | bytes 393224 | tf_op jit(solution)/shard_map/ppermute | solution.py:335
  28.7 1.3 %second.1 = (f32[1024,128]{1,0:T(8,128)S(1)}, f32[1024,128]{1,0:T(8,128)S(1)}, f32[1024,128]{1,0:T(8,128)S(1)}, f32[8,128]{1,0:T(8,128)S(1)}, f32[8,128]{1,0:T(8...) custom-call(bf16[128,1024]{1,0:T(8,128)(2,1)S(1)} %copy-done, ...), custom_call_target="tpu_custom_call" | custom-call | flops 1000000000 | bytes 1024 | tf_op jit(solution)/shard_map/second/pallas_call | solution.py:354
  30.0 1.9 %collective-permute-done.4.left_ref = bf16[4,2,128,128]{3,2,1,0:T(8,128)(2,1)S(1)} collective-permute-done((bf16[4,2,128,128]{3,2,1,0:T(8,128)(2,1)S(1)}, bf16[4,2,128,128]{3,2,1,0:T(8,128)(2,1)S(1)}, u32[]{:S(2)}, u32[]{:S(2)}) %collective-permute-start.4) | collective-permute-done | bytes 262176 | tf_op jit(solution)/shard_map/ppermute | solution.py:335
  31.9 0.2 collective-permute-done.5.right_ref
  32.1 1.5 %collective-permute-start.8 = (bf16[2,2,128,128]{3,2,1,0:T(8,128)(2,1)S(1)}, bf16[2,2,128,128]{3,2,1,0:T(8,128)(2,1)S(1)}, u32[]{:S(2)}, u32[]{:S(2)}) collective-permute-start(bf16[2,2,128,128]{3,2,1,0:T(8,128)(2,1)S(1)} %slice.12), channel_id=1, source_target_pairs={{0,64},{64,128},{128,192},{192,0},{1,65},{65,129},{129,193},{193,1... | collective-permute-start | bytes 393224 | tf_op jit(solution)/shard_map/ppermute | solution.py:335
  33.6 1.5 %collective-permute-start.9 = (bf16[2,2,128,128]{3,2,1,0:T(8,128)(2,1)S(1)}, bf16[2,2,128,128]{3,2,1,0:T(8,128)(2,1)S(1)}, u32[]{:S(2)}, u32[]{:S(2)}) collective-permute-start(bf16[2,2,128,128]{3,2,1,0:T(8,128)(2,1)S(1)} %slice.13), channel_id=1, source_target_pairs={{0,192},{64,0},{128,64},{192,128},{1,193},{65,1},{129,65},{193,129... | collective-permute-start | bytes 393224 | tf_op jit(solution)/shard_map/ppermute | solution.py:335
  35.1 0.0 collective-permute-done.10.far_0_ref
  35.1 0.0 collective-permute-done.11.far_1_ref
  35.1 0.3 third.1
  35.4 2.3 %collective-permute-done.8.far_2_ref = bf16[2,2,128,128]{3,2,1,0:T(8,128)(2,1)S(1)} collective-permute-done((bf16[2,2,128,128]{3,2,1,0:T(8,128)(2,1)S(1)}, bf16[2,2,128,128]{3,2,1,0:T(8,128)(2,1)S(1)}, u32[]{:S(2)}, u32[]{:S(2)}) %collective-permute-start.8) | collective-permute-done | bytes 131104 | tf_op jit(solution)/shard_map/ppermute | solution.py:335
  37.7 0.0 collective-permute-done.9.far_3_ref
  37.7 1.5 %last.1 = (bf16[128,1024]{1,0:T(8,128)(2,1)}, bf16[768,128]{1,0:T(8,128)(2,1)S(1)}) custom-call(bf16[128,1024]{1,0:T(8,128)(2,1)S(1)} %copy-done, bf16[2,2,128,128]{3,2,1,0:T(8,128)(2,1)S(1)} %collective-permute-done.8.far_2_ref, bf16[2,2,128,128]{3,2,1,0:T(8,128)(2,1)S(1)} %collective-permute-done.9.far_3_ref, f32[8,128]{1,0:T(8,128)S(1)} %get-tuple-element.49.text_ref, ...), custom_call_target="tpu_custom_call" | custom-call | flops 1000000000 | bytes 1024 | tf_op jit(solution)/shard_map/last/pallas_call | solution.py:354
  39.2 17.2 %all_to_all.10 = bf16[32,24,128]{2,1,0:T(8,128)(2,1)S(1)} all-to-all(bf16[32,24,128]{2,1,0:T(8,128)(2,1)S(1)} %bitcast.14), channel_id=1, replica_groups=mesh['x'=4,'zh'=4,'zl'=2,'y'=4,'core'=2] {'x','zh','zl'}, dimensions={0} | all-to-all | bytes 393216 | tf_op jit(solution)/shard_map/all_to_all | solution.py:405
  56.4 0.3 place_rows.1
  56.8 0.0 copy-start.1
  56.8 14.9 %all_to_all.11.pay_ref = f32[8,8,128]{2,1,0:T(8,128)S(1)} all-to-all(f32[8,8,128]{2,1,0:T(8,128)S(1)} %get-tuple-element.75), channel_id=1, replica_groups=mesh['x'=4,'zh'=4,'zl'=2,'y'=4,'core'=2] {'y','core'}, dimensions={0} | all-to-all | bytes 65536 | tf_op jit(solution)/shard_map/all_to_all | solution.py:416
  71.7 0.0 copy-done.1
  71.7 0.7 %finish.1 = (f32[1,128]{1,0:T(1,128)}, bf16[32,1024]{1,0:T(8,128)(2,1)}) custom-call(f32[8,8,128]{2,1,0:T(8,128)S(1)} %all_to_all.11.pay_ref, f32[128,256]{1,0:T(8,128)S(1)} %get-tuple-element.76.rows_ref, f32[1,1024]{1,0:T(1,128)S(1)} %bitcast.15, s32[1,128]{1,0:T(1,128)S(1)} %bitcast.17), custom_call_target="tpu_custom_call" | custom-call | tf_op jit(solution)/shard_map/finish/pallas_call | solution.py:417
  (5 shorter events, 0.1 us)
Async XLA Ops:
  1.4 11.4 %collective-permute-start = (bf16[2,128,128]{2,1,0:T(8,128)(2,1)S(1)}, bf16[2,128,128]{2,1,0:T(8,128)(2,1)S(1)}, u32[]{:S(2)}, u32[]{:S(2)}) collective-permute-start(bf16[2,128,128]{2,1,0:T(8,128)(2,1)S(1)} %get-tuple-element.80), channel_id=1, source_target_pairs={{0,32},{8,40},{16,48},{24,56},{32,0},{40,8},{48,16},{56,24},{1,33}... | collective-permute-start | bytes 196616 | tf_op jit(solution)/shard_map/ppermute | solution.py:335
  9.2 6.0 %collective-permute-start.1 = (bf16[2,128,128]{2,1,0:T(8,128)(2,1)S(1)}, bf16[2,128,128]{2,1,0:T(8,128)(2,1)S(1)}, u32[]{:S(2)}, u32[]{:S(2)}) collective-permute-start(bf16[2,128,128]{2,1,0:T(8,128)(2,1)S(1)} %get-tuple-element.80), channel_id=1, source_target_pairs={{0,16},{8,24},{16,32},{24,40},{32,48},{40,56},{48,0},{56,8},{1,17}... | collective-permute-start | bytes 196616 | tf_op jit(solution)/shard_map/ppermute | solution.py:335
  10.4 4.8 %collective-permute-start.2 = (bf16[2,128,128]{2,1,0:T(8,128)(2,1)S(1)}, bf16[2,128,128]{2,1,0:T(8,128)(2,1)S(1)}, u32[]{:S(2)}, u32[]{:S(2)}) collective-permute-start(bf16[2,128,128]{2,1,0:T(8,128)(2,1)S(1)} %get-tuple-element.80), channel_id=1, source_target_pairs={{0,48},{8,56},{16,0},{24,8},{32,16},{40,24},{48,32},{56,40},{1,49}... | collective-permute-start | bytes 196616 | tf_op jit(solution)/shard_map/ppermute | solution.py:335
  15.3 6.1 %copy-start = (bf16[128,1024]{1,0:T(8,128)(2,1)S(1)}, bf16[128,1024]{1,0:T(8,128)(2,1)}, u32[]{:S(2)}) copy-start(bf16[128,1024]{1,0:T(8,128)(2,1)} %q_ref.7) | copy-start | bytes 786436
  15.3 7.8 %collective-permute-start.3 = (bf16[4,2,128,128]{3,2,1,0:T(8,128)(2,1)S(1)}, bf16[4,2,128,128]{3,2,1,0:T(8,128)(2,1)S(1)}, u32[]{:S(2)}, u32[]{:S(2)}) collective-permute-start(bf16[4,2,128,128]{3,2,1,0:T(8,128)(2,1)S(1)} %pad_maximum_fusion.keys_ref), channel_id=1, source_target_pairs={{0,56},{8,0},{16,8},{24,16},{32,24},{40,32},{48,40},{56,48},{1,57}... | collective-permute-start | bytes 786440 | tf_op jit(solution)/shard_map/ppermute | solution.py:335
  18.6 7.2 %collective-permute-start.6 = (bf16[4,2,128,128]{3,2,1,0:T(8,128)(2,1)S(1)}, bf16[4,2,128,128]{3,2,1,0:T(8,128)(2,1)S(1)}, u32[]{:S(2)}, u32[]{:S(2)}) collective-permute-start(bf16[4,2,128,128]{3,2,1,0:T(8,128)(2,1)S(1)} %pad_maximum_fusion.keys_ref), channel_id=1, source_target_pairs={{0,64},{64,128},{128,192},{192,0},{1,65},{65,129},{129,193},{193,1... | collective-permute-start | bytes 786440 | tf_op jit(solution)/shard_map/ppermute | solution.py:335
  19.8 6.1 %collective-permute-start.7 = (bf16[4,2,128,128]{3,2,1,0:T(8,128)(2,1)S(1)}, bf16[4,2,128,128]{3,2,1,0:T(8,128)(2,1)S(1)}, u32[]{:S(2)}, u32[]{:S(2)}) collective-permute-start(bf16[4,2,128,128]{3,2,1,0:T(8,128)(2,1)S(1)} %pad_maximum_fusion.keys_ref), channel_id=1, source_target_pairs={{0,192},{64,0},{128,64},{192,128},{1,193},{65,1},{129,65},{193,129... | collective-permute-start | bytes 786440 | tf_op jit(solution)/shard_map/ppermute | solution.py:335
  21.3 0.7 copy-start.2
  21.3 0.7 copy-start.3
  23.1 8.8 %collective-permute-start.4 = (bf16[4,2,128,128]{3,2,1,0:T(8,128)(2,1)S(1)}, bf16[4,2,128,128]{3,2,1,0:T(8,128)(2,1)S(1)}, u32[]{:S(2)}, u32[]{:S(2)}) collective-permute-start(bf16[4,2,128,128]{3,2,1,0:T(8,128)(2,1)S(1)} %collective-permute-done.3.keys_ref), channel_id=1, source_target_pairs={{0,64},{64,128},{128,192},{192,0},{1,65},{65,129},{129,193},{193,1... | collective-permute-start | bytes 786440 | tf_op jit(solution)/shard_map/ppermute | solution.py:335
  23.8 8.3 %collective-permute-start.5 = (bf16[4,2,128,128]{3,2,1,0:T(8,128)(2,1)S(1)}, bf16[4,2,128,128]{3,2,1,0:T(8,128)(2,1)S(1)}, u32[]{:S(2)}, u32[]{:S(2)}) collective-permute-start(bf16[4,2,128,128]{3,2,1,0:T(8,128)(2,1)S(1)} %collective-permute-done.3.keys_ref), channel_id=1, source_target_pairs={{0,192},{64,0},{128,64},{192,128},{1,193},{65,1},{129,65},{193,129... | collective-permute-start | bytes 786440 | tf_op jit(solution)/shard_map/ppermute | solution.py:335
  25.9 9.3 %collective-permute-start.10 = (bf16[2,2,128,128]{3,2,1,0:T(8,128)(2,1)S(1)}, bf16[2,2,128,128]{3,2,1,0:T(8,128)(2,1)S(1)}, u32[]{:S(2)}, u32[]{:S(2)}) collective-permute-start(bf16[2,2,128,128]{3,2,1,0:T(8,128)(2,1)S(1)} %slice.16), channel_id=1, source_target_pairs={{0,64},{64,128},{128,192},{192,0},{1,65},{65,129},{129,193},{193,1... | collective-permute-start | bytes 393224 | tf_op jit(solution)/shard_map/ppermute | solution.py:335
  26.0 9.1 %collective-permute-start.11 = (bf16[2,2,128,128]{3,2,1,0:T(8,128)(2,1)S(1)}, bf16[2,2,128,128]{3,2,1,0:T(8,128)(2,1)S(1)}, u32[]{:S(2)}, u32[]{:S(2)}) collective-permute-start(bf16[2,2,128,128]{3,2,1,0:T(8,128)(2,1)S(1)} %slice.17), channel_id=1, source_target_pairs={{0,192},{64,0},{128,64},{192,128},{1,193},{65,1},{129,65},{193,129... | collective-permute-start | bytes 393224 | tf_op jit(solution)/shard_map/ppermute | solution.py:335
  32.1 5.6 %collective-permute-start.8 = (bf16[2,2,128,128]{3,2,1,0:T(8,128)(2,1)S(1)}, bf16[2,2,128,128]{3,2,1,0:T(8,128)(2,1)S(1)}, u32[]{:S(2)}, u32[]{:S(2)}) collective-permute-start(bf16[2,2,128,128]{3,2,1,0:T(8,128)(2,1)S(1)} %slice.12), channel_id=1, source_target_pairs={{0,64},{64,128},{128,192},{192,0},{1,65},{65,129},{129,193},{193,1... | collective-permute-start | bytes 393224 | tf_op jit(solution)/shard_map/ppermute | solution.py:335
  33.6 4.1 %collective-permute-start.9 = (bf16[2,2,128,128]{3,2,1,0:T(8,128)(2,1)S(1)}, bf16[2,2,128,128]{3,2,1,0:T(8,128)(2,1)S(1)}, u32[]{:S(2)}, u32[]{:S(2)}) collective-permute-start(bf16[2,2,128,128]{3,2,1,0:T(8,128)(2,1)S(1)} %slice.13), channel_id=1, source_target_pairs={{0,192},{64,0},{128,64},{192,128},{1,193},{65,1},{129,65},{193,129... | collective-permute-start | bytes 393224 | tf_op jit(solution)/shard_map/ppermute | solution.py:335
  56.8 15.0 %copy-start.1 = (f32[1024]{0:T(1024)S(1)}, f32[1024]{0:T(1024)}, u32[]{:S(2)}) copy-start(f32[1024]{0:T(1024)} %param.11) | copy-start | bytes 12292

commit v7 on v6

--- a/solution.py
+++ b/solution.py
@@ -24,6 +24,10 @@
 REST = (1, 5, -1, 3)
 FACTOR = math.log2(math.e) / math.sqrt(HD)
 LOW = -1e30
+TO_RIGHT = [(0, 1), (1, 2), (2, 3)]
+TO_LEFT = [(0, 3), (1, 0)]
+FAR_RIGHT = [(1, 2), (2, 3)]
+FAR_LEFT = [(0, 3), (3, 2)]
 NT = (((1,), (1,)), ((), ()))
 TN = (((0,), (0,)), ((), ()))
 VMEM_BYTES = 40 * 1024 * 1024
@@ -372,8 +376,8 @@
         + [shape_of((TOK, HD), bf16), shape_of((8, TOK), f32)],
     )
     other, now[0] = lax.optimization_barrier((other, now[0]))
-    left = [shifted(part, "x", 1, NX) for part in (same, other)]
-    right = [shifted(part, "x", -1, NX) for part in (same, other)]
+    left = [lax.ppermute(part, "x", TO_RIGHT) for part in (same, other)]
+    right = [lax.ppermute(part, "x", TO_LEFT) for part in (same, other)]
     outs = kernel(
         second_kernel,
         "second",
@@ -385,8 +389,8 @@
     half = 2
     far = []
     for i in range(2):
-        far.append(shifted(left[i][:half], "x", 1, NX))
-        far.append(shifted(right[i][half:], "x", -1, NX))
+        far.append(lax.ppermute(left[i][:half], "x", FAR_RIGHT))
+        far.append(lax.ppermute(right[i][half:], "x", FAR_LEFT))
     outs = kernel(
         third_kernel,
         "third",

time: 72.7 us -> 78.4 us (1.078)
  starting transfers between devices: 26 us -> 32.4 us
  waiting for transfers between devices: 6.88 us -> 5.43 us
    ppermute x0 -> x8, starting transfers between devices: none -> 17.6 us  [the longest x2 5.95 us: on_device(): far.append(lax.ppermute(right[i][half:], 'x', FAR_LEFT))]
    ppermute x12 -> x4, starting transfers between devices: 26 us -> 14.7 us  [shifted(): lax.ppermute(value, axis, [(i, (i + step) % count) for i in range(count)])]
    ppermute x12 -> x4, waiting for transfers between devices: 6.88 us -> 2.43 us  [shifted(): lax.ppermute(value, axis, [(i, (i + step) % count) for i in range(count)])]
    ppermute x0 -> x8, waiting for transfers between devices: none -> 3 us  [the longest x2 1.63 us: on_device(): far.append(lax.ppermute(right[i][half:], 'x', FAR_LEFT))]
    all_to_all x1, blocking collectives: 17.2 us -> 18.3 us  [on_device(): lax.all_to_all(send.reshape(SHARDS, SUB, HD), ('x', 'zh', 'zl'), split_ax...]
  transfers between devices with their start and end apart: 12 -> 12, of which waited for: 4 -> 3; matrix products, arithmetic and copies ran while one was open for 0% -> 0% of each run, Pallas kernels for 4% -> 3%
where the time goes in v7:
time: 78.4 us; the launch traced here: 78 us
  blocking collectives  32.7 us (42%)
  starting transfers between devices  32.4 us (41%)
  waiting for transfers between devices  5.43 us (7%)
  Pallas kernels  5.18 us (7%)
  between operations  0.84 us (1%)
  other arithmetic  0.82 us (1%)
    all_to_all x1, blocking collectives, on_device(): lax.all_to_all(send.reshape(SHARDS, SUB, HD), ('x', 'zh', 'zl'), split_ax...  18.3 us
    ppermute x4, starting transfers between devices, shifted(): lax.ppermute(value, axis, [(i, (i + step) % count) for i in range(count)])  14.7 us
    all_to_all x1, blocking collectives, on_device(): lax.all_to_all(pay, ('y', 'core'), split_axis=0, concat_axis=0, tiled=True)  14.4 us
    ppermute x2, starting transfers between devices, on_device(): far.append(lax.ppermute(right[i][half:], 'x', FAR_LEFT))  5.95 us
    ppermute x2, starting transfers between devices, on_device(): left = [lax.ppermute(part, 'x', TO_RIGHT) for part in (same, other)]  5.88 us
    ppermute x2, starting transfers between devices, on_device(): right = [lax.ppermute(part, 'x', TO_LEFT) for part in (same, other)]  4.47 us
    pallas_call x4, Pallas kernels, kernel(): pl.pallas_call(body, in_specs=[vmem()] * len(inputs), out_specs=[vmem()]...  4.13 us
    ppermute x4, waiting for transfers between devices, shifted(): lax.ppermute(value, axis, [(i, (i + step) % count) for i in range(count)])  2.43 us
  transfers between devices with their start and end apart: 12, of which 3 were waited for; matrix products, arithmetic and copies ran while one was open for 0% of the time, Pallas kernels for 3%

profile of v7, /device:TPU:1, one launch (start us, length us, event | category | flops | bytes accessed | tf_op | source)
XLA Modules:
  0.0 78.0 jit_solution(7283842101485575130)
XLA Ops:
  0.6 0.8 %fusion = (bf16[1,2,128,128]{3,2,1,0:T(8,128)(2,1)S(1)}, bf16[2,128,128]{2,1,0:T(8,128)(2,1)S(1)}) fusion(bf16[1,128,128]{2,1,0:T(8,128)(2,1)} %bitcast.22, bf16[1,128,128]{2,1,0:T(8,128)(2,1)} %bitcast.23), kind=kLoop, calls=%fused_computation.2 | loop fusion | flops 32768 | bytes 196608 | tf_op jit(solution)/shard_map/stack | solution.py:350
  1.4 7.8 %collective-permute-start = (bf16[2,128,128]{2,1,0:T(8,128)(2,1)S(1)}, bf16[2,128,128]{2,1,0:T(8,128)(2,1)S(1)}, u32[]{:S(2)}, u32[]{:S(2)}) collective-permute-start(bf16[2,128,128]{2,1,0:T(8,128)(2,1)S(1)} %get-tuple-element.80), channel_id=1, source_target_pairs={{0,32},{8,40},{16,48},{24,56},{32,0},{40,8},{48,16},{56,24},{1,33}... | collective-permute-start | bytes 196616 | tf_op jit(solution)/shard_map/ppermute | solution.py:339
  9.2 1.2 %collective-permute-start.1 = (bf16[2,128,128]{2,1,0:T(8,128)(2,1)S(1)}, bf16[2,128,128]{2,1,0:T(8,128)(2,1)S(1)}, u32[]{:S(2)}, u32[]{:S(2)}) collective-permute-start(bf16[2,128,128]{2,1,0:T(8,128)(2,1)S(1)} %get-tuple-element.80), channel_id=1, source_target_pairs={{0,16},{8,24},{16,32},{24,40},{32,48},{40,56},{48,0},{56,8},{1,17}... | collective-permute-start | bytes 196616 | tf_op jit(solution)/shard_map/ppermute | solution.py:339
  10.4 2.4 %collective-permute-start.2 = (bf16[2,128,128]{2,1,0:T(8,128)(2,1)S(1)}, bf16[2,128,128]{2,1,0:T(8,128)(2,1)S(1)}, u32[]{:S(2)}, u32[]{:S(2)}) collective-permute-start(bf16[2,128,128]{2,1,0:T(8,128)(2,1)S(1)} %get-tuple-element.80), channel_id=1, source_target_pairs={{0,48},{8,56},{16,0},{24,8},{32,16},{40,24},{48,32},{56,40},{1,49}... | collective-permute-start | bytes 196616 | tf_op jit(solution)/shard_map/ppermute | solution.py:339
  12.8 0.0 collective-permute-done
  12.8 2.4 %collective-permute-done.1 = bf16[2,128,128]{2,1,0:T(8,128)(2,1)S(1)} collective-permute-done((bf16[2,128,128]{2,1,0:T(8,128)(2,1)S(1)}, bf16[2,128,128]{2,1,0:T(8,128)(2,1)S(1)}, u32[]{:S(2)}, u32[]{:S(2)}) %collective-permute-start.1) | collective-permute-done | bytes 65568 | tf_op jit(solution)/shard_map/ppermute | solution.py:339
  15.2 0.0 collective-permute-done.2
  15.3 0.0 copy-start
  15.3 3.3 %collective-permute-start.3 = (bf16[4,2,128,128]{3,2,1,0:T(8,128)(2,1)S(1)}, bf16[4,2,128,128]{3,2,1,0:T(8,128)(2,1)S(1)}, u32[]{:S(2)}, u32[]{:S(2)}) collective-permute-start(bf16[4,2,128,128]{3,2,1,0:T(8,128)(2,1)S(1)} %pad_maximum_fusion.keys_ref), channel_id=1, source_target_pairs={{0,56},{8,0},{16,8},{24,16},{32,24},{40,32},{48,40},{56,48},{1,57}... | collective-permute-start | bytes 786440 | tf_op jit(solution)/shard_map/ppermute | solution.py:339
  18.6 3.1 %collective-permute-start.6 = (bf16[4,2,128,128]{3,2,1,0:T(8,128)(2,1)S(1)}, bf16[4,2,128,128]{3,2,1,0:T(8,128)(2,1)S(1)}, u32[]{:S(2)}, u32[]{:S(2)}) collective-permute-start(bf16[4,2,128,128]{3,2,1,0:T(8,128)(2,1)S(1)} %pad_maximum_fusion.keys_ref), channel_id=1, source_target_pairs={{0,64},{64,128},{128,192},{1,65},{65,129},{129,193},{2,66},{66,130... | collective-permute-start | bytes 786440 | tf_op jit(solution)/shard_map/ppermute | solution.py:379
  21.8 2.5 %collective-permute-start.7 = (bf16[4,2,128,128]{3,2,1,0:T(8,128)(2,1)S(1)}, bf16[4,2,128,128]{3,2,1,0:T(8,128)(2,1)S(1)}, u32[]{:S(2)}, u32[]{:S(2)}) collective-permute-start(bf16[4,2,128,128]{3,2,1,0:T(8,128)(2,1)S(1)} %pad_maximum_fusion.keys_ref), channel_id=1, source_target_pairs={{0,192},{64,0},{1,193},{65,1},{2,194},{66,2},{3,195},{67,3},{4,196... | collective-permute-start | bytes 786440 | tf_op jit(solution)/shard_map/ppermute | solution.py:380
  24.3 0.0 copy-start.2
  24.3 0.0 copy-start.3
  24.3 0.0 copy-done
  24.3 0.6 copy-done.2
  25.0 0.0 copy-done.3
  25.0 1.1 %first.1 = (f32[1024,128]{1,0:T(8,128)S(1)}, f32[1024,128]{1,0:T(8,128)S(1)}, f32[1024,128]{1,0:T(8,128)S(1)}, f32[8,128]{1,0:T(8,128)S(1)}, bf16[1024,512]{1,0:...) custom-call(bf16[128,1024]{1,0:T(8,128)(2,1)S(1)} %copy-done, ...), custom_call_target="tpu_custom_call" | custom-call | flops 1000000000 | bytes 1024 | tf_op jit(solution)/shard_map/first/pallas_call | solution.py:358
  26.1 0.0 collective-permute-done.3.keys_ref
  26.1 2.8 %collective-permute-start.4 = (bf16[4,2,128,128]{3,2,1,0:T(8,128)(2,1)S(1)}, bf16[4,2,128,128]{3,2,1,0:T(8,128)(2,1)S(1)}, u32[]{:S(2)}, u32[]{:S(2)}) collective-permute-start(bf16[4,2,128,128]{3,2,1,0:T(8,128)(2,1)S(1)} %collective-permute-done.3.keys_ref), channel_id=1, source_target_pairs={{0,64},{64,128},{128,192},{1,65},{65,129},{129,193},{2,66},{66,130... | collective-permute-start | bytes 786440 | tf_op jit(solution)/shard_map/ppermute | solution.py:379
  28.9 1.9 %collective-permute-start.5 = (bf16[4,2,128,128]{3,2,1,0:T(8,128)(2,1)S(1)}, bf16[4,2,128,128]{3,2,1,0:T(8,128)(2,1)S(1)}, u32[]{:S(2)}, u32[]{:S(2)}) collective-permute-start(bf16[4,2,128,128]{3,2,1,0:T(8,128)(2,1)S(1)} %collective-permute-done.3.keys_ref), channel_id=1, source_target_pairs={{0,192},{64,0},{1,193},{65,1},{2,194},{66,2},{3,195},{67,3},{4,196... | collective-permute-start | bytes 786440 | tf_op jit(solution)/shard_map/ppermute | solution.py:380
  30.8 0.0 collective-permute-done.6.left_ref
  30.8 0.7 collective-permute-start.10
  31.5 0.0 collective-permute-done.7.right_ref
  31.5 1.8 %collective-permute-start.11 = (bf16[2,2,128,128]{3,2,1,0:T(8,128)(2,1)S(1)}, bf16[2,2,128,128]{3,2,1,0:T(8,128)(2,1)S(1)}, u32[]{:S(2)}, u32[]{:S(2)}) collective-permute-start(bf16[2,2,128,128]{3,2,1,0:T(8,128)(2,1)S(1)} %slice.17), channel_id=1, source_target_pairs={{0,192},{192,128},{1,193},{193,129},{2,194},{194,130},{3,195},{195... | collective-permute-start | bytes 393224 | tf_op jit(solution)/shard_map/ppermute | solution.py:393
  33.3 1.3 %second.1 = (f32[1024,128]{1,0:T(8,128)S(1)}, f32[1024,128]{1,0:T(8,128)S(1)}, f32[1024,128]{1,0:T(8,128)S(1)}, f32[8,128]{1,0:T(8,128)S(1)}, f32[8,128]{1,0:T(8...) custom-call(bf16[128,1024]{1,0:T(8,128)(2,1)S(1)} %copy-done, ...), custom_call_target="tpu_custom_call" | custom-call | flops 1000000000 | bytes 1024 | tf_op jit(solution)/shard_map/second/pallas_call | solution.py:358
  34.6 0.0 collective-permute-done.4.left_ref
  34.6 1.4 %collective-permute-done.5.right_ref = bf16[4,2,128,128]{3,2,1,0:T(8,128)(2,1)S(1)} collective-permute-done((bf16[4,2,128,128]{3,2,1,0:T(8,128)(2,1)S(1)}, bf16[4,2,128,128]{3,2,1,0:T(8,128)(2,1)S(1)}, u32[]{:S(2)}, u32[]{:S(2)}) %collective-permute-start.5) | collective-permute-done | bytes 262176 | tf_op jit(solution)/shard_map/ppermute | solution.py:380
  36.0 0.7 collective-permute-start.8
  36.7 4.1 %collective-permute-start.9 = (bf16[2,2,128,128]{3,2,1,0:T(8,128)(2,1)S(1)}, bf16[2,2,128,128]{3,2,1,0:T(8,128)(2,1)S(1)}, u32[]{:S(2)}, u32[]{:S(2)}) collective-permute-start(bf16[2,2,128,128]{3,2,1,0:T(8,128)(2,1)S(1)} %slice.13), channel_id=1, source_target_pairs={{0,192},{192,128},{1,193},{193,129},{2,194},{194,130},{3,195},{195... | collective-permute-start | bytes 393224 | tf_op jit(solution)/shard_map/ppermute | solution.py:393
  40.8 0.0 collective-permute-done.10.far_0_ref
  40.8 0.0 collective-permute-done.11.far_1_ref
  40.8 0.3 third.1
  41.1 0.0 collective-permute-done.8.far_2_ref
  41.1 1.6 %collective-permute-done.9.far_3_ref = bf16[2,2,128,128]{3,2,1,0:T(8,128)(2,1)S(1)} collective-permute-done((bf16[2,2,128,128]{3,2,1,0:T(8,128)(2,1)S(1)}, bf16[2,2,128,128]{3,2,1,0:T(8,128)(2,1)S(1)}, u32[]{:S(2)}, u32[]{:S(2)}) %collective-permute-start.9) | collective-permute-done | bytes 131104 | tf_op jit(solution)/shard_map/ppermute | solution.py:393
  42.7 1.5 %last.1 = (bf16[128,1024]{1,0:T(8,128)(2,1)}, bf16[768,128]{1,0:T(8,128)(2,1)S(1)}) custom-call(bf16[128,1024]{1,0:T(8,128)(2,1)S(1)} %copy-done, bf16[2,2,128,128]{3,2,1,0:T(8,128)(2,1)S(1)} %collective-permute-done.8.far_2_ref, bf16[2,2,128,128]{3,2,1,0:T(8,128)(2,1)S(1)} %collective-permute-done.9.far_3_ref, f32[8,128]{1,0:T(8,128)S(1)} %get-tuple-element.49.text_ref, ...), custom_call_target="tpu_custom_call" | custom-call | flops 1000000000 | bytes 1024 | tf_op jit(solution)/shard_map/last/pallas_call | solution.py:358
  44.3 18.3 %all_to_all.10 = bf16[32,24,128]{2,1,0:T(8,128)(2,1)S(1)} all-to-all(bf16[32,24,128]{2,1,0:T(8,128)(2,1)S(1)} %bitcast.14), channel_id=1, replica_groups=mesh['x'=4,'zh'=4,'zl'=2,'y'=4,'core'=2] {'x','zh','zl'}, dimensions={0} | all-to-all | bytes 393216 | tf_op jit(solution)/shard_map/all_to_all | solution.py:409
  62.5 0.3 place_rows.1
  62.8 0.0 copy-start.1
  62.9 14.4 %all_to_all.11.pay_ref = f32[8,8,128]{2,1,0:T(8,128)S(1)} all-to-all(f32[8,8,128]{2,1,0:T(8,128)S(1)} %get-tuple-element.75), channel_id=1, replica_groups=mesh['x'=4,'zh'=4,'zl'=2,'y'=4,'core'=2] {'y','core'}, dimensions={0} | all-to-all | bytes 65536 | tf_op jit(solution)/shard_map/all_to_all | solution.py:420
  77.3 0.0 copy-done.1
  77.3 0.7 finish.1
  (5 shorter events, 0.1 us)
Async XLA Ops:
  1.4 11.4 %collective-permute-start = (bf16[2,128,128]{2,1,0:T(8,128)(2,1)S(1)}, bf16[2,128,128]{2,1,0:T(8,128)(2,1)S(1)}, u32[]{:S(2)}, u32[]{:S(2)}) collective-permute-start(bf16[2,128,128]{2,1,0:T(8,128)(2,1)S(1)} %get-tuple-element.80), channel_id=1, source_target_pairs={{0,32},{8,40},{16,48},{24,56},{32,0},{40,8},{48,16},{56,24},{1,33}... | collective-permute-start | bytes 196616 | tf_op jit(solution)/shard_map/ppermute | solution.py:339
  9.2 6.0 %collective-permute-start.1 = (bf16[2,128,128]{2,1,0:T(8,128)(2,1)S(1)}, bf16[2,128,128]{2,1,0:T(8,128)(2,1)S(1)}, u32[]{:S(2)}, u32[]{:S(2)}) collective-permute-start(bf16[2,128,128]{2,1,0:T(8,128)(2,1)S(1)} %get-tuple-element.80), channel_id=1, source_target_pairs={{0,16},{8,24},{16,32},{24,40},{32,48},{40,56},{48,0},{56,8},{1,17}... | collective-permute-start | bytes 196616 | tf_op jit(solution)/shard_map/ppermute | solution.py:339
  10.4 4.8 %collective-permute-start.2 = (bf16[2,128,128]{2,1,0:T(8,128)(2,1)S(1)}, bf16[2,128,128]{2,1,0:T(8,128)(2,1)S(1)}, u32[]{:S(2)}, u32[]{:S(2)}) collective-permute-start(bf16[2,128,128]{2,1,0:T(8,128)(2,1)S(1)} %get-tuple-element.80), channel_id=1, source_target_pairs={{0,48},{8,56},{16,0},{24,8},{32,16},{40,24},{48,32},{56,40},{1,49}... | collective-permute-start | bytes 196616 | tf_op jit(solution)/shard_map/ppermute | solution.py:339
  15.3 9.1 %copy-start = (bf16[128,1024]{1,0:T(8,128)(2,1)S(1)}, bf16[128,1024]{1,0:T(8,128)(2,1)}, u32[]{:S(2)}) copy-start(bf16[128,1024]{1,0:T(8,128)(2,1)} %q_ref.7) | copy-start | bytes 786436
  15.3 10.8 %collective-permute-start.3 = (bf16[4,2,128,128]{3,2,1,0:T(8,128)(2,1)S(1)}, bf16[4,2,128,128]{3,2,1,0:T(8,128)(2,1)S(1)}, u32[]{:S(2)}, u32[]{:S(2)}) collective-permute-start(bf16[4,2,128,128]{3,2,1,0:T(8,128)(2,1)S(1)} %pad_maximum_fusion.keys_ref), channel_id=1, source_target_pairs={{0,56},{8,0},{16,8},{24,16},{32,24},{40,32},{48,40},{56,48},{1,57}... | collective-permute-start | bytes 786440 | tf_op jit(solution)/shard_map/ppermute | solution.py:339
  18.6 12.2 %collective-permute-start.6 = (bf16[4,2,128,128]{3,2,1,0:T(8,128)(2,1)S(1)}, bf16[4,2,128,128]{3,2,1,0:T(8,128)(2,1)S(1)}, u32[]{:S(2)}, u32[]{:S(2)}) collective-permute-start(bf16[4,2,128,128]{3,2,1,0:T(8,128)(2,1)S(1)} %pad_maximum_fusion.keys_ref), channel_id=1, source_target_pairs={{0,64},{64,128},{128,192},{1,65},{65,129},{129,193},{2,66},{66,130... | collective-permute-start | bytes 786440 | tf_op jit(solution)/shard_map/ppermute | solution.py:379
  21.8 9.7 %collective-permute-start.7 = (bf16[4,2,128,128]{3,2,1,0:T(8,128)(2,1)S(1)}, bf16[4,2,128,128]{3,2,1,0:T(8,128)(2,1)S(1)}, u32[]{:S(2)}, u32[]{:S(2)}) collective-permute-start(bf16[4,2,128,128]{3,2,1,0:T(8,128)(2,1)S(1)} %pad_maximum_fusion.keys_ref), channel_id=1, source_target_pairs={{0,192},{64,0},{1,193},{65,1},{2,194},{66,2},{3,195},{67,3},{4,196... | collective-permute-start | bytes 786440 | tf_op jit(solution)/shard_map/ppermute | solution.py:380
  24.3 0.7 copy-start.2
  24.3 0.7 copy-start.3
  26.1 8.5 %collective-permute-start.4 = (bf16[4,2,128,128]{3,2,1,0:T(8,128)(2,1)S(1)}, bf16[4,2,128,128]{3,2,1,0:T(8,128)(2,1)S(1)}, u32[]{:S(2)}, u32[]{:S(2)}) collective-permute-start(bf16[4,2,128,128]{3,2,1,0:T(8,128)(2,1)S(1)} %collective-permute-done.3.keys_ref), channel_id=1, source_target_pairs={{0,64},{64,128},{128,192},{1,65},{65,129},{129,193},{2,66},{66,130... | collective-permute-start | bytes 786440 | tf_op jit(solution)/shard_map/ppermute | solution.py:379
  28.9 7.1 %collective-permute-start.5 = (bf16[4,2,128,128]{3,2,1,0:T(8,128)(2,1)S(1)}, bf16[4,2,128,128]{3,2,1,0:T(8,128)(2,1)S(1)}, u32[]{:S(2)}, u32[]{:S(2)}) collective-permute-start(bf16[4,2,128,128]{3,2,1,0:T(8,128)(2,1)S(1)} %collective-permute-done.3.keys_ref), channel_id=1, source_target_pairs={{0,192},{64,0},{1,193},{65,1},{2,194},{66,2},{3,195},{67,3},{4,196... | collective-permute-start | bytes 786440 | tf_op jit(solution)/shard_map/ppermute | solution.py:380
  30.8 10.0 %collective-permute-start.10 = (bf16[2,2,128,128]{3,2,1,0:T(8,128)(2,1)S(1)}, bf16[2,2,128,128]{3,2,1,0:T(8,128)(2,1)S(1)}, u32[]{:S(2)}, u32[]{:S(2)}) collective-permute-start(bf16[2,2,128,128]{3,2,1,0:T(8,128)(2,1)S(1)} %slice.16), channel_id=1, source_target_pairs={{64,128},{128,192},{65,129},{129,193},{66,130},{130,194},{67,131},... | collective-permute-start | bytes 393224 | tf_op jit(solution)/shard_map/ppermute | solution.py:392
  31.5 9.3 %collective-permute-start.11 = (bf16[2,2,128,128]{3,2,1,0:T(8,128)(2,1)S(1)}, bf16[2,2,128,128]{3,2,1,0:T(8,128)(2,1)S(1)}, u32[]{:S(2)}, u32[]{:S(2)}) collective-permute-start(bf16[2,2,128,128]{3,2,1,0:T(8,128)(2,1)S(1)} %slice.17), channel_id=1, source_target_pairs={{0,192},{192,128},{1,193},{193,129},{2,194},{194,130},{3,195},{195... | collective-permute-start | bytes 393224 | tf_op jit(solution)/shard_map/ppermute | solution.py:393
  36.0 5.1 %collective-permute-start.8 = (bf16[2,2,128,128]{3,2,1,0:T(8,128)(2,1)S(1)}, bf16[2,2,128,128]{3,2,1,0:T(8,128)(2,1)S(1)}, u32[]{:S(2)}, u32[]{:S(2)}) collective-permute-start(bf16[2,2,128,128]{3,2,1,0:T(8,128)(2,1)S(1)} %slice.12), channel_id=1, source_target_pairs={{64,128},{128,192},{65,129},{129,193},{66,130},{130,194},{67,131},... | collective-permute-start | bytes 393224 | tf_op jit(solution)/shard_map/ppermute | solution.py:392
  36.7 6.1 %collective-permute-start.9 = (bf16[2,2,128,128]{3,2,1,0:T(8,128)(2,1)S(1)}, bf16[2,2,128,128]{3,2,1,0:T(8,128)(2,1)S(1)}, u32[]{:S(2)}, u32[]{:S(2)}) collective-permute-start(bf16[2,2,128,128]{3,2,1,0:T(8,128)(2,1)S(1)} %slice.13), channel_id=1, source_target_pairs={{0,192},{192,128},{1,193},{193,129},{2,194},{194,130},{3,195},{195... | collective-permute-start | bytes 393224 | tf_op jit(solution)/shard_map/ppermute | solution.py:393
  62.8 14.4 %copy-start.1 = (f32[1024]{0:T(1024)S(1)}, f32[1024]{0:T(1024)}, u32[]{:S(2)}) copy-start(f32[1024]{0:T(1024)} %param.11) | copy-start | bytes 12292

commit v8 on v6

--- a/solution.py
+++ b/solution.py
@@ -21,7 +21,7 @@
 EIGHT = SHARDS * 8
 TP = 8
 NEAR = (0, 4, -2, 2)
-REST = (1, 5, -1, 3)
+REST = ((0,), (4,), (-2,), (2,))
 FACTOR = math.log2(math.e) / math.sqrt(HD)
 LOW = -1e30
 NT = (((1,), (1,)), ((), ()))
@@ -75,6 +75,8 @@
 
 
 def shard_of(z, offset):
+    if isinstance(offset, tuple):
+        return shard_of(z ^ 1, offset[0])
     return (z + offset) & (NZ - 1)
 
 
@@ -344,7 +346,7 @@
     both = jnp.stack([key_rows, value_rows])
     over_z = ("zh", "zl")
     same = jnp.stack([both] + [shifted(both, over_z, step, NZ) for step in (4, 2, -2)])
-    other = shifted(same, over_z, -1, NZ)
+    other = shifted(same, "zl", 1, 2)
     state = [shape_of((ROWS, HD), f32)] * 3
     level = shape_of((GROUP, TOK), f32)
     near_weights = shape_of((ROWS, len(NEAR) * TOK), bf16)

time: 72.7 us -> 72.4 us (level)
  starting transfers between devices: 26 us -> 23.2 us
  blocking collectives: 32.1 us -> 33.9 us
  waiting for transfers between devices: 6.88 us -> 7.72 us
    ppermute x12, starting transfers between devices: 26 us -> 23.2 us  [shifted(): lax.ppermute(value, axis, [(i, (i + step) % count) for i in range(count)])]
    all_to_all x1, blocking collectives: 17.2 us -> 18.6 us  [on_device(): lax.all_to_all(send.reshape(SHARDS, SUB, HD), ('x', 'zh', 'zl'), split_ax...]
    ppermute x12, waiting for transfers between devices: 6.88 us -> 7.72 us  [shifted(): lax.ppermute(value, axis, [(i, (i + step) % count) for i in range(count)])]
  transfers between devices with their start and end apart: 12 -> 12, of which waited for: 4 -> 6; matrix products, arithmetic and copies ran while one was open for 0% -> 0% of each run, Pallas kernels for 4% -> 4%
where the time goes in v8:
time: 72.4 us; the launch traced here: 72.3 us
  blocking collectives  33.9 us (47%)
  starting transfers between devices  23.2 us (32%)
  waiting for transfers between devices  7.72 us (11%)
  Pallas kernels  5.18 us (7%)
  other arithmetic  0.82 us (1%)
    ppermute x12, starting transfers between devices, shifted(): lax.ppermute(value, axis, [(i, (i + step) % count) for i in range(count)])  23.2 us
    all_to_all x1, blocking collectives, on_device(): lax.all_to_all(send.reshape(SHARDS, SUB, HD), ('x', 'zh', 'zl'), split_ax...  18.6 us
    all_to_all x1, blocking collectives, on_device(): lax.all_to_all(pay, ('y', 'core'), split_axis=0, concat_axis=0, tiled=True)  15.3 us
    ppermute x12, waiting for transfers between devices, shifted(): lax.ppermute(value, axis, [(i, (i + step) % count) for i in range(count)])  7.72 us
    pallas_call x4, Pallas kernels, kernel(): pl.pallas_call(body, in_specs=[vmem()] * len(inputs), out_specs=[vmem()]...  4.12 us
  transfers between devices with their start and end apart: 12, of which 6 were waited for; matrix products, arithmetic and copies ran while one was open for 0% of the time, Pallas kernels for 4%

profile of v8, /device:TPU:1, one launch (start us, length us, event | category | flops | bytes accessed | tf_op | source)
XLA Modules:
  0.0 72.3 jit_solution(4218328458742180341)
XLA Ops:
  0.6 0.8 %fusion = (bf16[1,2,128,128]{3,2,1,0:T(8,128)(2,1)S(1)}, bf16[2,128,128]{2,1,0:T(8,128)(2,1)S(1)}) fusion(bf16[1,128,128]{2,1,0:T(8,128)(2,1)} %bitcast.22, bf16[1,128,128]{2,1,0:T(8,128)(2,1)} %bitcast.23), kind=kLoop, calls=%fused_computation.2 | loop fusion | flops 32768 | bytes 196608 | tf_op jit(solution)/shard_map/stack | solution.py:348
  1.4 7.8 %collective-permute-start = (bf16[2,128,128]{2,1,0:T(8,128)(2,1)S(1)}, bf16[2,128,128]{2,1,0:T(8,128)(2,1)S(1)}, u32[]{:S(2)}, u32[]{:S(2)}) collective-permute-start(bf16[2,128,128]{2,1,0:T(8,128)(2,1)S(1)} %get-tuple-element.80), channel_id=1, source_target_pairs={{0,32},{8,40},{16,48},{24,56},{32,0},{40,8},{48,16},{56,24},{1,33}... | collective-permute-start | bytes 196616 | tf_op jit(solution)/shard_map/ppermute | solution.py:337
  9.2 1.2 %collective-permute-start.1 = (bf16[2,128,128]{2,1,0:T(8,128)(2,1)S(1)}, bf16[2,128,128]{2,1,0:T(8,128)(2,1)S(1)}, u32[]{:S(2)}, u32[]{:S(2)}) collective-permute-start(bf16[2,128,128]{2,1,0:T(8,128)(2,1)S(1)} %get-tuple-element.80), channel_id=1, source_target_pairs={{0,16},{8,24},{16,32},{24,40},{32,48},{40,56},{48,0},{56,8},{1,17}... | collective-permute-start | bytes 196616 | tf_op jit(solution)/shard_map/ppermute | solution.py:337
  10.4 2.4 %collective-permute-start.2 = (bf16[2,128,128]{2,1,0:T(8,128)(2,1)S(1)}, bf16[2,128,128]{2,1,0:T(8,128)(2,1)S(1)}, u32[]{:S(2)}, u32[]{:S(2)}) collective-permute-start(bf16[2,128,128]{2,1,0:T(8,128)(2,1)S(1)} %get-tuple-element.80), channel_id=1, source_target_pairs={{0,48},{8,56},{16,0},{24,8},{32,16},{40,24},{48,32},{56,40},{1,49}... | collective-permute-start | bytes 196616 | tf_op jit(solution)/shard_map/ppermute | solution.py:337
  12.8 0.0 collective-permute-done
  12.8 2.4 %collective-permute-done.1 = bf16[2,128,128]{2,1,0:T(8,128)(2,1)S(1)} collective-permute-done((bf16[2,128,128]{2,1,0:T(8,128)(2,1)S(1)}, bf16[2,128,128]{2,1,0:T(8,128)(2,1)S(1)}, u32[]{:S(2)}, u32[]{:S(2)}) %collective-permute-start.1) | collective-permute-done | bytes 65568 | tf_op jit(solution)/shard_map/ppermute | solution.py:337
  15.2 0.0 collective-permute-done.2
  15.3 0.0 copy-start
  15.3 0.6 collective-permute-start.3
  15.9 1.2 %collective-permute-start.6 = (bf16[4,2,128,128]{3,2,1,0:T(8,128)(2,1)S(1)}, bf16[4,2,128,128]{3,2,1,0:T(8,128)(2,1)S(1)}, u32[]{:S(2)}, u32[]{:S(2)}) collective-permute-start(bf16[4,2,128,128]{3,2,1,0:T(8,128)(2,1)S(1)} %pad_maximum_fusion.keys_ref), channel_id=1, source_target_pairs={{0,64},{64,128},{128,192},{192,0},{1,65},{65,129},{129,193},{193,1... | collective-permute-start | bytes 786440 | tf_op jit(solution)/shard_map/ppermute | solution.py:337
  17.1 1.5 %collective-permute-start.7 = (bf16[4,2,128,128]{3,2,1,0:T(8,128)(2,1)S(1)}, bf16[4,2,128,128]{3,2,1,0:T(8,128)(2,1)S(1)}, u32[]{:S(2)}, u32[]{:S(2)}) collective-permute-start(bf16[4,2,128,128]{3,2,1,0:T(8,128)(2,1)S(1)} %pad_maximum_fusion.keys_ref), channel_id=1, source_target_pairs={{0,192},{64,0},{128,64},{192,128},{1,193},{65,1},{129,65},{193,129... | collective-permute-start | bytes 786440 | tf_op jit(solution)/shard_map/ppermute | solution.py:337
  18.6 0.0 copy-start.2
  18.6 0.0 copy-start.3
  18.6 0.0 copy-done
  18.6 0.6 copy-done.2
  19.2 0.0 copy-done.3
  19.2 1.1 %first.1 = (f32[1024,128]{1,0:T(8,128)S(1)}, f32[1024,128]{1,0:T(8,128)S(1)}, f32[1024,128]{1,0:T(8,128)S(1)}, f32[8,128]{1,0:T(8,128)S(1)}, bf16[1024,512]{1,0:...) custom-call(bf16[128,1024]{1,0:T(8,128)(2,1)S(1)} %copy-done, ...), custom_call_target="tpu_custom_call" | custom-call | flops 1000000000 | bytes 1024 | tf_op jit(solution)/shard_map/first/pallas_call | solution.py:356
  20.3 1.0 %collective-permute-done.3.keys_ref = bf16[4,2,128,128]{3,2,1,0:T(8,128)(2,1)S(1)} collective-permute-done((bf16[4,2,128,128]{3,2,1,0:T(8,128)(2,1)S(1)}, bf16[4,2,128,128]{3,2,1,0:T(8,128)(2,1)S(1)}, u32[]{:S(2)}, u32[]{:S(2)}) %collective-permute-start.3) | collective-permute-done | bytes 262176 | tf_op jit(solution)/shard_map/ppermute | solution.py:337
  21.3 1.1 %collective-permute-start.4 = (bf16[4,2,128,128]{3,2,1,0:T(8,128)(2,1)S(1)}, bf16[4,2,128,128]{3,2,1,0:T(8,128)(2,1)S(1)}, u32[]{:S(2)}, u32[]{:S(2)}) collective-permute-start(bf16[4,2,128,128]{3,2,1,0:T(8,128)(2,1)S(1)} %collective-permute-done.3.keys_ref), channel_id=1, source_target_pairs={{0,64},{64,128},{128,192},{192,0},{1,65},{65,129},{129,193},{193,1... | collective-permute-start | bytes 786440 | tf_op jit(solution)/shard_map/ppermute | solution.py:337
  22.3 1.6 %collective-permute-start.5 = (bf16[4,2,128,128]{3,2,1,0:T(8,128)(2,1)S(1)}, bf16[4,2,128,128]{3,2,1,0:T(8,128)(2,1)S(1)}, u32[]{:S(2)}, u32[]{:S(2)}) collective-permute-start(bf16[4,2,128,128]{3,2,1,0:T(8,128)(2,1)S(1)} %collective-permute-done.3.keys_ref), channel_id=1, source_target_pairs={{0,192},{64,0},{128,64},{192,128},{1,193},{65,1},{129,65},{193,129... | collective-permute-start | bytes 786440 | tf_op jit(solution)/shard_map/ppermute | solution.py:337
  24.0 0.0 collective-permute-done.6.left_ref
  24.0 0.1 collective-permute-start.10
  24.1 0.0 collective-permute-done.7.right_ref
  24.1 2.7 %collective-permute-start.11 = (bf16[2,2,128,128]{3,2,1,0:T(8,128)(2,1)S(1)}, bf16[2,2,128,128]{3,2,1,0:T(8,128)(2,1)S(1)}, u32[]{:S(2)}, u32[]{:S(2)}) collective-permute-start(bf16[2,2,128,128]{3,2,1,0:T(8,128)(2,1)S(1)} %slice.17), channel_id=1, source_target_pairs={{0,192},{64,0},{128,64},{192,128},{1,193},{65,1},{129,65},{193,129... | collective-permute-start | bytes 393224 | tf_op jit(solution)/shard_map/ppermute | solution.py:337
  26.8 1.3 %second.1 = (f32[1024,128]{1,0:T(8,128)S(1)}, f32[1024,128]{1,0:T(8,128)S(1)}, f32[1024,128]{1,0:T(8,128)S(1)}, f32[8,128]{1,0:T(8,128)S(1)}, f32[8,128]{1,0:T(8...) custom-call(bf16[128,1024]{1,0:T(8,128)(2,1)S(1)} %copy-done, ...), custom_call_target="tpu_custom_call" | custom-call | flops 1000000000 | bytes 1024 | tf_op jit(solution)/shard_map/second/pallas_call | solution.py:356
  28.1 1.1 %collective-permute-done.4.left_ref = bf16[4,2,128,128]{3,2,1,0:T(8,128)(2,1)S(1)} collective-permute-done((bf16[4,2,128,128]{3,2,1,0:T(8,128)(2,1)S(1)}, bf16[4,2,128,128]{3,2,1,0:T(8,128)(2,1)S(1)}, u32[]{:S(2)}, u32[]{:S(2)}) %collective-permute-start.4) | collective-permute-done | bytes 262176 | tf_op jit(solution)/shard_map/ppermute | solution.py:337
  29.2 0.2 collective-permute-done.5.right_ref
  29.4 1.3 %collective-permute-start.8 = (bf16[2,2,128,128]{3,2,1,0:T(8,128)(2,1)S(1)}, bf16[2,2,128,128]{3,2,1,0:T(8,128)(2,1)S(1)}, u32[]{:S(2)}, u32[]{:S(2)}) collective-permute-start(bf16[2,2,128,128]{3,2,1,0:T(8,128)(2,1)S(1)} %slice.12), channel_id=1, source_target_pairs={{0,64},{64,128},{128,192},{192,0},{1,65},{65,129},{129,193},{193,1... | collective-permute-start | bytes 393224 | tf_op jit(solution)/shard_map/ppermute | solution.py:337
  30.7 1.8 %collective-permute-start.9 = (bf16[2,2,128,128]{3,2,1,0:T(8,128)(2,1)S(1)}, bf16[2,2,128,128]{3,2,1,0:T(8,128)(2,1)S(1)}, u32[]{:S(2)}, u32[]{:S(2)}) collective-permute-start(bf16[2,2,128,128]{3,2,1,0:T(8,128)(2,1)S(1)} %slice.13), channel_id=1, source_target_pairs={{0,192},{64,0},{128,64},{192,128},{1,193},{65,1},{129,65},{193,129... | collective-permute-start | bytes 393224 | tf_op jit(solution)/shard_map/ppermute | solution.py:337
  32.6 0.0 collective-permute-done.10.far_0_ref
  32.6 0.0 collective-permute-done.11.far_1_ref
  32.6 0.3 third.1
  32.8 2.8 %collective-permute-done.8.far_2_ref = bf16[2,2,128,128]{3,2,1,0:T(8,128)(2,1)S(1)} collective-permute-done((bf16[2,2,128,128]{3,2,1,0:T(8,128)(2,1)S(1)}, bf16[2,2,128,128]{3,2,1,0:T(8,128)(2,1)S(1)}, u32[]{:S(2)}, u32[]{:S(2)}) %collective-permute-start.8) | collective-permute-done | bytes 131104 | tf_op jit(solution)/shard_map/ppermute | solution.py:337
  35.6 0.2 collective-permute-done.9.far_3_ref
  35.8 1.5 %last.1 = (bf16[128,1024]{1,0:T(8,128)(2,1)}, bf16[768,128]{1,0:T(8,128)(2,1)S(1)}) custom-call(bf16[128,1024]{1,0:T(8,128)(2,1)S(1)} %copy-done, bf16[2,2,128,128]{3,2,1,0:T(8,128)(2,1)S(1)} %collective-permute-done.8.far_2_ref, bf16[2,2,128,128]{3,2,1,0:T(8,128)(2,1)S(1)} %collective-permute-done.9.far_3_ref, f32[8,128]{1,0:T(8,128)S(1)} %get-tuple-element.49.text_ref, ...), custom_call_target="tpu_custom_call" | custom-call | flops 1000000000 | bytes 1024 | tf_op jit(solution)/shard_map/last/pallas_call | solution.py:356
  37.3 18.6 %all_to_all.10 = bf16[32,24,128]{2,1,0:T(8,128)(2,1)S(1)} all-to-all(bf16[32,24,128]{2,1,0:T(8,128)(2,1)S(1)} %bitcast.14), channel_id=1, replica_groups=mesh['x'=4,'zh'=4,'zl'=2,'y'=4,'core'=2] {'x','zh','zl'}, dimensions={0} | all-to-all | bytes 393216 | tf_op jit(solution)/shard_map/all_to_all | solution.py:407
  55.9 0.3 place_rows.1
  56.2 0.0 copy-start.1
  56.2 15.3 %all_to_all.11.pay_ref = f32[8,8,128]{2,1,0:T(8,128)S(1)} all-to-all(f32[8,8,128]{2,1,0:T(8,128)S(1)} %get-tuple-element.75), channel_id=1, replica_groups=mesh['x'=4,'zh'=4,'zl'=2,'y'=4,'core'=2] {'y','core'}, dimensions={0} | all-to-all | bytes 65536 | tf_op jit(solution)/shard_map/all_to_all | solution.py:418
  71.6 0.0 copy-done.1
  71.6 0.7 %finish.1 = (f32[1,128]{1,0:T(1,128)}, bf16[32,1024]{1,0:T(8,128)(2,1)}) custom-call(f32[8,8,128]{2,1,0:T(8,128)S(1)} %all_to_all.11.pay_ref, f32[128,256]{1,0:T(8,128)S(1)} %get-tuple-element.76.rows_ref, f32[1,1024]{1,0:T(1,128)S(1)} %bitcast.15, s32[1,128]{1,0:T(1,128)S(1)} %bitcast.17), custom_call_target="tpu_custom_call" | custom-call | tf_op jit(solution)/shard_map/finish/pallas_call | solution.py:419
  (5 shorter events, 0.1 us)
Async XLA Ops:
  1.4 11.4 %collective-permute-start = (bf16[2,128,128]{2,1,0:T(8,128)(2,1)S(1)}, bf16[2,128,128]{2,1,0:T(8,128)(2,1)S(1)}, u32[]{:S(2)}, u32[]{:S(2)}) collective-permute-start(bf16[2,128,128]{2,1,0:T(8,128)(2,1)S(1)} %get-tuple-element.80), channel_id=1, source_target_pairs={{0,32},{8,40},{16,48},{24,56},{32,0},{40,8},{48,16},{56,24},{1,33}... | collective-permute-start | bytes 196616 | tf_op jit(solution)/shard_map/ppermute | solution.py:337
  9.2 6.0 %collective-permute-start.1 = (bf16[2,128,128]{2,1,0:T(8,128)(2,1)S(1)}, bf16[2,128,128]{2,1,0:T(8,128)(2,1)S(1)}, u32[]{:S(2)}, u32[]{:S(2)}) collective-permute-start(bf16[2,128,128]{2,1,0:T(8,128)(2,1)S(1)} %get-tuple-element.80), channel_id=1, source_target_pairs={{0,16},{8,24},{16,32},{24,40},{32,48},{40,56},{48,0},{56,8},{1,17}... | collective-permute-start | bytes 196616 | tf_op jit(solution)/shard_map/ppermute | solution.py:337
  10.4 4.8 %collective-permute-start.2 = (bf16[2,128,128]{2,1,0:T(8,128)(2,1)S(1)}, bf16[2,128,128]{2,1,0:T(8,128)(2,1)S(1)}, u32[]{:S(2)}, u32[]{:S(2)}) collective-permute-start(bf16[2,128,128]{2,1,0:T(8,128)(2,1)S(1)} %get-tuple-element.80), channel_id=1, source_target_pairs={{0,48},{8,56},{16,0},{24,8},{32,16},{40,24},{48,32},{56,40},{1,49}... | collective-permute-start | bytes 196616 | tf_op jit(solution)/shard_map/ppermute | solution.py:337
  15.3 3.3 %copy-start = (bf16[128,1024]{1,0:T(8,128)(2,1)S(1)}, bf16[128,1024]{1,0:T(8,128)(2,1)}, u32[]{:S(2)}) copy-start(bf16[128,1024]{1,0:T(8,128)(2,1)} %q_ref.7) | copy-start | bytes 786436
  15.3 6.0 %collective-permute-start.3 = (bf16[4,2,128,128]{3,2,1,0:T(8,128)(2,1)S(1)}, bf16[4,2,128,128]{3,2,1,0:T(8,128)(2,1)S(1)}, u32[]{:S(2)}, u32[]{:S(2)}) collective-permute-start(bf16[4,2,128,128]{3,2,1,0:T(8,128)(2,1)S(1)} %pad_maximum_fusion.keys_ref), channel_id=1, source_target_pairs={{0,8},{8,0},{1,9},{9,1},{2,10},{10,2},{3,11},{11,3},{4,12},{12,4},... | collective-permute-start | bytes 786440 | tf_op jit(solution)/shard_map/ppermute | solution.py:337
  15.9 8.1 %collective-permute-start.6 = (bf16[4,2,128,128]{3,2,1,0:T(8,128)(2,1)S(1)}, bf16[4,2,128,128]{3,2,1,0:T(8,128)(2,1)S(1)}, u32[]{:S(2)}, u32[]{:S(2)}) collective-permute-start(bf16[4,2,128,128]{3,2,1,0:T(8,128)(2,1)S(1)} %pad_maximum_fusion.keys_ref), channel_id=1, source_target_pairs={{0,64},{64,128},{128,192},{192,0},{1,65},{65,129},{129,193},{193,1... | collective-permute-start | bytes 786440 | tf_op jit(solution)/shard_map/ppermute | solution.py:337
  17.1 7.0 %collective-permute-start.7 = (bf16[4,2,128,128]{3,2,1,0:T(8,128)(2,1)S(1)}, bf16[4,2,128,128]{3,2,1,0:T(8,128)(2,1)S(1)}, u32[]{:S(2)}, u32[]{:S(2)}) collective-permute-start(bf16[4,2,128,128]{3,2,1,0:T(8,128)(2,1)S(1)} %pad_maximum_fusion.keys_ref), channel_id=1, source_target_pairs={{0,192},{64,0},{128,64},{192,128},{1,193},{65,1},{129,65},{193,129... | collective-permute-start | bytes 786440 | tf_op jit(solution)/shard_map/ppermute | solution.py:337
  18.6 0.7 copy-start.2
  18.6 0.7 copy-start.3
  21.3 7.9 %collective-permute-start.4 = (bf16[4,2,128,128]{3,2,1,0:T(8,128)(2,1)S(1)}, bf16[4,2,128,128]{3,2,1,0:T(8,128)(2,1)S(1)}, u32[]{:S(2)}, u32[]{:S(2)}) collective-permute-start(bf16[4,2,128,128]{3,2,1,0:T(8,128)(2,1)S(1)} %collective-permute-done.3.keys_ref), channel_id=1, source_target_pairs={{0,64},{64,128},{128,192},{192,0},{1,65},{65,129},{129,193},{193,1... | collective-permute-start | bytes 786440 | tf_op jit(solution)/shard_map/ppermute | solution.py:337
  22.3 7.1 %collective-permute-start.5 = (bf16[4,2,128,128]{3,2,1,0:T(8,128)(2,1)S(1)}, bf16[4,2,128,128]{3,2,1,0:T(8,128)(2,1)S(1)}, u32[]{:S(2)}, u32[]{:S(2)}) collective-permute-start(bf16[4,2,128,128]{3,2,1,0:T(8,128)(2,1)S(1)} %collective-permute-done.3.keys_ref), channel_id=1, source_target_pairs={{0,192},{64,0},{128,64},{192,128},{1,193},{65,1},{129,65},{193,129... | collective-permute-start | bytes 786440 | tf_op jit(solution)/shard_map/ppermute | solution.py:337
  24.0 8.6 %collective-permute-start.10 = (bf16[2,2,128,128]{3,2,1,0:T(8,128)(2,1)S(1)}, bf16[2,2,128,128]{3,2,1,0:T(8,128)(2,1)S(1)}, u32[]{:S(2)}, u32[]{:S(2)}) collective-permute-start(bf16[2,2,128,128]{3,2,1,0:T(8,128)(2,1)S(1)} %slice.16), channel_id=1, source_target_pairs={{0,64},{64,128},{128,192},{192,0},{1,65},{65,129},{129,193},{193,1... | collective-permute-start | bytes 393224 | tf_op jit(solution)/shard_map/ppermute | solution.py:337
  24.1 8.5 %collective-permute-start.11 = (bf16[2,2,128,128]{3,2,1,0:T(8,128)(2,1)S(1)}, bf16[2,2,128,128]{3,2,1,0:T(8,128)(2,1)S(1)}, u32[]{:S(2)}, u32[]{:S(2)}) collective-permute-start(bf16[2,2,128,128]{3,2,1,0:T(8,128)(2,1)S(1)} %slice.17), channel_id=1, source_target_pairs={{0,192},{64,0},{128,64},{192,128},{1,193},{65,1},{129,65},{193,129... | collective-permute-start | bytes 393224 | tf_op jit(solution)/shard_map/ppermute | solution.py:337
  29.4 6.2 %collective-permute-start.8 = (bf16[2,2,128,128]{3,2,1,0:T(8,128)(2,1)S(1)}, bf16[2,2,128,128]{3,2,1,0:T(8,128)(2,1)S(1)}, u32[]{:S(2)}, u32[]{:S(2)}) collective-permute-start(bf16[2,2,128,128]{3,2,1,0:T(8,128)(2,1)S(1)} %slice.12), channel_id=1, source_target_pairs={{0,64},{64,128},{128,192},{192,0},{1,65},{65,129},{129,193},{193,1... | collective-permute-start | bytes 393224 | tf_op jit(solution)/shard_map/ppermute | solution.py:337
  30.7 5.0 %collective-permute-start.9 = (bf16[2,2,128,128]{3,2,1,0:T(8,128)(2,1)S(1)}, bf16[2,2,128,128]{3,2,1,0:T(8,128)(2,1)S(1)}, u32[]{:S(2)}, u32[]{:S(2)}) collective-permute-start(bf16[2,2,128,128]{3,2,1,0:T(8,128)(2,1)S(1)} %slice.13), channel_id=1, source_target_pairs={{0,192},{64,0},{128,64},{192,128},{1,193},{65,1},{129,65},{193,129... | collective-permute-start | bytes 393224 | tf_op jit(solution)/shard_map/ppermute | solution.py:337
  56.2 15.3 %copy-start.1 = (f32[1024]{0:T(1024)S(1)}, f32[1024]{0:T(1024)}, u32[]{:S(2)}) copy-start(f32[1024]{0:T(1024)} %param.11) | copy-start | bytes 12292
